TPU v7x, 768 devices: a whole 4x8x12 slice. The times are simulated.
768 devices in a mesh: row: 24 (over y, z_hi), col: 32 (over x, z_lo, core).
Axes of the slice: x: 4, y: 8, z: 12 (z_hi: 3, z_lo: 4; z = z_hi * 4 + z_lo), core: 2. Of those that a mesh axis runs over, the one named last changes fastest.
Arguments:
- row_points: bfloat16 [24576, 64], P(('row', 'col')), may hold values from -0.75 to 0.75
- row_solves: bfloat16 [24576, 32], P(('row', 'col')), may hold values from -96 to 96
- col_points: bfloat16 [245760, 64], P(('col', 'row')), may hold values from -0.75 to 0.75
- col_probes: bfloat16 [245760, 32], P(('col', 'row')), may hold values from -6 to 6
Outputs:
- row_grad: float32 [24576, 64], P(('row', 'col'))
- col_grad: float32 [245760, 64], P(('col', 'row'))
All inputs are finite; a program needn't handle non-finite values.
Results may differ from a plain program's by a relative error of at most 0.007.
Values may be sent and summed in bfloat16 or wider, within the bound.
No kernel may reach another device: no remote copies, remote signals or barrier semaphores. Data moves between devices by JAX's collectives and lax.ppermute only.
A program may use at most 32 MiB of HBM per device.

v0:
```python
import math

import jax
import jax.numpy as jnp
from jax import lax
from jax.sharding import PartitionSpec as P

P_SIZE = 32


def tile_weight(row_feat, row_norm, row_solve, col_feat, col_probe):
    gram = jnp.dot(row_feat, col_feat.T, preferred_element_type=jnp.float32)
    col_wide = col_feat.astype(jnp.float32)
    col_norm = jnp.sum(col_wide * col_wide, axis=1)
    kernel = jnp.exp(-0.5 * (row_norm[:, None] + col_norm[None, :] - 2.0 * gram))
    mixing = jnp.dot(row_solve, col_probe.T, preferred_element_type=jnp.float32) * (1.0 / P_SIZE)
    return ((kernel * mixing).astype(jnp.bfloat16), col_wide)


def sweep(row_feat, row_norm, row_solve, col_feat, col_probe, width):
    count = col_feat.shape[0]
    block = math.gcd(count, width)
    feats = col_feat.reshape(count // block, block, col_feat.shape[1])
    probes = col_probe.reshape(count // block, block, col_probe.shape[1])
    initial = (jnp.zeros(row_feat.shape, jnp.float32), jnp.zeros((row_feat.shape[0],), jnp.float32))

    def advance(carry, pieces):
        feat, probe = pieces
        weight, col_wide = tile_weight(row_feat, row_norm, row_solve, feat, probe)
        wide = weight.astype(jnp.float32)
        carry = (
            carry[0] + jnp.dot(weight, feat, preferred_element_type=jnp.float32),
            carry[1] + jnp.sum(wide, axis=1),
        )
        result = (
            jnp.dot(weight.T, row_feat, preferred_element_type=jnp.float32)
            - jnp.sum(wide, axis=0)[:, None] * col_wide
        )
        return (carry, result)

    carry, results = lax.scan(advance, initial, (feats, probes))
    return (carry[0], carry[1], results.reshape(count, row_feat.shape[1]))


def body(row_points, row_solves, col_points, col_probes):
    row_feat, row_solve = (
        lax.all_gather(row_points, "col", axis=0, tiled=True),
        lax.all_gather(row_solves, "col", axis=0, tiled=True),
    )
    row_wide = row_feat.astype(jnp.float32)
    row_norm = jnp.sum(row_wide * row_wide, axis=1)
    piece_rows = col_points.shape[0]
    row_part, row_total, col_term = sweep(
        row_feat,
        row_norm,
        row_solve,
        lax.all_gather(col_points, "row", axis=0, tiled=True),
        lax.all_gather(col_probes, "row", axis=0, tiled=True),
        piece_rows,
    )
    row_acc, row_total, col_buffer = (row_part, row_total, col_term)
    col_grad = lax.psum_scatter(col_buffer, "row", scatter_dimension=0, tiled=True)
    row_term = row_acc - row_total[:, None] * row_wide
    row_grad = lax.psum_scatter(row_term, "col", scatter_dimension=0, tiled=True)
    return (row_grad, col_grad)


def solution(mesh):
    return jax.shard_map(
        body,
        mesh=mesh,
        in_specs=(
            P(("row", "col"), None),
            P(("row", "col"), None),
            P(("col", "row"), None),
            P(("col", "row"), None),
        ),
        out_specs=(P(("row", "col"), None), P(("col", "row"), None)),
        check_vma=False,
    )
```

profile of v0, /device:TPU:8, one launch (start us, length us, event | category | flops | bytes accessed | tf_op | source)
XLA Modules:
  0.0 1026.0 jit_solution(12965543875787069210)
XLA Ops:
  7.2 47.0 %all_gather.12 = bf16[1024,64]{1,0:T(8,128)(2,1)S(1)} all-gather(bf16[32,64]{1,0:T(8,128)(2,1)} %param.6), channel_id=1, replica_groups=mesh['row'=24,'col'=32] {'col'}, dimensions={0}, use_global_device_ids=true | all-gather | bytes 135168 | tf_op jit(solution)/shard_map/all_gather | solution.py:47
  54.5 39.2 %all_gather.15 = bf16[1024,32]{1,0:T(8,128)(2,1)S(1)} all-gather(bf16[32,32]{1,0:T(8,128)(2,1)} %param.7), channel_id=1, replica_groups=mesh['row'=24,'col'=32] {'col'}, dimensions={0}, use_global_device_ids=true | all-gather | bytes 67584 | tf_op jit(solution)/shard_map/all_gather | solution.py:48
  93.6 79.3 %all-gather.1 = bf16[24,320,32]{1,2,0:T(8,128)(2,1)S(1)} all-gather(bf16[1,320,32]{1,2,0:T(8,128)(2,1)} %bitcast.66), channel_id=1, replica_groups=mesh['row'=24,'col'=32] {'row'}, dimensions={0}, use_global_device_ids=true | all-gather | bytes 512000 | tf_op jit(solution)/shard_map/all_gather | solution.py:58
  172.9 102.2 %all-gather = bf16[24,320,64]{1,2,0:T(8,128)(2,1)S(1)} all-gather(bf16[1,320,64]{1,2,0:T(8,128)(2,1)S(1)} %bitcast.65), channel_id=1, replica_groups=mesh['row'=24,'col'=32] {'row'}, dimensions={0}, use_global_device_ids=true | all-gather | bytes 1024000 | tf_op jit(solution)/shard_map/all_gather | solution.py:57
  275.2 54.6 %while.15 = (s32[]{:T(128)}, f32[1024,64]{0,1:T(8,128)S(1)}, f32[1024]{0:T(1024)S(1)}, f32[24,320,64]{1,2,0:T(8,128)}, f32[1024]{0:T(1024)S(1)}, /*index=5*/bf16...) while((s32[]{:T(128)}, f32[1024,64]{0,1:T(8,128)S(1)}, ...), condition=%wide.region_5.6_spmd.clone, body=%wide.region_1.5_spmd.clone.sunk | while | flops 150331776 | bytes 6096788 | solution.py:41
  278.7 1.0 fusion.45
  290.1 1.0 fusion.45
  292.4 1.0 fusion.45
  294.6 1.0 fusion.45
  301.5 1.0 fusion.45
  303.7 1.0 fusion.45
  306.0 1.0 fusion.45
  310.6 1.0 fusion.45
  312.9 1.0 fusion.45
  315.2 1.0 fusion.45
  319.7 1.0 fusion.45
  322.0 1.0 fusion.45
  326.5 1.0 fusion.45
  328.8 1.0 fusion.45
  329.8 3.7 copy.14
  333.8 1.0 fusion.20
  334.8 532.5 %reduce-scatter.7.cloned.1.call-done = f32[320,64]{1,0:T(8,128)} async-done(((f32[7680,64]{1,0:T(8,128)}), f32[320,64]{1,0:T(8,128)}) %reduce-scatter.7.cloned.1.call-update) | async-done | bytes 81936
  867.3 1.7 copy.13
  869.0 150.1 %reduce-scatter.5.cloned.1.call-done = f32[32,64]{1,0:T(8,128)} async-done(((f32[1024,64]{1,0:T(8,128)}), f32[32,64]{1,0:T(8,128)}) %reduce-scatter.5.cloned.1.call-update) | async-done | bytes 8208 | tf_op jit(solution)/shard_map/reduce_scatter | solution.py:64
  (141 shorter events, 40.8 us)
Async XLA Ops:
  7.2 165.8 %copy-start = (bf16[320,64]{0,1:T(8,128)(2,1)S(1)}, bf16[320,64]{0,1:T(8,128)(2,1)}, u32[]{:S(2)}) copy-start(bf16[320,64]{0,1:T(8,128)(2,1)} %param.8) | copy-start | bytes 122884
  7.2 860.2 %reduce-scatter.7.cloned.1.call-start = ((), (), s32[]{:S(2)}) async-start(), calls=%async_computation.3 | async-start | bytes 4096000
  333.6 685.6 %reduce-scatter.5.cloned.1.call-start = ((), (), s32[]{:S(2)}) async-start(), calls=%async_computation.2 | async-start | bytes 540672 | tf_op jit(solution)/shard_map/reduce_scatter | solution.py:64
Sparse Core Ops, SparseCore 0:
  333.7 533.6 reduce-scatter.6
  871.3 147.7 reduce-scatter.4
where the time goes:
time: 1030 us
  waiting for transfers between devices  683 us (66%)
  blocking collectives  268 us (26%)
  matrix products  53.3 us (5%)
  between operations  14.1 us (1%)
    unnamed x3, waiting for transfers between devices  533 us
    reduce_scatter x1, waiting for transfers between devices, body(): lax.psum_scatter(row_term, 'col', scatter_dimension=0, tiled=True)  150 us
    all_gather x1, blocking collectives, body(): lax.all_gather(col_points, 'row', axis=0, tiled=True)  102 us
    all_gather x1, blocking collectives, body(): lax.all_gather(col_probes, 'row', axis=0, tiled=True)  79.3 us
    all_gather x1, blocking collectives, body(): lax.all_gather(row_points, 'col', axis=0, tiled=True)  47 us
    all_gather x1, blocking collectives, body(): lax.all_gather(row_solves, 'col', axis=0, tiled=True)  39.2 us
    dot_general x24, matrix products, advance(): jnp.dot(weight.T, row_feat, preferred_element_type=jnp.float32)  23.6 us
  transfers between devices with their start and end apart: 2, of which 2 were waited for; matrix products, arithmetic and copies ran while one was open for 0% of the time, Pallas kernels for 0%

commit v1 on v0

v1 whole, which is shorter than its diff:
```python
import jax
import jax.numpy as jnp
from jax import lax
from jax.experimental import pallas as pl
from jax.experimental.pallas import tpu as pltpu
from jax.sharding import Mesh, PartitionSpec as P

f32, bf16 = jnp.float32, jnp.bfloat16

NAMES = ("y", "zh", "x", "zl", "core")
SIZES = (8, 3, 4, 4, 2)
Z = ("zh", "zl")
NY, NZ, NC = 8, 12, 8
PR, PC, F, Q = 32, 320, 64, 32
R, C = PR * NY * NZ, PC * NC
NORM, ONES = F + Q, F + Q + 3
BI, BJ = 256, 512

VM = pl.BlockSpec(memory_space=pltpu.VMEM)


def thirds(v):
    a = v.astype(bf16)
    v = v - a.astype(f32)
    b = v.astype(bf16)
    return a, b, (v - b.astype(f32)).astype(bf16)


def pack_kernel(rp_ref, rs_ref, cp_ref, cq_ref, row_ref, col_ref):
    r = rp_ref[...].astype(f32)
    n = -0.5 * jnp.sum(r * r, axis=1, keepdims=True)
    ext = jnp.concatenate(
        [p.astype(f32) for p in thirds(n)] + [jnp.ones((PR, 3), f32), jnp.zeros((PR, 128 - ONES - 3), f32)], axis=1
    )
    rec = jnp.concatenate([r, rs_ref[...].astype(f32), ext], axis=1).astype(bf16)
    for k in range(NZ):
        row_ref[k] = rec
    c = jnp.concatenate([cp_ref[...].astype(f32), cq_ref[...].astype(f32) * (1.0 / Q)], axis=0)
    half = jnp.concatenate([c[:48, 256:], c[48:, 256:]], axis=1)
    piece = jnp.concatenate([c[:, :128], c[:, 128:256], half], axis=0).astype(bf16)
    for k in range(NC):
        col_ref[k] = piece


def main_kernel(r_ref, p_ref, row_ref, col_ref, acc_r, acc_c, rt, ct, ce, cm, cn, w_ref):
    for d in range(0, NC, 2):
        for e in (d, d + 1):
            ct[:96, (2 * e) * 128:(2 * e + 1) * 128] = p_ref[e, :96]
            ct[:96, (2 * e + 1) * 128:(2 * e + 2) * 128] = p_ref[e, 96:192]
        a, b = p_ref[d, 192:240], p_ref[d + 1, 192:240]
        at = (2 * NC + d // 2) * 128
        ct[:48, at:at + 128] = jnp.concatenate([a[:, :64], b[:, :64]], axis=1)
        ct[48:96, at:at + 128] = jnp.concatenate([a[:, 64:], b[:, 64:]], axis=1)
    wide = ct[:F, :].astype(f32)
    n = -0.5 * jnp.sum(wide * wide, axis=0, keepdims=True)
    ct[96:128, :] = jnp.concatenate(
        [jnp.ones((3, C), f32)] + [p.astype(f32) for p in thirds(n)] + [jnp.zeros((26, C), f32)], axis=0
    ).astype(bf16)
    ce[...] = ct[...]
    ce[F:F + Q, :] = jnp.zeros((Q, C), bf16)
    cm[...] = jnp.zeros_like(cm)
    cm[F:F + Q, :] = ct[F:F + Q, :]
    cn[...] = ce[...].T
    rt[...] = r_ref[...].T
    acc_c[...] = jnp.zeros_like(acc_c)

    def step(i, carry):
        at = pl.multiple_of(i * BI, BI)
        r = r_ref[pl.ds(at, BI), :]
        for j in range(0, C, BJ):
            e = jnp.dot(r, ce[:, j:j + BJ], preferred_element_type=f32)
            m = jnp.dot(r, cm[:, j:j + BJ], preferred_element_type=f32)
            w_ref[:, j:j + BJ] = (jnp.exp(e) * m).astype(bf16)
        for j in range(0, C, BJ):
            acc_c[:, j:j + BJ] += jnp.dot(rt[:, pl.ds(at, BI)], w_ref[:, j:j + BJ], preferred_element_type=f32)
        acc_r[pl.ds(at, BI), :] = jnp.dot(w_ref[...], cn[...], preferred_element_type=f32)
        return carry

    lax.fori_loop(0, R // BI, step, 0)

    a = acc_r[...]
    t = a[:, :F] - a[:, NORM:NORM + 1] * r_ref[:, :F].astype(f32)
    t = t.reshape(R // PR, 2, PR // 2, F)
    row_ref[...] = jnp.concatenate([t[:, 0], t[:, 1]], axis=-1).reshape(R // 2, 128).astype(bf16)
    u = acc_c[:F, :] - acc_c[ONES:ONES + 1, :] * ct[:F, :].astype(f32)
    for d in range(NC):
        col_ref[d, :64] = u[:, (2 * d) * 128:(2 * d + 1) * 128].astype(bf16)
        col_ref[d, 64:128] = u[:, (2 * d + 1) * 128:(2 * d + 2) * 128].astype(bf16)
        at = 2 * NC * 128 + d * 64
        h = u[:, at:at + 64]
        col_ref[d, 128:] = jnp.concatenate([h[:32], h[32:]], axis=1).astype(bf16)


def finish_kernel(row_ref, col_ref, rg_ref, cg_ref):
    s = jnp.sum(row_ref[...].astype(f32), axis=0)
    rg_ref[...] = jnp.concatenate([s[:, :F], s[:, F:]], axis=0)
    s = jnp.sum(col_ref[...].astype(f32), axis=0)
    half = jnp.concatenate([s[128:, :64], s[128:, 64:]], axis=0)
    cg_ref[...] = jnp.concatenate([s[:64], s[64:128], half], axis=1)


def body(row_points, row_solves, col_points, col_probes):
    shape = jax.ShapeDtypeStruct
    rows, cols = pl.pallas_call(
        pack_kernel,
        out_shape=(shape((NZ, PR, 128), bf16), shape((NC, 240, 128), bf16)),
        in_specs=[VM] * 4,
        out_specs=(VM, VM),
    )(row_points, row_solves, col_points.T, col_probes.T)
    rows = lax.all_to_all(rows, Z, 0, 0, tiled=True)
    cols = lax.all_to_all(cols, ("x", "core"), 0, 0, tiled=True)
    rows = jnp.broadcast_to(rows.reshape(1, NZ * PR, 128), (NY, NZ * PR, 128))
    rows = lax.all_to_all(rows, "y", 0, 0, tiled=True)
    row_part, col_part = pl.pallas_call(
        main_kernel,
        out_shape=(shape((R // 2, 128), bf16), shape((NC, 160, 128), bf16)),
        in_specs=[VM, VM],
        out_specs=(VM, VM),
        scratch_shapes=[
            pltpu.VMEM((R, 128), f32),
            pltpu.VMEM((128, C), f32),
            pltpu.VMEM((128, R), bf16),
            pltpu.VMEM((128, C), bf16),
            pltpu.VMEM((128, C), bf16),
            pltpu.VMEM((128, C), bf16),
            pltpu.VMEM((C, 128), bf16),
            pltpu.VMEM((BI, C), bf16),
        ],
        compiler_params=pltpu.CompilerParams(vmem_limit_bytes=40 * 2**20),
    )(rows.reshape(R, 128), cols)
    row_part = lax.all_to_all(row_part.reshape(NY, NZ * PR // 2, 128), "y", 0, 0, tiled=True)
    row_part = jnp.sum(row_part.astype(f32), axis=0).astype(bf16).reshape(NZ, PR // 2, 128)
    row_part = lax.all_to_all(row_part, Z, 0, 0, tiled=True)
    col_part = lax.all_to_all(col_part, ("x", "core"), 0, 0, tiled=True)
    row_grad, col_grad = pl.pallas_call(
        finish_kernel,
        out_shape=(shape((PR, F), f32), shape((F, PC), f32)),
        in_specs=[VM, VM],
        out_specs=(VM, VM),
    )(row_part, col_part)
    return row_grad, col_grad.T


def solution(mesh):
    rings = Mesh(mesh.devices.reshape(SIZES), NAMES)
    row = P(("y", "zh", "x", "zl", "core"), None)
    col = P(("x", "zl", "core", "y", "zh"), None)
    return jax.shard_map(
        body,
        mesh=rings,
        in_specs=(row, row, col, col),
        out_specs=(row, col),
        check_vma=False,
    )
```

time: 1030 us -> 135 us (0.13)
  the two profiles are of different devices: /device:TPU:8 before, /device:TPU:2 now
where the time goes in v1:
time: 135 us; the launch traced here: 134 us
  blocking collectives  99.8 us (74%)
  Pallas kernels  22 us (16%)
  waiting for transfers between devices  6.75 us (5%)
  starting transfers between devices  4.8 us (4%)
    all_to_all x1, blocking collectives, body(): rows = lax.all_to_all(rows, 'y', 0, 0, tiled=True)  29.7 us
    all_to_all x1, blocking collectives, body(): rows = lax.all_to_all(rows, Z, 0, 0, tiled=True)  27.1 us
    pallas_call x1, Pallas kernels, body(): pl.pallas_call(main_kernel, out_shape=(shape((R // 2, 128), bf16), shape(...  18.4 us
    all_to_all x1, blocking collectives, body(): lax.all_to_all(row_part.reshape(NY, NZ * PR // 2, 128), 'y', 0, 0, tiled=...  15.6 us
    all_to_all x1, blocking collectives, body(): row_part = lax.all_to_all(row_part, Z, 0, 0, tiled=True)  14 us
    all_to_all x1, blocking collectives, body(): cols = lax.all_to_all(cols, ('x', 'core'), 0, 0, tiled=True)  13.4 us
    all_to_all x1, waiting for transfers between devices, body(): col_part = lax.all_to_all(col_part, ('x', 'core'), 0, 0, tiled=True)  6.75 us
    all_to_all x1, starting transfers between devices, body(): col_part = lax.all_to_all(col_part, ('x', 'core'), 0, 0, tiled=True)  4.8 us
  transfers between devices with their start and end apart: 1, of which 1 were waited for; matrix products, arithmetic and copies ran while one was open for 0% of the time, Pallas kernels for 0%

profile of v1, /device:TPU:2, one launch (start us, length us, event | category | flops | bytes accessed | tf_op | source)
XLA Modules:
  0.0 134.2 jit_solution(9702261095912100487)
XLA Ops:
  0.6 1.8 %shard_map.59 = (bf16[12,32,128]{2,1,0:T(8,128)(2,1)}, bf16[8,240,128]{2,1,0:T(8,128)(2,1)}) custom-call(bf16[32,64]{1,0:T(8,128)(2,1)} %rp_ref.1, bf16[32,32]{1,0:T(8,128)(2,1)} %rs_ref.1, bf16[64,320]{1,0:T(8,128)(2,1)} %bitcast.11, bf16[32,320]{1,0:T(8,128)(2,1)} %bitcast.12), custom_call_target="tpu_custom_call" | custom-call | tf_op jit(solution)/shard_map/pallas_call | solution.py:104
  2.4 27.1 %all_to_all.30 = bf16[12,32,128]{2,1,0:T(8,128)(2,1)S(1)} all-to-all(bf16[12,32,128]{2,1,0:T(8,128)(2,1)} %get-tuple-element.8), channel_id=1, replica_groups=mesh['y'=8,'zh'=3,'x'=4,'zl'=4,'core'=2] {'zh','zl'}, dimensions={0} | all-to-all | bytes 196608 | tf_op jit(solution)/shard_map/all_to_all | solution.py:110
  29.6 13.4 %all_to_all.31.p_ref = bf16[8,240,128]{2,1,0:T(8,128)(2,1)S(1)} all-to-all(bf16[8,240,128]{2,1,0:T(8,128)(2,1)} %get-tuple-element.9), channel_id=1, replica_groups=mesh['y'=8,'zh'=3,'x'=4,'zl'=4,'core'=2] {'x','core'}, dimensions={0} | all-to-all | bytes 983040 | tf_op jit(solution)/shard_map/all_to_all | solution.py:111
  43.0 0.1 broadcast_in_dim.8
  43.1 29.7 %all_to_all.32 = bf16[8,384,128]{2,1,0:T(8,128)(2,1)S(1)} all-to-all(bf16[8,384,128]{2,1,0:T(8,128)(2,1)S(1)} %broadcast_in_dim.8), channel_id=1, replica_groups=mesh['y'=8,'zh'=3,'x'=4,'zl'=4,'core'=2] {'y'}, dimensions={0} | all-to-all | bytes 1572864 | tf_op jit(solution)/shard_map/all_to_all | solution.py:113
  72.8 18.4 %shard_map.60 = (bf16[1536,128]{1,0:T(8,128)(2,1)S(1)}, bf16[8,160,128]{2,1,0:T(8,128)(2,1)}) custom-call(bf16[3072,128]{1,0:T(8,128)(2,1)S(1)} %bitcast.7, bf16[8,240,128]{2,1,0:T(8,128)(2,1)S(1)} %all_to_all.31.p_ref), custom_call_target="tpu_custom_call" | custom-call | tf_op jit(solution)/shard_map/pallas_call | solution.py:114
  91.2 15.6 %all_to_all.33 = bf16[8,192,128]{2,1,0:T(8,128)(2,1)S(1)} all-to-all(bf16[8,192,128]{2,1,0:T(8,128)(2,1)S(1)} %bitcast.8), channel_id=1, replica_groups=mesh['y'=8,'zh'=3,'x'=4,'zl'=4,'core'=2] {'y'}, dimensions={0} | all-to-all | bytes 786432 | tf_op jit(solution)/shard_map/all_to_all | solution.py:131
  106.8 4.8 %all-to-all-start.5 = ((bf16[8,160,128]{2,1,0:T(8,128)(2,1)}), bf16[8,160,128]{2,1,0:T(8,128)(2,1)S(1)}, u32[]{:S(2)}, u32[]{:S(2)}) async-start(bf16[8,160,128]{2,1,0:T(8,128)(2,1)} %get-tuple-element.11), calls=%async_computation.5 | async-start | bytes 655360 | tf_op jit(solution)/shard_map/all_to_all | solution.py:134
  111.6 0.1 reduce_sum.12
  111.7 6.8 %all-to-all-done.5.col_ref = bf16[8,160,128]{2,1,0:T(8,128)(2,1)S(1)} async-done(((bf16[8,160,128]{2,1,0:T(8,128)(2,1)}), bf16[8,160,128]{2,1,0:T(8,128)(2,1)S(1)}, u32[]{:S(2)}, u32[]{:S(2)}) %all-to-all-start.5) | async-done | bytes 327712 | tf_op jit(solution)/shard_map/all_to_all | solution.py:134
  118.4 0.0 copy-start
  118.4 14.0 %all_to_all.34.row_ref = bf16[12,16,128]{2,1,0:T(8,128)(2,1)} all-to-all(bf16[12,16,128]{2,1,0:T(8,128)(2,1)S(1)} %bitcast.10), channel_id=1, replica_groups=mesh['y'=8,'zh'=3,'x'=4,'zl'=4,'core'=2] {'zh','zl'}, dimensions={0} | all-to-all | bytes 98304 | tf_op jit(solution)/shard_map/all_to_all | solution.py:133
  132.4 0.0 copy-done
  132.4 1.7 %shard_map.61 = (f32[32,64]{1,0:T(8,128)}, f32[64,320]{1,0:T(8,128)}) custom-call(bf16[12,16,128]{2,1,0:T(8,128)(2,1)} %all_to_all.34.row_ref, bf16[8,160,128]{2,1,0:T(8,128)(2,1)} %copy-done), custom_call_target="tpu_custom_call" | custom-call | tf_op jit(solution)/shard_map/pallas_call | solution.py:135
Async XLA Ops:
  106.8 11.6 %all-to-all-start.5 = ((bf16[8,160,128]{2,1,0:T(8,128)(2,1)}), bf16[8,160,128]{2,1,0:T(8,128)(2,1)S(1)}, u32[]{:S(2)}, u32[]{:S(2)}) async-start(bf16[8,160,128]{2,1,0:T(8,128)(2,1)} %get-tuple-element.11), calls=%async_computation.5 | async-start | bytes 655360 | tf_op jit(solution)/shard_map/all_to_all | solution.py:134
  118.4 14.0 %copy-start = (bf16[8,160,128]{2,1,0:T(8,128)(2,1)}, bf16[8,160,128]{2,1,0:T(8,128)(2,1)S(1)}, u32[]{:S(2)}) copy-start(bf16[8,160,128]{2,1,0:T(8,128)(2,1)S(1)} %all-to-all-done.5.col_ref) | copy-start | bytes 983044

commit v2 on v1

v2 whole, which is shorter than its diff:
```python
import jax
import jax.numpy as jnp
from jax import lax
from jax.experimental import pallas as pl
from jax.experimental.pallas import tpu as pltpu
from jax.sharding import Mesh, PartitionSpec as P

f32, bf16 = jnp.float32, jnp.bfloat16

NAMES = ("y", "zh", "x", "zl", "core")
SIZES = (8, 3, 4, 4, 2)
Z = ("zh", "zl")
NY, NZ, NC = 8, 12, 8
PR, PC, F, Q = 32, 320, 64, 32
R, C = PR * NY * NZ, PC * NC
NORM, ONES = F + Q, F + Q + 3
BI, BJ = 768, 512
PK = BI * 3 // 4

VM = pl.BlockSpec(memory_space=pltpu.VMEM)


def thirds(v):
    a = v.astype(bf16)
    v = v - a.astype(f32)
    b = v.astype(bf16)
    return a, b, (v - b.astype(f32)).astype(bf16)


def pack_kernel(rp_ref, rs_ref, cp_ref, cq_ref, row_ref, col_ref):
    r, s = rp_ref[...].astype(f32), rs_ref[...].astype(f32)
    rec = jnp.concatenate(
        [
            jnp.concatenate([r[:16], r[16:]], axis=1),
            jnp.concatenate([s[:8], s[8:16], s[16:24], s[24:]], axis=1),
        ],
        axis=0,
    ).astype(bf16)
    for k in range(NZ):
        row_ref[k] = rec
    c = jnp.concatenate([cp_ref[...].astype(f32), cq_ref[...].astype(f32) * (1.0 / Q)], axis=0)
    half = jnp.concatenate([c[:48, 256:], c[48:, 256:]], axis=1)
    col_ref[...] = jnp.concatenate([c[:, :128], c[:, 128:256], half], axis=0).astype(bf16)


def column_records(p_ref, ct, ce, cm, cn):
    for d in range(0, NC, 2):
        for e in (d, d + 1):
            ct[:96, (2 * e) * 128:(2 * e + 1) * 128] = p_ref[e, :96]
            ct[:96, (2 * e + 1) * 128:(2 * e + 2) * 128] = p_ref[e, 96:192]
        a, b = p_ref[d, 192:240], p_ref[d + 1, 192:240]
        at = (2 * NC + d // 2) * 128
        ct[:48, at:at + 128] = jnp.concatenate([a[:, :64], b[:, :64]], axis=1)
        ct[48:96, at:at + 128] = jnp.concatenate([a[:, 64:], b[:, 64:]], axis=1)
    wide = ct[:F, :].astype(f32)
    n = -0.5 * jnp.sum(wide * wide, axis=0, keepdims=True)
    ct[96:128, :] = jnp.concatenate(
        [jnp.ones((3, C), f32)] + [p.astype(f32) for p in thirds(n)] + [jnp.zeros((26, C), f32)], axis=0
    ).astype(bf16)
    ce[...] = ct[...]
    ce[F:F + Q, :] = jnp.zeros((Q, C), bf16)
    cm[...] = jnp.zeros_like(cm)
    cm[F:F + Q, :] = ct[F:F + Q, :]
    cn[...] = ce[...].T


def row_records(packed):
    n = packed.shape[0] // 24
    rec = packed.astype(f32).reshape(n, 24, 128)
    points, solves = rec[:, :16], rec[:, 16:]

    def roll(x, k):
        return pltpu.roll(x.reshape(-1, 128), k, 1).reshape(x.shape)

    r = jnp.stack([points, roll(points, 64)], axis=1).reshape(n * PR, 128)
    s = jnp.stack([roll(solves, 64), roll(solves, 32), solves, roll(solves, 96)], axis=1).reshape(n * PR, 128)
    lane = lax.broadcasted_iota(jnp.int32, (n * PR, 128), 1)
    r = jnp.where(lane < F, r, 0.0)
    a, b, c = [t.astype(f32) for t in thirds(-0.5 * jnp.sum(r * r, axis=1, keepdims=True))]
    ext = jnp.where(lane < ONES + 3, 1.0, 0.0)
    ext = jnp.where(lane == NORM, a, jnp.where(lane == NORM + 1, b, jnp.where(lane == NORM + 2, c, ext)))
    return r, jnp.where(lane < F, r, jnp.where(lane < NORM, s, ext)).astype(bf16)


def main_kernel(r_ref, p_ref, row_ref, col_ref, acc_c, ct, ce, cm, cn, w0, w1, rt0, rt1, rf0, rf1):
    column_records(p_ref, ct, ce, cm, cn)
    acc_c[...] = jnp.zeros_like(acc_c)
    bufs = ((w0, rt0, rf0), (w1, rt1, rf1))
    n = R // BI

    def front(i, buf):
        r, rb = row_records(r_ref[pl.ds(pl.multiple_of(i * PK, PK), PK), :])
        buf[1][...] = rb.T
        buf[2][...] = r
        return rb

    def weights(rb, j, buf):
        e = jnp.dot(rb, ce[:, j:j + BJ], preferred_element_type=f32)
        m = jnp.dot(rb, cm[:, j:j + BJ], preferred_element_type=f32)
        buf[0][:, j:j + BJ] = (jnp.exp(e) * m).astype(bf16)

    def columns(j, buf):
        acc_c[:, j:j + BJ] += jnp.dot(buf[1][...], buf[0][:, j:j + BJ], preferred_element_type=f32)

    def rows(i, buf):
        a = jnp.dot(buf[0][...], cn[...], preferred_element_type=f32)
        t = a[:, :F] - a[:, NORM:NORM + 1] * buf[2][:, :F]
        t = t.reshape(BI // PR, 2, PR // 2, F)
        row_ref[pl.ds(pl.multiple_of(i * BI // 2, BI // 2), BI // 2), :] = (
            jnp.concatenate([t[:, 0], t[:, 1]], axis=-1).reshape(BI // 2, 128).astype(bf16)
        )

    def both(i, new, old):
        rb = front(i, new)
        for j in range(0, C, BJ):
            weights(rb, j, new)
            columns(j, old)
        rows(i - 1, old)

    rb = front(0, bufs[0])
    for j in range(0, C, BJ):
        weights(rb, j, bufs[0])

    def step(k, carry):
        both(2 * k + 1, bufs[1], bufs[0])
        both(2 * k + 2, bufs[0], bufs[1])
        return carry

    lax.fori_loop(0, (n - 2) // 2, step, 0)
    both(n - 1, bufs[1], bufs[0])
    for j in range(0, C, BJ):
        columns(j, bufs[1])
    rows(n - 1, bufs[1])

    u = acc_c[:F, :] - acc_c[ONES:ONES + 1, :] * ct[:F, :].astype(f32)
    for d in range(NC):
        col_ref[d, :64] = u[:, (2 * d) * 128:(2 * d + 1) * 128]
        col_ref[d, 64:128] = u[:, (2 * d + 1) * 128:(2 * d + 2) * 128]
        at = 2 * NC * 128 + d * 64
        h = u[:, at:at + 64]
        col_ref[d, 128:] = jnp.concatenate([h[:32], h[32:]], axis=1)


def finish_kernel(row_ref, col_ref, rg_ref, cg_ref):
    s = jnp.sum(row_ref[...].astype(f32), axis=0)
    rg_ref[...] = jnp.concatenate([s[:, :F], s[:, F:]], axis=0)
    s = col_ref[...]
    half = jnp.concatenate([s[128:, :64], s[128:, 64:]], axis=0)
    cg_ref[...] = jnp.concatenate([s[:64], s[64:128], half], axis=1)


def body(row_points, row_solves, col_points, col_probes):
    shape = jax.ShapeDtypeStruct
    rows, cols = pl.pallas_call(
        pack_kernel,
        out_shape=(shape((NZ, 24, 128), bf16), shape((240, 128), bf16)),
        in_specs=[VM] * 4,
        out_specs=(VM, VM),
    )(row_points, row_solves, col_points.T, col_probes.T)
    rows = lax.all_to_all(rows, Z, 0, 0, tiled=True)
    cols = lax.all_gather(cols, ("x", "core"), axis=0, tiled=False)
    rows = jnp.broadcast_to(rows.reshape(1, NZ * 24, 128), (NY, NZ * 24, 128))
    rows = lax.all_to_all(rows, "y", 0, 0, tiled=True)
    row_part, col_part = pl.pallas_call(
        main_kernel,
        out_shape=(shape((R // 2, 128), bf16), shape((NC, 160, 128), f32)),
        in_specs=[VM, VM],
        out_specs=(VM, VM),
        scratch_shapes=[
            pltpu.VMEM((128, C), f32),
            pltpu.VMEM((128, C), bf16),
            pltpu.VMEM((128, C), bf16),
            pltpu.VMEM((128, C), bf16),
            pltpu.VMEM((C, 128), bf16),
            pltpu.VMEM((BI, C), bf16),
            pltpu.VMEM((BI, C), bf16),
            pltpu.VMEM((128, BI), bf16),
            pltpu.VMEM((128, BI), bf16),
            pltpu.VMEM((BI, 128), f32),
            pltpu.VMEM((BI, 128), f32),
        ],
        compiler_params=pltpu.CompilerParams(vmem_limit_bytes=40 * 2**20),
    )(rows.reshape(R * 3 // 4, 128), cols)
    row_part = lax.all_to_all(row_part.reshape(NY, NZ * PR // 2, 128), "y", 0, 0, tiled=True)
    row_part = jnp.sum(row_part.astype(f32), axis=0).astype(bf16).reshape(NZ, PR // 2, 128)
    row_part = lax.all_to_all(row_part, Z, 0, 0, tiled=True)
    col_part = lax.psum_scatter(col_part.reshape(NC * 160, 128), ("x", "core"), scatter_dimension=0, tiled=True)
    row_grad, col_grad = pl.pallas_call(
        finish_kernel,
        out_shape=(shape((PR, F), f32), shape((F, PC), f32)),
        in_specs=[VM, VM],
        out_specs=(VM, VM),
    )(row_part, col_part)
    return row_grad, col_grad.T


def solution(mesh):
    rings = Mesh(mesh.devices.reshape(SIZES), NAMES)
    row = P(("y", "zh", "x", "zl", "core"), None)
    col = P(("x", "zl", "core", "y", "zh"), None)
    return jax.shard_map(
        body,
        mesh=rings,
        in_specs=(row, row, col, col),
        out_specs=(row, col),
        check_vma=False,
    )
```

time: 135 us -> 118 us (0.87)
  blocking collectives: 99.8 us -> 71.8 us
  between operations: 0.64 us -> 14 us
  waiting for transfers between devices: 6.75 us -> 3.96 us
  starting transfers between devices: 4.8 us -> 7.27 us
  Pallas kernels: 22 us -> 19.8 us
    all_to_all x2 -> x0, blocking collectives: 43.1 us -> none  [the longest x1 29.7 us: body(): rows = lax.all_to_all(rows, 'y', 0, 0, tiled=True)]
    all_gather x0 -> x1, blocking collectives: none -> 13.1 us  [body(): cols = lax.all_gather(cols, ('x', 'core'), axis=0, tiled=False)]
    all_to_all x1, waiting for transfers between devices: 6.75 us -> 3.94 us  [body(): rows = lax.all_to_all(rows, 'y', 0, 0, tiled=True)]
    all_to_all x1, blocking collectives: 15.6 us -> 18.2 us  [body(): lax.all_to_all(row_part.reshape(NY, NZ * PR // 2, 128), 'y', 0, 0, tiled=...]
    all_to_all x1, starting transfers between devices: 4.8 us -> 7.23 us  [body(): rows = lax.all_to_all(rows, 'y', 0, 0, tiled=True)]
    pallas_call x1, Pallas kernels: 18.4 us -> 16.6 us  [body(): pl.pallas_call(main_kernel, out_shape=(shape((R // 2, 128), bf16), shape(...]
  transfers between devices with their start and end apart: 1 -> 2, of which waited for: 1 -> 1; matrix products, arithmetic and copies ran while one was open for 0% -> 0% of each run, Pallas kernels for 0% -> 0%
where the time goes in v2:
time: 118 us
  blocking collectives  71.8 us (61%)
  Pallas kernels  19.8 us (17%)
  between operations  14 us (12%)
  starting transfers between devices  7.27 us (6%)
  waiting for transfers between devices  3.96 us (3%)
    all_to_all x1, blocking collectives, body(): rows = lax.all_to_all(rows, Z, 0, 0, tiled=True)  26.4 us
    all_to_all x1, blocking collectives, body(): lax.all_to_all(row_part.reshape(NY, NZ * PR // 2, 128), 'y', 0, 0, tiled=...  18.2 us
    pallas_call x1, Pallas kernels, body(): pl.pallas_call(main_kernel, out_shape=(shape((R // 2, 128), bf16), shape(...  16.6 us
    all_to_all x1, blocking collectives, body(): row_part = lax.all_to_all(row_part, Z, 0, 0, tiled=True)  14 us
    all_gather x1, blocking collectives, body(): cols = lax.all_gather(cols, ('x', 'core'), axis=0, tiled=False)  13.1 us
    all_to_all x1, starting transfers between devices, body(): rows = lax.all_to_all(rows, 'y', 0, 0, tiled=True)  7.23 us
    all_to_all x1, waiting for transfers between devices, body(): rows = lax.all_to_all(rows, 'y', 0, 0, tiled=True)  3.94 us
  transfers between devices with their start and end apart: 2, of which 1 were waited for; matrix products, arithmetic and copies ran while one was open for 0% of the time, Pallas kernels for 0%

profile of v2, /device:TPU:2, one launch (start us, length us, event | category | flops | bytes accessed | tf_op | source)
XLA Modules:
  0.0 117.8 jit_solution(6538968561412860393)
XLA Ops:
  7.2 1.6 %shard_map.59 = (bf16[12,24,128]{2,1,0:T(8,128)(2,1)}, bf16[240,128]{1,0:T(8,128)(2,1)}) custom-call(bf16[32,64]{1,0:T(8,128)(2,1)} %rp_ref.1, bf16[32,32]{1,0:T(8,128)(2,1)} %rs_ref.1, bf16[64,320]{1,0:T(8,128)(2,1)} %bitcast.14, bf16[32,320]{1,0:T(8,128)(2,1)} %bitcast.15), custom_call_target="tpu_custom_call" | custom-call | tf_op jit(solution)/shard_map/pallas_call | solution.py:154
  8.7 26.4 %all_to_all.20 = bf16[12,24,128]{2,1,0:T(8,128)(2,1)S(1)} all-to-all(bf16[12,24,128]{2,1,0:T(8,128)(2,1)} %get-tuple-element.8), channel_id=1, replica_groups=mesh['y'=8,'zh'=3,'x'=4,'zl'=4,'core'=2] {'zh','zl'}, dimensions={0} | all-to-all | bytes 147456 | tf_op jit(solution)/shard_map/all_to_all | solution.py:160
  35.1 0.9 broadcast_in_dim.8
  36.0 0.0 copy-start
  36.0 7.2 %all-to-all-start.1 = ((bf16[8,288,128]{2,1,0:T(8,128)(2,1)}), bf16[8,288,128]{2,1,0:T(8,128)(2,1)S(1)}, u32[]{:S(2)}, u32[]{:S(2)}) async-start(bf16[8,288,128]{2,1,0:T(8,128)(2,1)} %broadcast_in_dim.8), calls=%async_computation.1 | async-start | bytes 1179648 | tf_op jit(solution)/shard_map/all_to_all | solution.py:163
  43.2 0.0 reduce-scatter.2.cloned.1.call-start
  43.3 0.0 copy-done
  43.3 13.1 %all-gather = bf16[1920,128]{1,0:T(8,128)(2,1)S(1)} all-gather(bf16[240,128]{1,0:T(8,128)(2,1)S(1)} %copy-done), channel_id=2, replica_groups=mesh['y'=8,'zh'=3,'x'=4,'zl'=4,'core'=2] {'x','core'}, dimensions={0}, use_global_device_ids=true | all-gather | bytes 552960 | tf_op jit(solution)/shard_map/all_gather | solution.py:161
  56.4 3.9 %all-to-all-done.1 = bf16[8,288,128]{2,1,0:T(8,128)(2,1)S(1)} async-done(((bf16[8,288,128]{2,1,0:T(8,128)(2,1)}), bf16[8,288,128]{2,1,0:T(8,128)(2,1)S(1)}, u32[]{:S(2)}, u32[]{:S(2)}) %all-to-all-start.1) | async-done | bytes 589856 | tf_op jit(solution)/shard_map/all_to_all | solution.py:163
  60.4 16.6 %shard_map.60 = (bf16[1536,128]{1,0:T(8,128)(2,1)S(1)}, f32[8,160,128]{2,1,0:T(8,128)}) custom-call(bf16[2304,128]{1,0:T(8,128)(2,1)S(1)} %bitcast.9, bf16[8,240,128]{2,1,0:T(8,128)(2,1)S(1)} %bitcast.10), custom_call_target="tpu_custom_call" | custom-call | tf_op jit(solution)/shard_map/pallas_call | solution.py:164
  77.0 0.0 reduce-scatter.2.cloned.1.call-update
  77.0 18.2 %all_to_all.21 = bf16[8,192,128]{2,1,0:T(8,128)(2,1)S(1)} all-to-all(bf16[8,192,128]{2,1,0:T(8,128)(2,1)S(1)} %bitcast.11), channel_id=1, replica_groups=mesh['y'=8,'zh'=3,'x'=4,'zl'=4,'core'=2] {'y'}, dimensions={0} | all-to-all | bytes 786432 | tf_op jit(solution)/shard_map/all_to_all | solution.py:184
  95.2 0.1 reduce_sum.12
  95.3 14.0 %all_to_all.22.row_ref = bf16[12,16,128]{2,1,0:T(8,128)(2,1)} all-to-all(bf16[12,16,128]{2,1,0:T(8,128)(2,1)S(1)} %bitcast.13), channel_id=1, replica_groups=mesh['y'=8,'zh'=3,'x'=4,'zl'=4,'core'=2] {'zh','zl'}, dimensions={0} | all-to-all | bytes 98304 | tf_op jit(solution)/shard_map/all_to_all | solution.py:186
  109.3 0.0 reduce-scatter.2.cloned.1.call-done.col_ref
  109.3 1.6 %shard_map.61 = (f32[32,64]{1,0:T(8,128)}, f32[64,320]{1,0:T(8,128)}) custom-call(bf16[12,16,128]{2,1,0:T(8,128)(2,1)} %all_to_all.22.row_ref, f32[160,128]{1,0:T(8,128)} %reduce-scatter.2.cloned.1.call-done.col_ref), custom_call_target="tpu_custom_call" | custom-call | tf_op jit(solution)/shard_map/pallas_call | solution.py:188
Async XLA Ops:
  36.0 7.3 %copy-start = (bf16[240,128]{1,0:T(8,128)(2,1)S(1)}, bf16[240,128]{1,0:T(8,128)(2,1)}, u32[]{:S(2)}) copy-start(bf16[240,128]{1,0:T(8,128)(2,1)} %get-tuple-element.9) | copy-start | bytes 184324
  36.0 24.4 %all-to-all-start.1 = ((bf16[8,288,128]{2,1,0:T(8,128)(2,1)}), bf16[8,288,128]{2,1,0:T(8,128)(2,1)S(1)}, u32[]{:S(2)}, u32[]{:S(2)}) async-start(bf16[8,288,128]{2,1,0:T(8,128)(2,1)} %broadcast_in_dim.8), calls=%async_computation.1 | async-start | bytes 1179648 | tf_op jit(solution)/shard_map/all_to_all | solution.py:163
  43.2 66.0 %reduce-scatter.2.cloned.1.call-start = ((), (), s32[]{:S(2)}) async-start(), calls=%async_computation.5 | async-start | bytes 737280 | tf_op jit(solution)/shard_map/reduce_scatter | solution.py:187
Sparse Core Ops, SparseCore 0:
  77.1 26.3 reduce-scatter.1

commit v3 on v2

--- a/solution.py
+++ b/solution.py
@@ -10,7 +10,7 @@
 NAMES = ("y", "zh", "x", "zl", "core")
 SIZES = (8, 3, 4, 4, 2)
 Z = ("zh", "zl")
-NY, NZ, NC = 8, 12, 8
+NX, NY, NZ, NC = 4, 8, 12, 8
 PR, PC, F, Q = 32, 320, 64, 32
 R, C = PR * NY * NZ, PC * NC
 NORM, ONES = F + Q, F + Q + 3
@@ -18,6 +18,7 @@
 PK = BI * 3 // 4
 
 VM = pl.BlockSpec(memory_space=pltpu.VMEM)
+SMALL = pltpu.CompilerParams(vmem_limit_bytes=8 * 2**20)
 
 
 def thirds(v):
@@ -82,7 +83,7 @@
     return r, jnp.where(lane < F, r, jnp.where(lane < NORM, s, ext)).astype(bf16)
 
 
-def main_kernel(r_ref, p_ref, row_ref, col_ref, acc_c, ct, ce, cm, cn, w0, w1, rt0, rt1, rf0, rf1):
+def main_kernel(r_ref, p_ref, row_ref, keep_ref, swap_ref, acc_c, ct, ce, cm, cn, w0, w1, rt0, rt1, rf0, rf1):
     column_records(p_ref, ct, ce, cm, cn)
     acc_c[...] = jnp.zeros_like(acc_c)
     bufs = ((w0, rt0, rf0), (w1, rt1, rf1))
@@ -133,20 +134,43 @@
     rows(n - 1, bufs[1])
 
     u = acc_c[:F, :] - acc_c[ONES:ONES + 1, :] * ct[:F, :].astype(f32)
-    for d in range(NC):
-        col_ref[d, :64] = u[:, (2 * d) * 128:(2 * d + 1) * 128]
-        col_ref[d, 64:128] = u[:, (2 * d + 1) * 128:(2 * d + 2) * 128]
-        at = 2 * NC * 128 + d * 64
-        h = u[:, at:at + 64]
-        col_ref[d, 128:] = jnp.concatenate([h[:32], h[32:]], axis=1)
-
-
-def finish_kernel(row_ref, col_ref, rg_ref, cg_ref):
+
+    def piece(d):
+        h = u[:, 2 * NC * 128 + d * 64:2 * NC * 128 + d * 64 + 64]
+        return jnp.concatenate(
+            [
+                u[:, (2 * d) * 128:(2 * d + 1) * 128],
+                u[:, (2 * d + 1) * 128:(2 * d + 2) * 128],
+                jnp.concatenate([h[:32], h[32:]], axis=1),
+            ],
+            axis=0,
+        )
+
+    x, core = lax.axis_index("x"), lax.axis_index("core")
+    for i in range(NX):
+        k = lax.rem(i - x + NX, NX)
+        a, b = piece(2 * i), piece(2 * i + 1)
+        keep_ref[k] = jnp.where(core == 0, a, b)
+        swap_ref[k] = jnp.where(core == 0, b, a).astype(bf16)
+
+
+def add_kernel(keep_ref, swap_ref, own_ref, *out_refs):
+    own_ref[...] = keep_ref[0] + swap_ref[0].astype(f32)
+    for k in range(1, NX):
+        out_refs[k - 1][...] = (keep_ref[k] + swap_ref[k].astype(f32)).astype(bf16)
+
+
+def finish_rows(row_ref, out_ref):
     s = jnp.sum(row_ref[...].astype(f32), axis=0)
-    rg_ref[...] = jnp.concatenate([s[:, :F], s[:, F:]], axis=0)
-    s = col_ref[...]
+    out_ref[...] = jnp.concatenate([s[:, :F], s[:, F:]], axis=0)
+
+
+def finish_cols(own_ref, *refs):
+    s = own_ref[...]
+    for ref in refs[:-1]:
+        s = s + ref[...].astype(f32)
     half = jnp.concatenate([s[128:, :64], s[128:, 64:]], axis=0)
-    cg_ref[...] = jnp.concatenate([s[:64], s[64:128], half], axis=1)
+    refs[-1][...] = jnp.concatenate([s[:64], s[64:128], half], axis=1)
 
 
 def body(row_points, row_solves, col_points, col_probes):
@@ -161,11 +185,11 @@
     cols = lax.all_gather(cols, ("x", "core"), axis=0, tiled=False)
     rows = jnp.broadcast_to(rows.reshape(1, NZ * 24, 128), (NY, NZ * 24, 128))
     rows = lax.all_to_all(rows, "y", 0, 0, tiled=True)
-    row_part, col_part = pl.pallas_call(
+    row_part, keep, swap = pl.pallas_call(
         main_kernel,
-        out_shape=(shape((R // 2, 128), bf16), shape((NC, 160, 128), f32)),
+        out_shape=(shape((R // 2, 128), bf16), shape((NX, 160, 128), f32), shape((NX, 160, 128), bf16)),
         in_specs=[VM, VM],
-        out_specs=(VM, VM),
+        out_specs=(VM, VM, VM),
         scratch_shapes=[
             pltpu.VMEM((128, C), f32),
             pltpu.VMEM((128, C), bf16),
@@ -184,13 +208,29 @@
     row_part = lax.all_to_all(row_part.reshape(NY, NZ * PR // 2, 128), "y", 0, 0, tiled=True)
     row_part = jnp.sum(row_part.astype(f32), axis=0).astype(bf16).reshape(NZ, PR // 2, 128)
     row_part = lax.all_to_all(row_part, Z, 0, 0, tiled=True)
-    col_part = lax.psum_scatter(col_part.reshape(NC * 160, 128), ("x", "core"), scatter_dimension=0, tiled=True)
-    row_grad, col_grad = pl.pallas_call(
-        finish_kernel,
-        out_shape=(shape((PR, F), f32), shape((F, PC), f32)),
+    swap = lax.ppermute(swap, "core", [(0, 1), (1, 0)])
+    parts = pl.pallas_call(
+        add_kernel,
+        out_shape=(shape((160, 128), f32),) + (shape((160, 128), bf16),) * (NX - 1),
         in_specs=[VM, VM],
-        out_specs=(VM, VM),
-    )(row_part, col_part)
+        out_specs=(VM,) * NX,
+        compiler_params=SMALL,
+    )(keep, swap)
+    parts = [parts[0]] + [lax.ppermute(parts[k], "x", [(i, (i + k) % NX) for i in range(NX)]) for k in range(1, NX)]
+    col_grad = pl.pallas_call(
+        finish_cols,
+        out_shape=shape((F, PC), f32),
+        in_specs=[VM] * NX,
+        out_specs=VM,
+        compiler_params=SMALL,
+    )(*parts)
+    row_grad = pl.pallas_call(
+        finish_rows,
+        out_shape=shape((PR, F), f32),
+        in_specs=[VM],
+        out_specs=VM,
+        compiler_params=SMALL,
+    )(row_part)
     return row_grad, col_grad.T
 
 

time: 118 us -> 108 us (0.915)
  the two profiles are of different devices: /device:TPU:2 before, /device:TPU:64 now
where the time goes in v3:
time: 108 us
  blocking collectives  38 us (35%)
  starting transfers between devices  27.2 us (25%)
  waiting for transfers between devices  20.8 us (19%)
  Pallas kernels  19.5 us (18%)
    all_to_all x1, blocking collectives, body(): rows = lax.all_to_all(rows, Z, 0, 0, tiled=True)  24.6 us
    pallas_call x1, Pallas kernels, body(): pl.pallas_call(main_kernel, out_shape=(shape((R // 2, 128), bf16), shape(...  16.5 us
    all_gather x1, blocking collectives, body(): cols = lax.all_gather(cols, ('x', 'core'), axis=0, tiled=False)  13.4 us
    all_to_all x1, waiting for transfers between devices, body(): lax.all_to_all(row_part.reshape(NY, NZ * PR // 2, 128), 'y', 0, 0, tiled=...  13 us
    ppermute x3, starting transfers between devices, body(): lax.ppermute(parts[k], 'x', [(i, (i + k) % NX) for i in range(NX)])  9.82 us
    all_to_all x1, starting transfers between devices, body(): rows = lax.all_to_all(rows, 'y', 0, 0, tiled=True)  7.23 us
    all_to_all x1, starting transfers between devices, body(): row_part = lax.all_to_all(row_part, Z, 0, 0, tiled=True)  4.8 us
    all_to_all x1, waiting for transfers between devices, body(): rows = lax.all_to_all(rows, 'y', 0, 0, tiled=True)  4.04 us
  transfers between devices with their start and end apart: 7, of which 4 were waited for; matrix products, arithmetic and copies ran while one was open for 1% of the time, Pallas kernels for 1%

profile of v3, /device:TPU:64, one launch (start us, length us, event | category | flops | bytes accessed | tf_op | source)
XLA Modules:
  0.0 107.7 jit_solution(10313893535937038455)
XLA Ops:
  0.6 1.6 %shard_map.59 = (bf16[12,24,128]{2,1,0:T(8,128)(2,1)}, bf16[240,128]{1,0:T(8,128)(2,1)}) custom-call(bf16[32,64]{1,0:T(8,128)(2,1)} %rp_ref.1, bf16[32,32]{1,0:T(8,128)(2,1)} %rs_ref.1, bf16[64,320]{1,0:T(8,128)(2,1)} %bitcast.12, bf16[32,320]{1,0:T(8,128)(2,1)} %bitcast.13), custom_call_target="tpu_custom_call" | custom-call | tf_op jit(solution)/shard_map/pallas_call | solution.py:178
  2.2 24.6 %all_to_all.20 = bf16[12,24,128]{2,1,0:T(8,128)(2,1)S(1)} all-to-all(bf16[12,24,128]{2,1,0:T(8,128)(2,1)} %get-tuple-element.11), channel_id=1, replica_groups=mesh['y'=8,'zh'=3,'x'=4,'zl'=4,'core'=2] {'zh','zl'}, dimensions={0} | all-to-all | bytes 147456 | tf_op jit(solution)/shard_map/all_to_all | solution.py:184
  26.8 0.9 broadcast_in_dim.8
  27.6 0.0 copy-start
  27.6 7.2 %all-to-all-start.1 = ((bf16[8,288,128]{2,1,0:T(8,128)(2,1)}), bf16[8,288,128]{2,1,0:T(8,128)(2,1)S(1)}, u32[]{:S(2)}, u32[]{:S(2)}) async-start(bf16[8,288,128]{2,1,0:T(8,128)(2,1)} %broadcast_in_dim.8), calls=%async_computation.1 | async-start | bytes 1179648 | tf_op jit(solution)/shard_map/all_to_all | solution.py:187
  34.9 0.0 copy-done
  34.9 13.4 %all-gather = bf16[1920,128]{1,0:T(8,128)(2,1)S(1)} all-gather(bf16[240,128]{1,0:T(8,128)(2,1)S(1)} %copy-done), channel_id=2, replica_groups=mesh['y'=8,'zh'=3,'x'=4,'zl'=4,'core'=2] {'x','core'}, dimensions={0}, use_global_device_ids=true | all-gather | bytes 552960 | tf_op jit(solution)/shard_map/all_gather | solution.py:185
  48.3 4.0 %all-to-all-done.1 = bf16[8,288,128]{2,1,0:T(8,128)(2,1)S(1)} async-done(((bf16[8,288,128]{2,1,0:T(8,128)(2,1)}), bf16[8,288,128]{2,1,0:T(8,128)(2,1)S(1)}, u32[]{:S(2)}, u32[]{:S(2)}) %all-to-all-start.1) | async-done | bytes 589856 | tf_op jit(solution)/shard_map/all_to_all | solution.py:187
  52.4 16.5 %shard_map.60 = (bf16[1536,128]{1,0:T(8,128)(2,1)}, f32[4,160,128]{2,1,0:T(8,128)S(1)}, bf16[4,160,128]{2,1,0:T(8,128)(2,1)S(1)}) custom-call(bf16[2304,128]{1,0:T(8,128)(2,1)S(1)} %bitcast.8, bf16[8,240,128]{2,1,0:T(8,128)(2,1)S(1)} %bitcast.9), custom_call_target="tpu_custom_call" | custom-call | tf_op jit(solution)/shard_map/pallas_call | solution.py:188
  68.8 3.5 %all-to-all-start.2 = ((bf16[8,192,128]{2,1,0:T(8,128)(2,1)}), bf16[8,192,128]{2,1,0:T(8,128)(2,1)S(1)}, u32[]{:S(2)}, u32[]{:S(2)}) async-start(bf16[8,192,128]{2,1,0:T(8,128)(2,1)} %bitcast.5), calls=%async_computation.2 | async-start | bytes 786432 | tf_op jit(solution)/shard_map/all_to_all | solution.py:208
  72.3 1.9 %collective-permute-start = (bf16[4,160,128]{2,1,0:T(8,128)(2,1)S(1)}, bf16[4,160,128]{2,1,0:T(8,128)(2,1)S(1)}, u32[]{:S(2)}, u32[]{:S(2)}) collective-permute-start(bf16[4,160,128]{2,1,0:T(8,128)(2,1)S(1)} %get-tuple-element.15), channel_id=1, source_target_pairs={{0,1},{1,0},{2,3},{3,2},{4,5},{5,4},{6,7},{7,6},{8,9},{9,8},{10,11... | collective-permute-start | bytes 491528 | tf_op jit(solution)/shard_map/ppermute | solution.py:211
  74.2 13.0 %all-to-all-done.2 = bf16[8,192,128]{2,1,0:T(8,128)(2,1)S(1)} async-done(((bf16[8,192,128]{2,1,0:T(8,128)(2,1)}), bf16[8,192,128]{2,1,0:T(8,128)(2,1)S(1)}, u32[]{:S(2)}, u32[]{:S(2)}) %all-to-all-start.2) | async-done | bytes 393248 | tf_op jit(solution)/shard_map/all_to_all | solution.py:208
  87.2 0.7 reduce_sum.12
  87.8 4.8 %all-to-all-start.3 = ((bf16[12,16,128]{2,1,0:T(8,128)(2,1)}), bf16[12,16,128]{2,1,0:T(8,128)(2,1)S(1)}, u32[]{:S(2)}, u32[]{:S(2)}) async-start(bf16[12,16,128]{2,1,0:T(8,128)(2,1)} %bitcast.6), calls=%async_computation.3 | async-start | bytes 98304 | tf_op jit(solution)/shard_map/all_to_all | solution.py:210
  92.6 0.0 collective-permute-done.swap_ref
  92.7 3.1 %collective-permute-start.1 = (bf16[160,128]{1,0:T(8,128)(2,1)S(1)}, bf16[160,128]{1,0:T(8,128)(2,1)S(1)}, u32[]{:S(2)}, u32[]{:S(2)}) collective-permute-start(bf16[160,128]{1,0:T(8,128)(2,1)S(1)} %get-tuple-element.17), channel_id=1, source_target_pairs={{0,8},{8,16},{16,24},{24,0},{1,9},{9,17},{17,25},{25,1},{2,10},{10... | collective-permute-start | bytes 122888 | tf_op jit(solution)/shard_map/ppermute | solution.py:219
  95.8 4.6 %collective-permute-start.2 = (bf16[160,128]{1,0:T(8,128)(2,1)S(1)}, bf16[160,128]{1,0:T(8,128)(2,1)S(1)}, u32[]{:S(2)}, u32[]{:S(2)}) collective-permute-start(bf16[160,128]{1,0:T(8,128)(2,1)S(1)} %get-tuple-element.18), channel_id=1, source_target_pairs={{0,16},{8,24},{16,0},{24,8},{1,17},{9,25},{17,1},{25,9},{2,18},{10... | collective-permute-start | bytes 122888 | tf_op jit(solution)/shard_map/ppermute | solution.py:219
  100.4 2.1 %collective-permute-start.3 = (bf16[160,128]{1,0:T(8,128)(2,1)S(1)}, bf16[160,128]{1,0:T(8,128)(2,1)S(1)}, u32[]{:S(2)}, u32[]{:S(2)}) collective-permute-start(bf16[160,128]{1,0:T(8,128)(2,1)S(1)} %get-tuple-element.19), channel_id=1, source_target_pairs={{0,24},{8,0},{16,8},{24,16},{1,25},{9,1},{17,9},{25,17},{2,26},{10... | collective-permute-start | bytes 122888 | tf_op jit(solution)/shard_map/ppermute | solution.py:219
  102.5 0.0 collective-permute-done.1.refs_0_
  102.5 0.7 collective-permute-done.2.refs_1_
  103.2 3.1 %collective-permute-done.3.refs_2_ = bf16[160,128]{1,0:T(8,128)(2,1)S(1)} collective-permute-done((bf16[160,128]{1,0:T(8,128)(2,1)S(1)}, bf16[160,128]{1,0:T(8,128)(2,1)S(1)}, u32[]{:S(2)}, u32[]{:S(2)}) %collective-permute-start.3) | collective-permute-done | bytes 40992 | tf_op jit(solution)/shard_map/ppermute | solution.py:219
  106.3 0.7 shard_map.63
  107.0 0.0 all-to-all-done.3.row_ref
  107.0 0.7 shard_map.61
  (1 shorter events, 0.0 us)
Async XLA Ops:
  27.6 7.2 %copy-start = (bf16[240,128]{1,0:T(8,128)(2,1)S(1)}, bf16[240,128]{1,0:T(8,128)(2,1)}, u32[]{:S(2)}) copy-start(bf16[240,128]{1,0:T(8,128)(2,1)} %get-tuple-element.12) | copy-start | bytes 184324
  27.6 24.7 %all-to-all-start.1 = ((bf16[8,288,128]{2,1,0:T(8,128)(2,1)}), bf16[8,288,128]{2,1,0:T(8,128)(2,1)S(1)}, u32[]{:S(2)}, u32[]{:S(2)}) async-start(bf16[8,288,128]{2,1,0:T(8,128)(2,1)} %broadcast_in_dim.8), calls=%async_computation.1 | async-start | bytes 1179648 | tf_op jit(solution)/shard_map/all_to_all | solution.py:187
  68.8 18.4 %all-to-all-start.2 = ((bf16[8,192,128]{2,1,0:T(8,128)(2,1)}), bf16[8,192,128]{2,1,0:T(8,128)(2,1)S(1)}, u32[]{:S(2)}, u32[]{:S(2)}) async-start(bf16[8,192,128]{2,1,0:T(8,128)(2,1)} %bitcast.5), calls=%async_computation.2 | async-start | bytes 786432 | tf_op jit(solution)/shard_map/all_to_all | solution.py:208
  72.3 20.4 %collective-permute-start = (bf16[4,160,128]{2,1,0:T(8,128)(2,1)S(1)}, bf16[4,160,128]{2,1,0:T(8,128)(2,1)S(1)}, u32[]{:S(2)}, u32[]{:S(2)}) collective-permute-start(bf16[4,160,128]{2,1,0:T(8,128)(2,1)S(1)} %get-tuple-element.15), channel_id=1, source_target_pairs={{0,1},{1,0},{2,3},{3,2},{4,5},{5,4},{6,7},{7,6},{8,9},{9,8},{10,11... | collective-permute-start | bytes 491528 | tf_op jit(solution)/shard_map/ppermute | solution.py:211
  87.8 19.2 %all-to-all-start.3 = ((bf16[12,16,128]{2,1,0:T(8,128)(2,1)}), bf16[12,16,128]{2,1,0:T(8,128)(2,1)S(1)}, u32[]{:S(2)}, u32[]{:S(2)}) async-start(bf16[12,16,128]{2,1,0:T(8,128)(2,1)} %bitcast.6), calls=%async_computation.3 | async-start | bytes 98304 | tf_op jit(solution)/shard_map/all_to_all | solution.py:210
  92.7 9.8 %collective-permute-start.1 = (bf16[160,128]{1,0:T(8,128)(2,1)S(1)}, bf16[160,128]{1,0:T(8,128)(2,1)S(1)}, u32[]{:S(2)}, u32[]{:S(2)}) collective-permute-start(bf16[160,128]{1,0:T(8,128)(2,1)S(1)} %get-tuple-element.17), channel_id=1, source_target_pairs={{0,8},{8,16},{16,24},{24,0},{1,9},{9,17},{17,25},{25,1},{2,10},{10... | collective-permute-start | bytes 122888 | tf_op jit(solution)/shard_map/ppermute | solution.py:219
  95.8 7.4 %collective-permute-start.2 = (bf16[160,128]{1,0:T(8,128)(2,1)S(1)}, bf16[160,128]{1,0:T(8,128)(2,1)S(1)}, u32[]{:S(2)}, u32[]{:S(2)}) collective-permute-start(bf16[160,128]{1,0:T(8,128)(2,1)S(1)} %get-tuple-element.18), channel_id=1, source_target_pairs={{0,16},{8,24},{16,0},{24,8},{1,17},{9,25},{17,1},{25,9},{2,18},{10... | collective-permute-start | bytes 122888 | tf_op jit(solution)/shard_map/ppermute | solution.py:219
  100.4 5.9 %collective-permute-start.3 = (bf16[160,128]{1,0:T(8,128)(2,1)S(1)}, bf16[160,128]{1,0:T(8,128)(2,1)S(1)}, u32[]{:S(2)}, u32[]{:S(2)}) collective-permute-start(bf16[160,128]{1,0:T(8,128)(2,1)S(1)} %get-tuple-element.19), channel_id=1, source_target_pairs={{0,24},{8,0},{16,8},{24,16},{1,25},{9,1},{17,9},{25,17},{2,26},{10... | collective-permute-start | bytes 122888 | tf_op jit(solution)/shard_map/ppermute | solution.py:219

commit v4 on v3

--- a/solution.py
+++ b/solution.py
@@ -10,11 +10,11 @@
 NAMES = ("y", "zh", "x", "zl", "core")
 SIZES = (8, 3, 4, 4, 2)
 Z = ("zh", "zl")
-NX, NY, NZ, NC = 4, 8, 12, 8
+NX, NY, NZ, NC = 4, 8, 12, 2
 PR, PC, F, Q = 32, 320, 64, 32
-R, C = PR * NY * NZ, PC * NC
+R, C = PR * NX * NZ * NC, PC * NY
 NORM, ONES = F + Q, F + Q + 3
-BI, BJ = 768, 512
+BI, BJ = R // NX, 512
 PK = BI * 3 // 4
 
 VM = pl.BlockSpec(memory_space=pltpu.VMEM)
@@ -41,16 +41,18 @@
         row_ref[k] = rec
     c = jnp.concatenate([cp_ref[...].astype(f32), cq_ref[...].astype(f32) * (1.0 / Q)], axis=0)
     half = jnp.concatenate([c[:48, 256:], c[48:, 256:]], axis=1)
-    col_ref[...] = jnp.concatenate([c[:, :128], c[:, 128:256], half], axis=0).astype(bf16)
+    piece = jnp.concatenate([c[:, :128], c[:, 128:256], half], axis=0).astype(bf16)
+    for k in range(NY):
+        col_ref[k] = piece
 
 
 def column_records(p_ref, ct, ce, cm, cn):
-    for d in range(0, NC, 2):
+    for d in range(0, NY, 2):
         for e in (d, d + 1):
             ct[:96, (2 * e) * 128:(2 * e + 1) * 128] = p_ref[e, :96]
             ct[:96, (2 * e + 1) * 128:(2 * e + 2) * 128] = p_ref[e, 96:192]
         a, b = p_ref[d, 192:240], p_ref[d + 1, 192:240]
-        at = (2 * NC + d // 2) * 128
+        at = (2 * NY + d // 2) * 128
         ct[:48, at:at + 128] = jnp.concatenate([a[:, :64], b[:, :64]], axis=1)
         ct[48:96, at:at + 128] = jnp.concatenate([a[:, 64:], b[:, 64:]], axis=1)
     wide = ct[:F, :].astype(f32)
@@ -83,11 +85,12 @@
     return r, jnp.where(lane < F, r, jnp.where(lane < NORM, s, ext)).astype(bf16)
 
 
-def main_kernel(r_ref, p_ref, row_ref, keep_ref, swap_ref, acc_c, ct, ce, cm, cn, w0, w1, rt0, rt1, rf0, rf1):
+def main_kernel(r_ref, p_ref, keep_ref, swap_ref, col_ref, acc_c, ct, ce, cm, cn, w0, w1, rt0, rt1, rf0, rf1):
     column_records(p_ref, ct, ce, cm, cn)
     acc_c[...] = jnp.zeros_like(acc_c)
     bufs = ((w0, rt0, rf0), (w1, rt1, rf1))
     n = R // BI
+    x, core = lax.axis_index("x"), lax.axis_index("core")
 
     def front(i, buf):
         r, rb = row_records(r_ref[pl.ds(pl.multiple_of(i * PK, PK), PK), :])
@@ -107,9 +110,11 @@
         a = jnp.dot(buf[0][...], cn[...], preferred_element_type=f32)
         t = a[:, :F] - a[:, NORM:NORM + 1] * buf[2][:, :F]
         t = t.reshape(BI // PR, 2, PR // 2, F)
-        row_ref[pl.ds(pl.multiple_of(i * BI // 2, BI // 2), BI // 2), :] = (
-            jnp.concatenate([t[:, 0], t[:, 1]], axis=-1).reshape(BI // 2, 128).astype(bf16)
-        )
+        t = jnp.concatenate([t[:, 0], t[:, 1]], axis=-1).reshape(BI // 2, 128)
+        k = lax.rem(i - x + NX, NX)
+        a, b = t[:BI // 4], t[BI // 4:]
+        keep_ref[k] = jnp.where(core == 0, a, b)
+        swap_ref[k] = jnp.where(core == 0, b, a).astype(bf16)
 
     def both(i, new, old):
         rb = front(i, new)
@@ -135,23 +140,11 @@
 
     u = acc_c[:F, :] - acc_c[ONES:ONES + 1, :] * ct[:F, :].astype(f32)
 
-    def piece(d):
-        h = u[:, 2 * NC * 128 + d * 64:2 * NC * 128 + d * 64 + 64]
-        return jnp.concatenate(
-            [
-                u[:, (2 * d) * 128:(2 * d + 1) * 128],
-                u[:, (2 * d + 1) * 128:(2 * d + 2) * 128],
-                jnp.concatenate([h[:32], h[32:]], axis=1),
-            ],
-            axis=0,
-        )
-
-    x, core = lax.axis_index("x"), lax.axis_index("core")
-    for i in range(NX):
-        k = lax.rem(i - x + NX, NX)
-        a, b = piece(2 * i), piece(2 * i + 1)
-        keep_ref[k] = jnp.where(core == 0, a, b)
-        swap_ref[k] = jnp.where(core == 0, b, a).astype(bf16)
+    for d in range(NY):
+        col_ref[d, :64] = u[:, (2 * d) * 128:(2 * d + 1) * 128].astype(bf16)
+        col_ref[d, 64:128] = u[:, (2 * d + 1) * 128:(2 * d + 2) * 128].astype(bf16)
+        h = u[:, 2 * NY * 128 + d * 64:2 * NY * 128 + d * 64 + 64]
+        col_ref[d, 128:] = jnp.concatenate([h[:32], h[32:]], axis=1).astype(bf16)
 
 
 def add_kernel(keep_ref, swap_ref, own_ref, *out_refs):
@@ -165,29 +158,28 @@
     out_ref[...] = jnp.concatenate([s[:, :F], s[:, F:]], axis=0)
 
 
-def finish_cols(own_ref, *refs):
-    s = own_ref[...]
-    for ref in refs[:-1]:
-        s = s + ref[...].astype(f32)
+def finish_cols(col_ref, out_ref):
+    s = jnp.sum(col_ref[...].astype(f32), axis=0)
     half = jnp.concatenate([s[128:, :64], s[128:, 64:]], axis=0)
-    refs[-1][...] = jnp.concatenate([s[:64], s[64:128], half], axis=1)
+    out_ref[...] = jnp.concatenate([s[:64], s[64:128], half], axis=1)
 
 
 def body(row_points, row_solves, col_points, col_probes):
     shape = jax.ShapeDtypeStruct
     rows, cols = pl.pallas_call(
         pack_kernel,
-        out_shape=(shape((NZ, 24, 128), bf16), shape((240, 128), bf16)),
+        out_shape=(shape((NZ, 24, 128), bf16), shape((NY, 240, 128), bf16)),
         in_specs=[VM] * 4,
         out_specs=(VM, VM),
     )(row_points, row_solves, col_points.T, col_probes.T)
     rows = lax.all_to_all(rows, Z, 0, 0, tiled=True)
-    cols = lax.all_gather(cols, ("x", "core"), axis=0, tiled=False)
-    rows = jnp.broadcast_to(rows.reshape(1, NZ * 24, 128), (NY, NZ * 24, 128))
-    rows = lax.all_to_all(rows, "y", 0, 0, tiled=True)
-    row_part, keep, swap = pl.pallas_call(
+    rows, cols = lax.optimization_barrier((rows, cols))
+    cols = lax.all_to_all(cols, "y", 0, 0, tiled=True)
+    rows = lax.all_gather(rows.reshape(NZ * 24, 128), ("x", "core"), axis=0, tiled=True)
+    part = R // (2 * NX * NC)
+    keep, swap, col_part = pl.pallas_call(
         main_kernel,
-        out_shape=(shape((R // 2, 128), bf16), shape((NX, 160, 128), f32), shape((NX, 160, 128), bf16)),
+        out_shape=(shape((NX, part, 128), f32), shape((NX, part, 128), bf16), shape((NY, 160, 128), bf16)),
         in_specs=[VM, VM],
         out_specs=(VM, VM, VM),
         scratch_shapes=[
@@ -204,26 +196,22 @@
             pltpu.VMEM((BI, 128), f32),
         ],
         compiler_params=pltpu.CompilerParams(vmem_limit_bytes=40 * 2**20),
-    )(rows.reshape(R * 3 // 4, 128), cols)
-    row_part = lax.all_to_all(row_part.reshape(NY, NZ * PR // 2, 128), "y", 0, 0, tiled=True)
-    row_part = jnp.sum(row_part.astype(f32), axis=0).astype(bf16).reshape(NZ, PR // 2, 128)
-    row_part = lax.all_to_all(row_part, Z, 0, 0, tiled=True)
+    )(rows, cols)
+    col_part = lax.all_to_all(col_part, "y", 0, 0, tiled=True)
     swap = lax.ppermute(swap, "core", [(0, 1), (1, 0)])
     parts = pl.pallas_call(
         add_kernel,
-        out_shape=(shape((160, 128), f32),) + (shape((160, 128), bf16),) * (NX - 1),
+        out_shape=(shape((part, 128), f32),) + (shape((part, 128), bf16),) * (NX - 1),
         in_specs=[VM, VM],
         out_specs=(VM,) * NX,
         compiler_params=SMALL,
     )(keep, swap)
-    parts = [parts[0]] + [lax.ppermute(parts[k], "x", [(i, (i + k) % NX) for i in range(NX)]) for k in range(1, NX)]
-    col_grad = pl.pallas_call(
-        finish_cols,
-        out_shape=shape((F, PC), f32),
-        in_specs=[VM] * NX,
-        out_specs=VM,
-        compiler_params=SMALL,
-    )(*parts)
+    row_part = parts[0]
+    for k in range(1, NX):
+        row_part = row_part + lax.ppermute(parts[k], "x", [(i, (i + k) % NX) for i in range(NX)]).astype(f32)
+    row_part = row_part.astype(bf16).reshape(NZ, PR // 2, 128)
+    row_part, col_part = lax.optimization_barrier((row_part, col_part))
+    row_part = lax.all_to_all(row_part, Z, 0, 0, tiled=True)
     row_grad = pl.pallas_call(
         finish_rows,
         out_shape=shape((PR, F), f32),
@@ -231,6 +219,13 @@
         out_specs=VM,
         compiler_params=SMALL,
     )(row_part)
+    col_grad = pl.pallas_call(
+        finish_cols,
+        out_shape=shape((F, PC), f32),
+        in_specs=[VM],
+        out_specs=VM,
+        compiler_params=SMALL,
+    )(col_part)
     return row_grad, col_grad.T
 
 

time: 108 us -> 107 us (level)
  the two profiles are of different devices: /device:TPU:64 before, /device:TPU:8 now
where the time goes in v4:
time: 107 us; the launch traced here: 106 us
  blocking collectives  39.9 us (37%)
  starting transfers between devices  29.9 us (28%)
  Pallas kernels  19.6 us (18%)
  waiting for transfers between devices  15.3 us (14%)
    all_to_all x1, blocking collectives, body(): rows = lax.all_to_all(rows, Z, 0, 0, tiled=True)  26.4 us
    pallas_call x1, Pallas kernels, body(): pl.pallas_call(main_kernel, out_shape=(shape((NX, part, 128), f32), shape...  16.4 us
    all_gather x1, blocking collectives, body(): lax.all_gather(rows.reshape(NZ * 24, 128), ('x', 'core'), axis=0, tiled=T...  13.5 us
    all_to_all x1, waiting for transfers between devices, body(): row_part = lax.all_to_all(row_part, Z, 0, 0, tiled=True)  10 us
    ppermute x3, starting transfers between devices, body(): lax.ppermute(parts[k], 'x', [(i, (i + k) % NX) for i in range(NX)])  9.82 us
    all_to_all x1, starting transfers between devices, body(): cols = lax.all_to_all(cols, 'y', 0, 0, tiled=True)  7.55 us
    all_to_all x1, starting transfers between devices, body(): col_part = lax.all_to_all(col_part, 'y', 0, 0, tiled=True)  7.17 us
    ppermute x3, waiting for transfers between devices, body(): lax.ppermute(parts[k], 'x', [(i, (i + k) % NX) for i in range(NX)])  3.83 us
  transfers between devices with their start and end apart: 7, of which 5 were waited for; matrix products, arithmetic and copies ran while one was open for 1% of the time, Pallas kernels for 1%

profile of v4, /device:TPU:8, one launch (start us, length us, event | category | flops | bytes accessed | tf_op | source)
XLA Modules:
  0.0 106.1 jit_solution(6350896670512565746)
XLA Ops:
  0.6 1.7 %shard_map.59 = (bf16[12,24,128]{2,1,0:T(8,128)(2,1)}, bf16[8,240,128]{2,1,0:T(8,128)(2,1)}) custom-call(bf16[32,64]{1,0:T(8,128)(2,1)} %rp_ref.1, bf16[32,32]{1,0:T(8,128)(2,1)} %rs_ref.1, bf16[64,320]{1,0:T(8,128)(2,1)} %bitcast.7, bf16[32,320]{1,0:T(8,128)(2,1)} %bitcast.8), custom_call_target="tpu_custom_call" | custom-call | tf_op jit(solution)/shard_map/pallas_call | solution.py:169
  2.4 26.4 %all_to_all.20 = bf16[12,24,128]{2,1,0:T(8,128)(2,1)S(1)} all-to-all(bf16[12,24,128]{2,1,0:T(8,128)(2,1)} %get-tuple-element.15), channel_id=1, replica_groups=mesh['y'=8,'zh'=3,'x'=4,'zl'=4,'core'=2] {'zh','zl'}, dimensions={0} | all-to-all | bytes 147456 | tf_op jit(solution)/shard_map/all_to_all | solution.py:175
  28.7 7.5 %all-to-all-start.1 = ((bf16[8,240,128]{2,1,0:T(8,128)(2,1)}), bf16[8,240,128]{2,1,0:T(8,128)(2,1)S(1)}, u32[]{:S(2)}, u32[]{:S(2)}) async-start(bf16[8,240,128]{2,1,0:T(8,128)(2,1)} %get-tuple-element.18), calls=%async_computation.1 | async-start | bytes 983040 | tf_op jit(solution)/shard_map/all_to_all | solution.py:177
  36.3 13.5 %all_gather.3.r_ref = bf16[2304,128]{1,0:T(8,128)(2,1)S(1)} all-gather(bf16[288,128]{1,0:T(8,128)(2,1)S(1)} %bitcast.5), channel_id=1, replica_groups=mesh['y'=8,'zh'=3,'x'=4,'zl'=4,'core'=2] {'x','core'}, dimensions={0}, use_global_device_ids=true | all-gather | bytes 663552 | tf_op jit(solution)/shard_map/all_gather | solution.py:178
  49.8 0.1 all-to-all-done.1.p_ref
  49.9 16.4 %shard_map.60 = (f32[4,192,128]{2,1,0:T(8,128)S(1)}, bf16[4,192,128]{2,1,0:T(8,128)(2,1)S(1)}, bf16[8,160,128]{2,1,0:T(8,128)(2,1)}) custom-call(bf16[2304,128]{1,0:T(8,128)(2,1)S(1)} %all_gather.3.r_ref, bf16[8,240,128]{2,1,0:T(8,128)(2,1)S(1)} %all-to-all-done.1.p_ref), custom_call_target="tpu_custom_call" | custom-call | tf_op jit(solution)/shard_map/pallas_call | solution.py:180
  66.3 7.2 %all-to-all-start.2 = ((bf16[8,160,128]{2,1,0:T(8,128)(2,1)}), bf16[8,160,128]{2,1,0:T(8,128)(2,1)S(1)}, u32[]{:S(2)}, u32[]{:S(2)}) async-start(bf16[8,160,128]{2,1,0:T(8,128)(2,1)} %get-tuple-element.25), calls=%async_computation.2 | async-start | bytes 655360 | tf_op jit(solution)/shard_map/all_to_all | solution.py:200
  73.5 1.9 %collective-permute-start = (bf16[4,192,128]{2,1,0:T(8,128)(2,1)S(1)}, bf16[4,192,128]{2,1,0:T(8,128)(2,1)S(1)}, u32[]{:S(2)}, u32[]{:S(2)}) collective-permute-start(bf16[4,192,128]{2,1,0:T(8,128)(2,1)S(1)} %get-tuple-element.20), channel_id=1, source_target_pairs={{0,1},{1,0},{2,3},{3,2},{4,5},{5,4},{6,7},{7,6},{8,9},{9,8},{10,11... | collective-permute-start | bytes 589832 | tf_op jit(solution)/shard_map/ppermute | solution.py:201
  75.4 1.4 %collective-permute-done.swap_ref = bf16[4,192,128]{2,1,0:T(8,128)(2,1)S(1)} collective-permute-done((bf16[4,192,128]{2,1,0:T(8,128)(2,1)S(1)}, bf16[4,192,128]{2,1,0:T(8,128)(2,1)S(1)}, u32[]{:S(2)}, u32[]{:S(2)}) %collective-permute-start) | collective-permute-done | bytes 196640 | tf_op jit(solution)/shard_map/ppermute | solution.py:201
  76.8 3.1 %collective-permute-start.1 = (bf16[192,128]{1,0:T(8,128)(2,1)S(1)}, bf16[192,128]{1,0:T(8,128)(2,1)S(1)}, u32[]{:S(2)}, u32[]{:S(2)}) collective-permute-start(bf16[192,128]{1,0:T(8,128)(2,1)S(1)} %get-tuple-element.22), channel_id=1, source_target_pairs={{0,8},{8,16},{16,24},{24,0},{1,9},{9,17},{17,25},{25,1},{2,10},{10... | collective-permute-start | bytes 147464 | tf_op jit(solution)/shard_map/ppermute | solution.py:211
  79.9 4.6 %collective-permute-start.2 = (bf16[192,128]{1,0:T(8,128)(2,1)S(1)}, bf16[192,128]{1,0:T(8,128)(2,1)S(1)}, u32[]{:S(2)}, u32[]{:S(2)}) collective-permute-start(bf16[192,128]{1,0:T(8,128)(2,1)S(1)} %get-tuple-element.23), channel_id=1, source_target_pairs={{0,16},{8,24},{16,0},{24,8},{1,17},{9,25},{17,1},{25,9},{2,18},{10... | collective-permute-start | bytes 147464 | tf_op jit(solution)/shard_map/ppermute | solution.py:211
  84.5 2.1 %collective-permute-start.3 = (bf16[192,128]{1,0:T(8,128)(2,1)S(1)}, bf16[192,128]{1,0:T(8,128)(2,1)S(1)}, u32[]{:S(2)}, u32[]{:S(2)}) collective-permute-start(bf16[192,128]{1,0:T(8,128)(2,1)S(1)} %get-tuple-element.24), channel_id=1, source_target_pairs={{0,24},{8,0},{16,8},{24,16},{1,25},{9,1},{17,9},{25,17},{2,26},{10... | collective-permute-start | bytes 147464 | tf_op jit(solution)/shard_map/ppermute | solution.py:211
  86.7 0.0 collective-permute-done.1
  86.7 0.7 collective-permute-done.2
  87.4 3.1 %collective-permute-done.3 = bf16[192,128]{1,0:T(8,128)(2,1)S(1)} collective-permute-done((bf16[192,128]{1,0:T(8,128)(2,1)S(1)}, bf16[192,128]{1,0:T(8,128)(2,1)S(1)}, u32[]{:S(2)}, u32[]{:S(2)}) %collective-permute-start.3) | collective-permute-done | bytes 49184 | tf_op jit(solution)/shard_map/ppermute | solution.py:211
  90.5 0.6 add_convert_fusion
  91.2 0.0 all-to-all-done.2.col_ref
  91.2 3.5 %all-to-all-start.3 = ((bf16[12,16,128]{2,1,0:T(8,128)(2,1)}), bf16[12,16,128]{2,1,0:T(8,128)(2,1)S(1)}, u32[]{:S(2)}, u32[]{:S(2)}) async-start(bf16[12,16,128]{2,1,0:T(8,128)(2,1)} %bitcast.3), calls=%async_computation.3 | async-start | bytes 98304 | tf_op jit(solution)/shard_map/all_to_all | solution.py:214
  94.7 0.7 shard_map.63
  95.4 10.0 %all-to-all-done.3.row_ref = bf16[12,16,128]{2,1,0:T(8,128)(2,1)S(1)} async-done(((bf16[12,16,128]{2,1,0:T(8,128)(2,1)}), bf16[12,16,128]{2,1,0:T(8,128)(2,1)S(1)}, u32[]{:S(2)}, u32[]{:S(2)}) %all-to-all-start.3) | async-done | bytes 49184 | tf_op jit(solution)/shard_map/all_to_all | solution.py:214
  105.4 0.7 shard_map.62
  (1 shorter events, 0.0 us)
Async XLA Ops:
  28.7 21.1 %all-to-all-start.1 = ((bf16[8,240,128]{2,1,0:T(8,128)(2,1)}), bf16[8,240,128]{2,1,0:T(8,128)(2,1)S(1)}, u32[]{:S(2)}, u32[]{:S(2)}) async-start(bf16[8,240,128]{2,1,0:T(8,128)(2,1)} %get-tuple-element.18), calls=%async_computation.1 | async-start | bytes 983040 | tf_op jit(solution)/shard_map/all_to_all | solution.py:177
  66.3 24.9 %all-to-all-start.2 = ((bf16[8,160,128]{2,1,0:T(8,128)(2,1)}), bf16[8,160,128]{2,1,0:T(8,128)(2,1)S(1)}, u32[]{:S(2)}, u32[]{:S(2)}) async-start(bf16[8,160,128]{2,1,0:T(8,128)(2,1)} %get-tuple-element.25), calls=%async_computation.2 | async-start | bytes 655360 | tf_op jit(solution)/shard_map/all_to_all | solution.py:200
  73.5 3.3 %collective-permute-start = (bf16[4,192,128]{2,1,0:T(8,128)(2,1)S(1)}, bf16[4,192,128]{2,1,0:T(8,128)(2,1)S(1)}, u32[]{:S(2)}, u32[]{:S(2)}) collective-permute-start(bf16[4,192,128]{2,1,0:T(8,128)(2,1)S(1)} %get-tuple-element.20), channel_id=1, source_target_pairs={{0,1},{1,0},{2,3},{3,2},{4,5},{5,4},{6,7},{7,6},{8,9},{9,8},{10,11... | collective-permute-start | bytes 589832 | tf_op jit(solution)/shard_map/ppermute | solution.py:201
  76.8 9.8 %collective-permute-start.1 = (bf16[192,128]{1,0:T(8,128)(2,1)S(1)}, bf16[192,128]{1,0:T(8,128)(2,1)S(1)}, u32[]{:S(2)}, u32[]{:S(2)}) collective-permute-start(bf16[192,128]{1,0:T(8,128)(2,1)S(1)} %get-tuple-element.22), channel_id=1, source_target_pairs={{0,8},{8,16},{16,24},{24,0},{1,9},{9,17},{17,25},{25,1},{2,10},{10... | collective-permute-start | bytes 147464 | tf_op jit(solution)/shard_map/ppermute | solution.py:211
  79.9 7.5 %collective-permute-start.2 = (bf16[192,128]{1,0:T(8,128)(2,1)S(1)}, bf16[192,128]{1,0:T(8,128)(2,1)S(1)}, u32[]{:S(2)}, u32[]{:S(2)}) collective-permute-start(bf16[192,128]{1,0:T(8,128)(2,1)S(1)} %get-tuple-element.23), channel_id=1, source_target_pairs={{0,16},{8,24},{16,0},{24,8},{1,17},{9,25},{17,1},{25,9},{2,18},{10... | collective-permute-start | bytes 147464 | tf_op jit(solution)/shard_map/ppermute | solution.py:211
  84.5 6.0 %collective-permute-start.3 = (bf16[192,128]{1,0:T(8,128)(2,1)S(1)}, bf16[192,128]{1,0:T(8,128)(2,1)S(1)}, u32[]{:S(2)}, u32[]{:S(2)}) collective-permute-start(bf16[192,128]{1,0:T(8,128)(2,1)S(1)} %get-tuple-element.24), channel_id=1, source_target_pairs={{0,24},{8,0},{16,8},{24,16},{1,25},{9,1},{17,9},{25,17},{2,26},{10... | collective-permute-start | bytes 147464 | tf_op jit(solution)/shard_map/ppermute | solution.py:211
  91.2 14.2 %all-to-all-start.3 = ((bf16[12,16,128]{2,1,0:T(8,128)(2,1)}), bf16[12,16,128]{2,1,0:T(8,128)(2,1)S(1)}, u32[]{:S(2)}, u32[]{:S(2)}) async-start(bf16[12,16,128]{2,1,0:T(8,128)(2,1)} %bitcast.3), calls=%async_computation.3 | async-start | bytes 98304 | tf_op jit(solution)/shard_map/all_to_all | solution.py:214

commit v5 on v4

--- a/solution.py
+++ b/solution.py
@@ -111,7 +111,8 @@
         t = a[:, :F] - a[:, NORM:NORM + 1] * buf[2][:, :F]
         t = t.reshape(BI // PR, 2, PR // 2, F)
         t = jnp.concatenate([t[:, 0], t[:, 1]], axis=-1).reshape(BI // 2, 128)
-        k = lax.rem(i - x + NX, NX)
+        d = lax.bitwise_xor(jnp.int32(i), jnp.int32(x))
+        k = jnp.where(d == 0, 0, jnp.where(d == 3, 1, d + 1))
         a, b = t[:BI // 4], t[BI // 4:]
         keep_ref[k] = jnp.where(core == 0, a, b)
         swap_ref[k] = jnp.where(core == 0, b, a).astype(bf16)
@@ -147,10 +148,22 @@
         col_ref[d, 128:] = jnp.concatenate([h[:32], h[32:]], axis=1).astype(bf16)
 
 
-def add_kernel(keep_ref, swap_ref, own_ref, *out_refs):
-    own_ref[...] = keep_ref[0] + swap_ref[0].astype(f32)
-    for k in range(1, NX):
-        out_refs[k - 1][...] = (keep_ref[k] + swap_ref[k].astype(f32)).astype(bf16)
+def add_kernel(keep_ref, got_ref, own_ref, out_ref):
+    half = keep_ref.shape[0] // 2
+    s = keep_ref[...] + got_ref[...].astype(f32)
+    own_ref[...] = s[:half]
+    out_ref[...] = s[half:].astype(bf16)
+
+
+def add(keep, got):
+    half = (keep.shape[0] // 2,) + keep.shape[1:]
+    return pl.pallas_call(
+        add_kernel,
+        out_shape=(jax.ShapeDtypeStruct(half, f32), jax.ShapeDtypeStruct(half, bf16)),
+        in_specs=[VM, VM],
+        out_specs=(VM, VM),
+        compiler_params=SMALL,
+    )(keep, got)
 
 
 def finish_rows(row_ref, out_ref):
@@ -199,16 +212,9 @@
     )(rows, cols)
     col_part = lax.all_to_all(col_part, "y", 0, 0, tiled=True)
     swap = lax.ppermute(swap, "core", [(0, 1), (1, 0)])
-    parts = pl.pallas_call(
-        add_kernel,
-        out_shape=(shape((part, 128), f32),) + (shape((part, 128), bf16),) * (NX - 1),
-        in_specs=[VM, VM],
-        out_specs=(VM,) * NX,
-        compiler_params=SMALL,
-    )(keep, swap)
-    row_part = parts[0]
-    for k in range(1, NX):
-        row_part = row_part + lax.ppermute(parts[k], "x", [(i, (i + k) % NX) for i in range(NX)]).astype(f32)
+    keep, out = add(keep, swap)
+    keep, out = add(keep, lax.ppermute(out, "x", [(0, 1), (1, 0), (2, 3), (3, 2)]))
+    row_part = keep + lax.ppermute(out, "x", [(0, 3), (3, 0), (1, 2), (2, 1)]).astype(f32)
     row_part = row_part.astype(bf16).reshape(NZ, PR // 2, 128)
     row_part, col_part = lax.optimization_barrier((row_part, col_part))
     row_part = lax.all_to_all(row_part, Z, 0, 0, tiled=True)

time: 107 us -> 106 us (level)
  starting transfers between devices: 29.9 us -> 27.9 us
    ppermute x3 -> x2, waiting for transfers between devices: 3.83 us -> 6.27 us  [the longest x1 3.39 us: body(): lax.ppermute(out, 'x', [(0, 1), (1, 0), (2, 3), (3, 2)])]
    ppermute x3 -> x2, starting transfers between devices: 9.82 us -> 7.42 us  [the longest x1 4.32 us: body(): lax.ppermute(out, 'x', [(0, 3), (3, 0), (1, 2), (2, 1)]).astype(f32)]
    ppermute x1, waiting for transfers between devices: 1.41 us -> 0.01 us  [body(): swap = lax.ppermute(swap, 'core', [(0, 1), (1, 0)])]
  transfers between devices with their start and end apart: 7 -> 6, of which waited for: 5 -> 4; matrix products, arithmetic and copies ran while one was open for 1% -> 1% of each run, Pallas kernels for 1% -> 1%
where the time goes in v5:
time: 106 us; the launch traced here: 105 us
  blocking collectives  39.9 us (38%)
  starting transfers between devices  27.9 us (26%)
  Pallas kernels  19.6 us (18%)
  waiting for transfers between devices  16.3 us (15%)
    all_to_all x1, blocking collectives, body(): rows = lax.all_to_all(rows, Z, 0, 0, tiled=True)  26.4 us
    pallas_call x1, Pallas kernels, body(): pl.pallas_call(main_kernel, out_shape=(shape((NX, part, 128), f32), shape...  16.4 us
    all_gather x1, blocking collectives, body(): lax.all_gather(rows.reshape(NZ * 24, 128), ('x', 'core'), axis=0, tiled=T...  13.5 us
    all_to_all x1, waiting for transfers between devices, body(): row_part = lax.all_to_all(row_part, Z, 0, 0, tiled=True)  10 us
    all_to_all x1, starting transfers between devices, body(): cols = lax.all_to_all(cols, 'y', 0, 0, tiled=True)  7.55 us
    all_to_all x1, starting transfers between devices, body(): col_part = lax.all_to_all(col_part, 'y', 0, 0, tiled=True)  7.22 us
    ppermute x1, starting transfers between devices, body(): lax.ppermute(out, 'x', [(0, 3), (3, 0), (1, 2), (2, 1)]).astype(f32)  4.32 us
    all_to_all x1, starting transfers between devices, body(): row_part = lax.all_to_all(row_part, Z, 0, 0, tiled=True)  3.48 us
  transfers between devices with their start and end apart: 6, of which 4 were waited for; matrix products, arithmetic and copies ran while one was open for 1% of the time, Pallas kernels for 1%

profile of v5, /device:TPU:8, one launch (start us, length us, event | category | flops | bytes accessed | tf_op | source)
XLA Modules:
  0.0 105.1 jit_solution(6290045171998722624)
XLA Ops:
  0.6 1.7 %shard_map.59 = (bf16[12,24,128]{2,1,0:T(8,128)(2,1)}, bf16[8,240,128]{2,1,0:T(8,128)(2,1)}) custom-call(bf16[32,64]{1,0:T(8,128)(2,1)} %rp_ref.1, bf16[32,32]{1,0:T(8,128)(2,1)} %rs_ref.1, bf16[64,320]{1,0:T(8,128)(2,1)} %bitcast.7, bf16[32,320]{1,0:T(8,128)(2,1)} %bitcast.8), custom_call_target="tpu_custom_call" | custom-call | tf_op jit(solution)/shard_map/pallas_call | solution.py:182
  2.4 26.4 %all_to_all.20 = bf16[12,24,128]{2,1,0:T(8,128)(2,1)S(1)} all-to-all(bf16[12,24,128]{2,1,0:T(8,128)(2,1)} %get-tuple-element.15), channel_id=1, replica_groups=mesh['y'=8,'zh'=3,'x'=4,'zl'=4,'core'=2] {'zh','zl'}, dimensions={0} | all-to-all | bytes 147456 | tf_op jit(solution)/shard_map/all_to_all | solution.py:188
  28.7 7.5 %all-to-all-start.1 = ((bf16[8,240,128]{2,1,0:T(8,128)(2,1)}), bf16[8,240,128]{2,1,0:T(8,128)(2,1)S(1)}, u32[]{:S(2)}, u32[]{:S(2)}) async-start(bf16[8,240,128]{2,1,0:T(8,128)(2,1)} %get-tuple-element.18), calls=%async_computation.1 | async-start | bytes 983040 | tf_op jit(solution)/shard_map/all_to_all | solution.py:190
  36.3 13.5 %all_gather.3.r_ref = bf16[2304,128]{1,0:T(8,128)(2,1)S(1)} all-gather(bf16[288,128]{1,0:T(8,128)(2,1)S(1)} %bitcast.5), channel_id=1, replica_groups=mesh['y'=8,'zh'=3,'x'=4,'zl'=4,'core'=2] {'x','core'}, dimensions={0}, use_global_device_ids=true | all-gather | bytes 663552 | tf_op jit(solution)/shard_map/all_gather | solution.py:191
  49.8 0.1 all-to-all-done.1.p_ref
  49.9 16.4 %shard_map.60 = (f32[4,192,128]{2,1,0:T(8,128)S(1)}, bf16[4,192,128]{2,1,0:T(8,128)(2,1)S(1)}, bf16[8,160,128]{2,1,0:T(8,128)(2,1)}) custom-call(bf16[2304,128]{1,0:T(8,128)(2,1)S(1)} %all_gather.3.r_ref, bf16[8,240,128]{2,1,0:T(8,128)(2,1)S(1)} %all-to-all-done.1.p_ref), custom_call_target="tpu_custom_call" | custom-call | tf_op jit(solution)/shard_map/pallas_call | solution.py:193
  66.3 2.2 %collective-permute-start = (bf16[4,192,128]{2,1,0:T(8,128)(2,1)S(1)}, bf16[4,192,128]{2,1,0:T(8,128)(2,1)S(1)}, u32[]{:S(2)}, u32[]{:S(2)}) collective-permute-start(bf16[4,192,128]{2,1,0:T(8,128)(2,1)S(1)} %get-tuple-element.20), channel_id=1, source_target_pairs={{0,1},{1,0},{2,3},{3,2},{4,5},{5,4},{6,7},{7,6},{8,9},{9,8},{10,11... | collective-permute-start | bytes 589832 | tf_op jit(solution)/shard_map/ppermute | solution.py:214
  68.5 7.2 %all-to-all-start.2 = ((bf16[8,160,128]{2,1,0:T(8,128)(2,1)}), bf16[8,160,128]{2,1,0:T(8,128)(2,1)S(1)}, u32[]{:S(2)}, u32[]{:S(2)}) async-start(bf16[8,160,128]{2,1,0:T(8,128)(2,1)} %get-tuple-element.25), calls=%async_computation.2 | async-start | bytes 655360 | tf_op jit(solution)/shard_map/all_to_all | solution.py:213
  75.7 0.0 collective-permute-done.got_ref
  75.8 3.1 %collective-permute-start.1 = (bf16[2,192,128]{2,1,0:T(8,128)(2,1)S(1)}, bf16[2,192,128]{2,1,0:T(8,128)(2,1)S(1)}, u32[]{:S(2)}, u32[]{:S(2)}) collective-permute-start(bf16[2,192,128]{2,1,0:T(8,128)(2,1)S(1)} %get-tuple-element.22), channel_id=1, source_target_pairs={{0,8},{8,0},{16,24},{24,16},{1,9},{9,1},{17,25},{25,17},{2,10},{10... | collective-permute-start | bytes 294920 | tf_op jit(solution)/shard_map/ppermute | solution.py:216
  78.9 3.4 %collective-permute-done.1.got_ref = bf16[2,192,128]{2,1,0:T(8,128)(2,1)S(1)} collective-permute-done((bf16[2,192,128]{2,1,0:T(8,128)(2,1)S(1)}, bf16[2,192,128]{2,1,0:T(8,128)(2,1)S(1)}, u32[]{:S(2)}, u32[]{:S(2)}) %collective-permute-start.1) | collective-permute-done | bytes 98336 | tf_op jit(solution)/shard_map/ppermute | solution.py:216
  82.3 4.3 %collective-permute-start.2 = (bf16[1,192,128]{2,1,0:T(8,128)(2,1)S(1)}, bf16[1,192,128]{2,1,0:T(8,128)(2,1)S(1)}, u32[]{:S(2)}, u32[]{:S(2)}) collective-permute-start(bf16[1,192,128]{2,1,0:T(8,128)(2,1)S(1)} %get-tuple-element.24), channel_id=1, source_target_pairs={{0,24},{24,0},{8,16},{16,8},{1,25},{25,1},{9,17},{17,9},{2,26},{26... | collective-permute-start | bytes 147464 | tf_op jit(solution)/shard_map/ppermute | solution.py:217
  86.6 2.9 %collective-permute-done.2 = bf16[1,192,128]{2,1,0:T(8,128)(2,1)S(1)} collective-permute-done((bf16[1,192,128]{2,1,0:T(8,128)(2,1)S(1)}, bf16[1,192,128]{2,1,0:T(8,128)(2,1)S(1)}, u32[]{:S(2)}, u32[]{:S(2)}) %collective-permute-start.2) | collective-permute-done | bytes 49184 | tf_op jit(solution)/shard_map/ppermute | solution.py:217
  89.5 0.6 add_convert_fusion
  90.1 0.0 all-to-all-done.2.col_ref
  90.1 3.5 %all-to-all-start.3 = ((bf16[12,16,128]{2,1,0:T(8,128)(2,1)}), bf16[12,16,128]{2,1,0:T(8,128)(2,1)S(1)}, u32[]{:S(2)}, u32[]{:S(2)}) async-start(bf16[12,16,128]{2,1,0:T(8,128)(2,1)} %bitcast.3), calls=%async_computation.3 | async-start | bytes 98304 | tf_op jit(solution)/shard_map/all_to_all | solution.py:220
  93.6 0.7 shard_map.64
  94.3 10.0 %all-to-all-done.3.row_ref = bf16[12,16,128]{2,1,0:T(8,128)(2,1)S(1)} async-done(((bf16[12,16,128]{2,1,0:T(8,128)(2,1)}), bf16[12,16,128]{2,1,0:T(8,128)(2,1)S(1)}, u32[]{:S(2)}, u32[]{:S(2)}) %all-to-all-start.3) | async-done | bytes 49184 | tf_op jit(solution)/shard_map/all_to_all | solution.py:220
  104.4 0.7 shard_map.63
  (2 shorter events, 0.1 us)
Async XLA Ops:
  28.7 21.1 %all-to-all-start.1 = ((bf16[8,240,128]{2,1,0:T(8,128)(2,1)}), bf16[8,240,128]{2,1,0:T(8,128)(2,1)S(1)}, u32[]{:S(2)}, u32[]{:S(2)}) async-start(bf16[8,240,128]{2,1,0:T(8,128)(2,1)} %get-tuple-element.18), calls=%async_computation.1 | async-start | bytes 983040 | tf_op jit(solution)/shard_map/all_to_all | solution.py:190
  66.3 9.4 %collective-permute-start = (bf16[4,192,128]{2,1,0:T(8,128)(2,1)S(1)}, bf16[4,192,128]{2,1,0:T(8,128)(2,1)S(1)}, u32[]{:S(2)}, u32[]{:S(2)}) collective-permute-start(bf16[4,192,128]{2,1,0:T(8,128)(2,1)S(1)} %get-tuple-element.20), channel_id=1, source_target_pairs={{0,1},{1,0},{2,3},{3,2},{4,5},{5,4},{6,7},{7,6},{8,9},{9,8},{10,11... | collective-permute-start | bytes 589832 | tf_op jit(solution)/shard_map/ppermute | solution.py:214
  68.5 21.6 %all-to-all-start.2 = ((bf16[8,160,128]{2,1,0:T(8,128)(2,1)}), bf16[8,160,128]{2,1,0:T(8,128)(2,1)S(1)}, u32[]{:S(2)}, u32[]{:S(2)}) async-start(bf16[8,160,128]{2,1,0:T(8,128)(2,1)} %get-tuple-element.25), calls=%async_computation.2 | async-start | bytes 655360 | tf_op jit(solution)/shard_map/all_to_all | solution.py:213
  75.8 6.5 %collective-permute-start.1 = (bf16[2,192,128]{2,1,0:T(8,128)(2,1)S(1)}, bf16[2,192,128]{2,1,0:T(8,128)(2,1)S(1)}, u32[]{:S(2)}, u32[]{:S(2)}) collective-permute-start(bf16[2,192,128]{2,1,0:T(8,128)(2,1)S(1)} %get-tuple-element.22), channel_id=1, source_target_pairs={{0,8},{8,0},{16,24},{24,16},{1,9},{9,1},{17,25},{25,17},{2,10},{10... | collective-permute-start | bytes 294920 | tf_op jit(solution)/shard_map/ppermute | solution.py:216
  82.3 7.2 %collective-permute-start.2 = (bf16[1,192,128]{2,1,0:T(8,128)(2,1)S(1)}, bf16[1,192,128]{2,1,0:T(8,128)(2,1)S(1)}, u32[]{:S(2)}, u32[]{:S(2)}) collective-permute-start(bf16[1,192,128]{2,1,0:T(8,128)(2,1)S(1)} %get-tuple-element.24), channel_id=1, source_target_pairs={{0,24},{24,0},{8,16},{16,8},{1,25},{25,1},{9,17},{17,9},{2,26},{26... | collective-permute-start | bytes 147464 | tf_op jit(solution)/shard_map/ppermute | solution.py:217
  90.1 14.2 %all-to-all-start.3 = ((bf16[12,16,128]{2,1,0:T(8,128)(2,1)}), bf16[12,16,128]{2,1,0:T(8,128)(2,1)S(1)}, u32[]{:S(2)}, u32[]{:S(2)}) async-start(bf16[12,16,128]{2,1,0:T(8,128)(2,1)} %bitcast.3), calls=%async_computation.3 | async-start | bytes 98304 | tf_op jit(solution)/shard_map/all_to_all | solution.py:220

commit v6 on v5

--- a/solution.py
+++ b/solution.py
@@ -28,7 +28,7 @@
     return a, b, (v - b.astype(f32)).astype(bf16)
 
 
-def pack_kernel(rp_ref, rs_ref, cp_ref, cq_ref, row_ref, col_ref):
+def pack_rows(rp_ref, rs_ref, row_ref):
     r, s = rp_ref[...].astype(f32), rs_ref[...].astype(f32)
     rec = jnp.concatenate(
         [
@@ -39,6 +39,9 @@
     ).astype(bf16)
     for k in range(NZ):
         row_ref[k] = rec
+
+
+def pack_cols(cp_ref, cq_ref, col_ref):
     c = jnp.concatenate([cp_ref[...].astype(f32), cq_ref[...].astype(f32) * (1.0 / Q)], axis=0)
     half = jnp.concatenate([c[:48, 256:], c[48:, 256:]], axis=1)
     piece = jnp.concatenate([c[:, :128], c[:, 128:256], half], axis=0).astype(bf16)
@@ -179,12 +182,18 @@
 
 def body(row_points, row_solves, col_points, col_probes):
     shape = jax.ShapeDtypeStruct
-    rows, cols = pl.pallas_call(
-        pack_kernel,
-        out_shape=(shape((NZ, 24, 128), bf16), shape((NY, 240, 128), bf16)),
-        in_specs=[VM] * 4,
-        out_specs=(VM, VM),
-    )(row_points, row_solves, col_points.T, col_probes.T)
+    rows = pl.pallas_call(
+        pack_rows,
+        out_shape=shape((NZ, 24, 128), bf16),
+        in_specs=[VM] * 2,
+        out_specs=VM,
+    )(row_points, row_solves)
+    cols = pl.pallas_call(
+        pack_cols,
+        out_shape=shape((NY, 240, 128), bf16),
+        in_specs=[VM] * 2,
+        out_specs=VM,
+    )(col_points.T, col_probes.T)
     rows = lax.all_to_all(rows, Z, 0, 0, tiled=True)
     rows, cols = lax.optimization_barrier((rows, cols))
     cols = lax.all_to_all(cols, "y", 0, 0, tiled=True)
@@ -211,8 +220,7 @@
         compiler_params=pltpu.CompilerParams(vmem_limit_bytes=40 * 2**20),
     )(rows, cols)
     col_part = lax.all_to_all(col_part, "y", 0, 0, tiled=True)
-    swap = lax.ppermute(swap, "core", [(0, 1), (1, 0)])
-    keep, out = add(keep, swap)
+    keep, out = add(keep, lax.ppermute(swap, "core", [(0, 1), (1, 0)]))
     keep, out = add(keep, lax.ppermute(out, "x", [(0, 1), (1, 0), (2, 3), (3, 2)]))
     row_part = keep + lax.ppermute(out, "x", [(0, 3), (3, 0), (1, 2), (2, 1)]).astype(f32)
     row_part = row_part.astype(bf16).reshape(NZ, PR // 2, 128)

time: 106 us -> 105 us (level)
  blocking collectives: 39.9 us -> 13.5 us
  starting transfers between devices: 27.9 us -> 43 us
  waiting for transfers between devices: 16.3 us -> 25.9 us
  Pallas kernels: 19.6 us -> 21 us
    all_to_all x1 -> x0, blocking collectives: 26.4 us -> none  [body(): rows = lax.all_to_all(rows, Z, 0, 0, tiled=True)]
    all_to_all x0 -> x1, starting transfers between devices: none -> 15.2 us  [body(): rows = lax.all_to_all(rows, Z, 0, 0, tiled=True)]
    all_to_all x0 -> x1, waiting for transfers between devices: none -> 9.57 us  [body(): rows = lax.all_to_all(rows, Z, 0, 0, tiled=True)]
    pallas_call x1 -> x2, Pallas kernels: 1.73 us -> 3.08 us  [the longest x1 1.66 us: body(): pl.pallas_call(pack_cols, out_shape=shape((NY, 240, 128), bf16), in_specs...]
  transfers between devices with their start and end apart: 6 -> 7, of which waited for: 4 -> 5; matrix products, arithmetic and copies ran while one was open for 1% -> 1% of each run, Pallas kernels for 1% -> 2%
where the time goes in v6:
time: 105 us
  starting transfers between devices  43 us (41%)
  waiting for transfers between devices  25.9 us (25%)
  Pallas kernels  21 us (20%)
  blocking collectives  13.5 us (13%)
    pallas_call x1, Pallas kernels, body(): pl.pallas_call(main_kernel, out_shape=(shape((NX, part, 128), f32), shape...  16.5 us
    all_to_all x1, starting transfers between devices, body(): rows = lax.all_to_all(rows, Z, 0, 0, tiled=True)  15.2 us
    all_gather x1, blocking collectives, body(): lax.all_gather(rows.reshape(NZ * 24, 128), ('x', 'core'), axis=0, tiled=T...  13.5 us
    all_to_all x1, waiting for transfers between devices, body(): row_part = lax.all_to_all(row_part, Z, 0, 0, tiled=True)  10 us
    all_to_all x1, waiting for transfers between devices, body(): rows = lax.all_to_all(rows, Z, 0, 0, tiled=True)  9.57 us
    all_to_all x1, starting transfers between devices, body(): cols = lax.all_to_all(cols, 'y', 0, 0, tiled=True)  7.55 us
    all_to_all x1, starting transfers between devices, body(): col_part = lax.all_to_all(col_part, 'y', 0, 0, tiled=True)  7.22 us
    ppermute x1, starting transfers between devices, body(): lax.ppermute(out, 'x', [(0, 3), (3, 0), (1, 2), (2, 1)]).astype(f32)  4.31 us
  transfers between devices with their start and end apart: 7, of which 5 were waited for; matrix products, arithmetic and copies ran while one was open for 1% of the time, Pallas kernels for 2%

profile of v6, /device:TPU:8, one launch (start us, length us, event | category | flops | bytes accessed | tf_op | source)
XLA Modules:
  0.0 104.8 jit_solution(3254898212577297745)
XLA Ops:
  0.6 1.4 %shard_map.59 = bf16[12,24,128]{2,1,0:T(8,128)(2,1)} custom-call(bf16[32,64]{1,0:T(8,128)(2,1)} %rp_ref.1, bf16[32,32]{1,0:T(8,128)(2,1)} %rs_ref.1), custom_call_target="tpu_custom_call" | custom-call | tf_op jit(solution)/shard_map/pallas_call | solution.py:185
  2.1 15.2 %all-to-all-start = ((bf16[12,24,128]{2,1,0:T(8,128)(2,1)}), bf16[12,24,128]{2,1,0:T(8,128)(2,1)S(1)}, u32[]{:S(2)}, u32[]{:S(2)}) async-start(bf16[12,24,128]{2,1,0:T(8,128)(2,1)} %shard_map.59), calls=%async_computation | async-start | bytes 147456 | tf_op jit(solution)/shard_map/all_to_all | solution.py:197
  17.2 1.7 %shard_map.60 = bf16[8,240,128]{2,1,0:T(8,128)(2,1)} custom-call(bf16[64,320]{1,0:T(8,128)(2,1)} %bitcast.7, bf16[32,320]{1,0:T(8,128)(2,1)} %bitcast.8), custom_call_target="tpu_custom_call" | custom-call | tf_op jit(solution)/shard_map/pallas_call | solution.py:191
  18.9 9.6 %all-to-all-done = bf16[12,24,128]{2,1,0:T(8,128)(2,1)S(1)} async-done(((bf16[12,24,128]{2,1,0:T(8,128)(2,1)}), bf16[12,24,128]{2,1,0:T(8,128)(2,1)S(1)}, u32[]{:S(2)}, u32[]{:S(2)}) %all-to-all-start) | async-done | bytes 73760 | tf_op jit(solution)/shard_map/all_to_all | solution.py:197
  28.4 7.5 %all-to-all-start.1 = ((bf16[8,240,128]{2,1,0:T(8,128)(2,1)}), bf16[8,240,128]{2,1,0:T(8,128)(2,1)S(1)}, u32[]{:S(2)}, u32[]{:S(2)}) async-start(bf16[8,240,128]{2,1,0:T(8,128)(2,1)} %shard_map.60), calls=%async_computation.1 | async-start | bytes 983040 | tf_op jit(solution)/shard_map/all_to_all | solution.py:199
  36.0 13.5 %all_gather.3.r_ref = bf16[2304,128]{1,0:T(8,128)(2,1)S(1)} all-gather(bf16[288,128]{1,0:T(8,128)(2,1)S(1)} %bitcast.5), channel_id=1, replica_groups=mesh['y'=8,'zh'=3,'x'=4,'zl'=4,'core'=2] {'x','core'}, dimensions={0}, use_global_device_ids=true | all-gather | bytes 663552 | tf_op jit(solution)/shard_map/all_gather | solution.py:200
  49.5 0.1 all-to-all-done.1.p_ref
  49.6 16.5 %shard_map.61 = (f32[4,192,128]{2,1,0:T(8,128)S(1)}, bf16[4,192,128]{2,1,0:T(8,128)(2,1)S(1)}, bf16[8,160,128]{2,1,0:T(8,128)(2,1)}) custom-call(bf16[2304,128]{1,0:T(8,128)(2,1)S(1)} %all_gather.3.r_ref, bf16[8,240,128]{2,1,0:T(8,128)(2,1)S(1)} %all-to-all-done.1.p_ref), custom_call_target="tpu_custom_call" | custom-call | tf_op jit(solution)/shard_map/pallas_call | solution.py:202
  66.0 2.2 %collective-permute-start = (bf16[4,192,128]{2,1,0:T(8,128)(2,1)S(1)}, bf16[4,192,128]{2,1,0:T(8,128)(2,1)S(1)}, u32[]{:S(2)}, u32[]{:S(2)}) collective-permute-start(bf16[4,192,128]{2,1,0:T(8,128)(2,1)S(1)} %get-tuple-element.16), channel_id=1, source_target_pairs={{0,1},{1,0},{2,3},{3,2},{4,5},{5,4},{6,7},{7,6},{8,9},{9,8},{10,11... | collective-permute-start | bytes 589832 | tf_op jit(solution)/shard_map/ppermute | solution.py:223
  68.2 7.2 %all-to-all-start.2 = ((bf16[8,160,128]{2,1,0:T(8,128)(2,1)}), bf16[8,160,128]{2,1,0:T(8,128)(2,1)S(1)}, u32[]{:S(2)}, u32[]{:S(2)}) async-start(bf16[8,160,128]{2,1,0:T(8,128)(2,1)} %get-tuple-element.21), calls=%async_computation.2 | async-start | bytes 655360 | tf_op jit(solution)/shard_map/all_to_all | solution.py:222
  75.4 0.0 collective-permute-done.got_ref
  75.5 3.1 %collective-permute-start.1 = (bf16[2,192,128]{2,1,0:T(8,128)(2,1)S(1)}, bf16[2,192,128]{2,1,0:T(8,128)(2,1)S(1)}, u32[]{:S(2)}, u32[]{:S(2)}) collective-permute-start(bf16[2,192,128]{2,1,0:T(8,128)(2,1)S(1)} %get-tuple-element.18), channel_id=1, source_target_pairs={{0,8},{8,0},{16,24},{24,16},{1,9},{9,1},{17,25},{25,17},{2,10},{10... | collective-permute-start | bytes 294920 | tf_op jit(solution)/shard_map/ppermute | solution.py:224
  78.6 3.4 %collective-permute-done.1.got_ref = bf16[2,192,128]{2,1,0:T(8,128)(2,1)S(1)} collective-permute-done((bf16[2,192,128]{2,1,0:T(8,128)(2,1)S(1)}, bf16[2,192,128]{2,1,0:T(8,128)(2,1)S(1)}, u32[]{:S(2)}, u32[]{:S(2)}) %collective-permute-start.1) | collective-permute-done | bytes 98336 | tf_op jit(solution)/shard_map/ppermute | solution.py:224
  82.0 4.3 %collective-permute-start.2 = (bf16[1,192,128]{2,1,0:T(8,128)(2,1)S(1)}, bf16[1,192,128]{2,1,0:T(8,128)(2,1)S(1)}, u32[]{:S(2)}, u32[]{:S(2)}) collective-permute-start(bf16[1,192,128]{2,1,0:T(8,128)(2,1)S(1)} %get-tuple-element.20), channel_id=1, source_target_pairs={{0,24},{24,0},{8,16},{16,8},{1,25},{25,1},{9,17},{17,9},{2,26},{26... | collective-permute-start | bytes 147464 | tf_op jit(solution)/shard_map/ppermute | solution.py:225
  86.3 2.9 %collective-permute-done.2 = bf16[1,192,128]{2,1,0:T(8,128)(2,1)S(1)} collective-permute-done((bf16[1,192,128]{2,1,0:T(8,128)(2,1)S(1)}, bf16[1,192,128]{2,1,0:T(8,128)(2,1)S(1)}, u32[]{:S(2)}, u32[]{:S(2)}) %collective-permute-start.2) | collective-permute-done | bytes 49184 | tf_op jit(solution)/shard_map/ppermute | solution.py:225
  89.2 0.6 add_convert_fusion
  89.8 0.0 all-to-all-done.2.col_ref
  89.8 3.5 %all-to-all-start.3 = ((bf16[12,16,128]{2,1,0:T(8,128)(2,1)}), bf16[12,16,128]{2,1,0:T(8,128)(2,1)S(1)}, u32[]{:S(2)}, u32[]{:S(2)}) async-start(bf16[12,16,128]{2,1,0:T(8,128)(2,1)} %bitcast.3), calls=%async_computation.3 | async-start | bytes 98304 | tf_op jit(solution)/shard_map/all_to_all | solution.py:228
  93.3 0.7 shard_map.65
  94.1 10.0 %all-to-all-done.3.row_ref = bf16[12,16,128]{2,1,0:T(8,128)(2,1)S(1)} async-done(((bf16[12,16,128]{2,1,0:T(8,128)(2,1)}), bf16[12,16,128]{2,1,0:T(8,128)(2,1)S(1)}, u32[]{:S(2)}, u32[]{:S(2)}) %all-to-all-start.3) | async-done | bytes 49184 | tf_op jit(solution)/shard_map/all_to_all | solution.py:228
  104.1 0.7 shard_map.64
  (2 shorter events, 0.1 us)
Async XLA Ops:
  2.1 26.4 %all-to-all-start = ((bf16[12,24,128]{2,1,0:T(8,128)(2,1)}), bf16[12,24,128]{2,1,0:T(8,128)(2,1)S(1)}, u32[]{:S(2)}, u32[]{:S(2)}) async-start(bf16[12,24,128]{2,1,0:T(8,128)(2,1)} %shard_map.59), calls=%async_computation | async-start | bytes 147456 | tf_op jit(solution)/shard_map/all_to_all | solution.py:197
  28.4 21.1 %all-to-all-start.1 = ((bf16[8,240,128]{2,1,0:T(8,128)(2,1)}), bf16[8,240,128]{2,1,0:T(8,128)(2,1)S(1)}, u32[]{:S(2)}, u32[]{:S(2)}) async-start(bf16[8,240,128]{2,1,0:T(8,128)(2,1)} %shard_map.60), calls=%async_computation.1 | async-start | bytes 983040 | tf_op jit(solution)/shard_map/all_to_all | solution.py:199
  66.0 9.4 %collective-permute-start = (bf16[4,192,128]{2,1,0:T(8,128)(2,1)S(1)}, bf16[4,192,128]{2,1,0:T(8,128)(2,1)S(1)}, u32[]{:S(2)}, u32[]{:S(2)}) collective-permute-start(bf16[4,192,128]{2,1,0:T(8,128)(2,1)S(1)} %get-tuple-element.16), channel_id=1, source_target_pairs={{0,1},{1,0},{2,3},{3,2},{4,5},{5,4},{6,7},{7,6},{8,9},{9,8},{10,11... | collective-permute-start | bytes 589832 | tf_op jit(solution)/shard_map/ppermute | solution.py:223
  68.2 21.6 %all-to-all-start.2 = ((bf16[8,160,128]{2,1,0:T(8,128)(2,1)}), bf16[8,160,128]{2,1,0:T(8,128)(2,1)S(1)}, u32[]{:S(2)}, u32[]{:S(2)}) async-start(bf16[8,160,128]{2,1,0:T(8,128)(2,1)} %get-tuple-element.21), calls=%async_computation.2 | async-start | bytes 655360 | tf_op jit(solution)/shard_map/all_to_all | solution.py:222
  75.5 6.5 %collective-permute-start.1 = (bf16[2,192,128]{2,1,0:T(8,128)(2,1)S(1)}, bf16[2,192,128]{2,1,0:T(8,128)(2,1)S(1)}, u32[]{:S(2)}, u32[]{:S(2)}) collective-permute-start(bf16[2,192,128]{2,1,0:T(8,128)(2,1)S(1)} %get-tuple-element.18), channel_id=1, source_target_pairs={{0,8},{8,0},{16,24},{24,16},{1,9},{9,1},{17,25},{25,17},{2,10},{10... | collective-permute-start | bytes 294920 | tf_op jit(solution)/shard_map/ppermute | solution.py:224
  82.0 7.2 %collective-permute-start.2 = (bf16[1,192,128]{2,1,0:T(8,128)(2,1)S(1)}, bf16[1,192,128]{2,1,0:T(8,128)(2,1)S(1)}, u32[]{:S(2)}, u32[]{:S(2)}) collective-permute-start(bf16[1,192,128]{2,1,0:T(8,128)(2,1)S(1)} %get-tuple-element.20), channel_id=1, source_target_pairs={{0,24},{24,0},{8,16},{16,8},{1,25},{25,1},{9,17},{17,9},{2,26},{26... | collective-permute-start | bytes 147464 | tf_op jit(solution)/shard_map/ppermute | solution.py:225
  89.8 14.2 %all-to-all-start.3 = ((bf16[12,16,128]{2,1,0:T(8,128)(2,1)}), bf16[12,16,128]{2,1,0:T(8,128)(2,1)S(1)}, u32[]{:S(2)}, u32[]{:S(2)}) async-start(bf16[12,16,128]{2,1,0:T(8,128)(2,1)} %bitcast.3), calls=%async_computation.3 | async-start | bytes 98304 | tf_op jit(solution)/shard_map/all_to_all | solution.py:228

commit v7 on v6

--- a/solution.py
+++ b/solution.py
@@ -7,9 +7,10 @@
 
 f32, bf16 = jnp.float32, jnp.bfloat16
 
-NAMES = ("y", "zh", "x", "zl", "core")
-SIZES = (8, 3, 4, 4, 2)
-Z = ("zh", "zl")
+NAMES = ("y", "zh", "xa", "xb", "zl", "core")
+SIZES = (8, 3, 2, 2, 4, 2)
+XZ = ("xa", "zh", "zl")
+ORDER = [[0, 2, 4, 6, 1, 3, 5, 7]]
 NX, NY, NZ, NC = 4, 8, 12, 2
 PR, PC, F, Q = 32, 320, 64, 32
 R, C = PR * NX * NZ * NC, PC * NY
@@ -37,7 +38,7 @@
         ],
         axis=0,
     ).astype(bf16)
-    for k in range(NZ):
+    for k in range(2 * NZ):
         row_ref[k] = rec
 
 
@@ -88,12 +89,12 @@
     return r, jnp.where(lane < F, r, jnp.where(lane < NORM, s, ext)).astype(bf16)
 
 
-def main_kernel(r_ref, p_ref, keep_ref, swap_ref, col_ref, acc_c, ct, ce, cm, cn, w0, w1, rt0, rt1, rf0, rf1):
+def main_kernel(r_ref, p_ref, keep_ref, swap_ref, col_ref, acc_c, ct, ce, cm, cn, w0, w1, rt0, rt1, rf0, rf1, part):
     column_records(p_ref, ct, ce, cm, cn)
     acc_c[...] = jnp.zeros_like(acc_c)
     bufs = ((w0, rt0, rf0), (w1, rt1, rf1))
     n = R // BI
-    x, core = lax.axis_index("x"), lax.axis_index("core")
+    xb, core = lax.axis_index("xb"), lax.axis_index("core")
 
     def front(i, buf):
         r, rb = row_records(r_ref[pl.ds(pl.multiple_of(i * PK, PK), PK), :])
@@ -114,11 +115,9 @@
         t = a[:, :F] - a[:, NORM:NORM + 1] * buf[2][:, :F]
         t = t.reshape(BI // PR, 2, PR // 2, F)
         t = jnp.concatenate([t[:, 0], t[:, 1]], axis=-1).reshape(BI // 2, 128)
-        d = lax.bitwise_xor(jnp.int32(i), jnp.int32(x))
-        k = jnp.where(d == 0, 0, jnp.where(d == 3, 1, d + 1))
-        a, b = t[:BI // 4], t[BI // 4:]
-        keep_ref[k] = jnp.where(core == 0, a, b)
-        swap_ref[k] = jnp.where(core == 0, b, a).astype(bf16)
+        at = 4 * jnp.int32(i % 2 != core) + 2 * jnp.int32(i // 2 != xb)
+        for h in range(2):
+            part[at + h] = t[h * (BI // 4):(h + 1) * (BI // 4)]
 
     def both(i, new, old):
         rb = front(i, new)
@@ -142,6 +141,8 @@
         columns(j, bufs[1])
     rows(n - 1, bufs[1])
 
+    keep_ref[...] = part[:4]
+    swap_ref[...] = part[4:].astype(bf16)
     u = acc_c[:F, :] - acc_c[ONES:ONES + 1, :] * ct[:F, :].astype(f32)
 
     for d in range(NY):
@@ -184,7 +185,7 @@
     shape = jax.ShapeDtypeStruct
     rows = pl.pallas_call(
         pack_rows,
-        out_shape=shape((NZ, 24, 128), bf16),
+        out_shape=shape((2 * NZ, 24, 128), bf16),
         in_specs=[VM] * 2,
         out_specs=VM,
     )(row_points, row_solves)
@@ -194,10 +195,10 @@
         in_specs=[VM] * 2,
         out_specs=VM,
     )(col_points.T, col_probes.T)
-    rows = lax.all_to_all(rows, Z, 0, 0, tiled=True)
+    rows = lax.all_to_all(rows, XZ, 0, 0, tiled=True)
     rows, cols = lax.optimization_barrier((rows, cols))
-    cols = lax.all_to_all(cols, "y", 0, 0, tiled=True)
-    rows = lax.all_gather(rows.reshape(NZ * 24, 128), ("x", "core"), axis=0, tiled=True)
+    cols = lax.all_to_all(cols, "y", 0, 0, tiled=True, axis_index_groups=ORDER)
+    rows = lax.all_gather(rows.reshape(2 * NZ * 24, 128), ("xb", "core"), axis=0, tiled=True)
     part = R // (2 * NX * NC)
     keep, swap, col_part = pl.pallas_call(
         main_kernel,
@@ -216,16 +217,16 @@
             pltpu.VMEM((128, BI), bf16),
             pltpu.VMEM((BI, 128), f32),
             pltpu.VMEM((BI, 128), f32),
+            pltpu.VMEM((2 * NX, part, 128), f32),
         ],
         compiler_params=pltpu.CompilerParams(vmem_limit_bytes=40 * 2**20),
     )(rows, cols)
-    col_part = lax.all_to_all(col_part, "y", 0, 0, tiled=True)
+    col_part = lax.all_to_all(col_part, "y", 0, 0, tiled=True, axis_index_groups=ORDER)
     keep, out = add(keep, lax.ppermute(swap, "core", [(0, 1), (1, 0)]))
-    keep, out = add(keep, lax.ppermute(out, "x", [(0, 1), (1, 0), (2, 3), (3, 2)]))
-    row_part = keep + lax.ppermute(out, "x", [(0, 3), (3, 0), (1, 2), (2, 1)]).astype(f32)
-    row_part = row_part.astype(bf16).reshape(NZ, PR // 2, 128)
+    row_part = keep + lax.ppermute(out, "xb", [(0, 1), (1, 0)]).astype(f32)
+    row_part = row_part.astype(bf16).reshape(2 * NZ, PR // 2, 128)
     row_part, col_part = lax.optimization_barrier((row_part, col_part))
-    row_part = lax.all_to_all(row_part, Z, 0, 0, tiled=True)
+    row_part = lax.all_to_all(row_part, XZ, 0, 0, tiled=True)
     row_grad = pl.pallas_call(
         finish_rows,
         out_shape=shape((PR, F), f32),
@@ -245,8 +246,8 @@
 
 def solution(mesh):
     rings = Mesh(mesh.devices.reshape(SIZES), NAMES)
-    row = P(("y", "zh", "x", "zl", "core"), None)
-    col = P(("x", "zl", "core", "y", "zh"), None)
+    row = P(("y", "zh", "xa", "xb", "zl", "core"), None)
+    col = P(("xa", "xb", "zl", "core", "y", "zh"), None)
     return jax.shard_map(
         body,
         mesh=rings,

time: 105 us -> 105 us (level)
  waiting for transfers between devices: 25.9 us -> 34.8 us
  blocking collectives: 13.5 us -> 6.68 us
  starting transfers between devices: 43 us -> 40.3 us
    all_to_all x4, waiting for transfers between devices: 19.6 us -> 29.2 us  [the longest x1 12.7 us: body(): rows = lax.all_to_all(rows, XZ, 0, 0, tiled=True)]
    all_gather x1, blocking collectives: 13.5 us -> 6.68 us  [body(): lax.all_gather(rows.reshape(2 * NZ * 24, 128), ('xb', 'core'), axis=0, ti...]
    ppermute x2 -> x1, starting transfers between devices: 7.42 us -> 2.52 us  [body(): row_part = keep + lax.ppermute(out, 'xb', [(0, 1), (1, 0)]).astype(f32)]
    all_to_all x4, starting transfers between devices: 33.4 us -> 35.9 us  [the longest x1 17.8 us: body(): rows = lax.all_to_all(rows, XZ, 0, 0, tiled=True)]
    ppermute x2 -> x1, waiting for transfers between devices: 6.27 us -> 4.21 us  [body(): row_part = keep + lax.ppermute(out, 'xb', [(0, 1), (1, 0)]).astype(f32)]
    ppermute x1, waiting for transfers between devices: 0.01 us -> 1.41 us  [body(): keep, out = add(keep, lax.ppermute(swap, 'core', [(0, 1), (1, 0)]))]
  transfers between devices with their start and end apart: 7 -> 6, of which waited for: 5 -> 5; matrix products, arithmetic and copies ran while one was open for 1% -> 1% of each run, Pallas kernels for 2% -> 2%
where the time goes in v7:
time: 105 us; the launch traced here: 104 us
  starting transfers between devices  40.3 us (38%)
  waiting for transfers between devices  34.8 us (33%)
  Pallas kernels  21.1 us (20%)
  blocking collectives  6.68 us (6%)
    all_to_all x1, starting transfers between devices, body(): rows = lax.all_to_all(rows, XZ, 0, 0, tiled=True)  17.8 us
    pallas_call x1, Pallas kernels, body(): pl.pallas_call(main_kernel, out_shape=(shape((NX, part, 128), f32), shape...  16.5 us
    all_to_all x1, waiting for transfers between devices, body(): rows = lax.all_to_all(rows, XZ, 0, 0, tiled=True)  12.7 us
    all_to_all x1, waiting for transfers between devices, body(): row_part = lax.all_to_all(row_part, XZ, 0, 0, tiled=True)  11.7 us
    all_to_all x1, starting transfers between devices, body(): cols = lax.all_to_all(cols, 'y', 0, 0, tiled=True, axis_index_groups=ORDER)  7.55 us
    all_gather x1, blocking collectives, body(): lax.all_gather(rows.reshape(2 * NZ * 24, 128), ('xb', 'core'), axis=0, ti...  6.68 us
    all_to_all x1, starting transfers between devices, body(): row_part = lax.all_to_all(row_part, XZ, 0, 0, tiled=True)  5.86 us
    all_to_all x1, waiting for transfers between devices, body(): cols = lax.all_to_all(cols, 'y', 0, 0, tiled=True, axis_index_groups=ORDER)  4.78 us
  transfers between devices with their start and end apart: 6, of which 5 were waited for; matrix products, arithmetic and copies ran while one was open for 1% of the time, Pallas kernels for 2%

profile of v7, /device:TPU:8, one launch (start us, length us, event | category | flops | bytes accessed | tf_op | source)
XLA Modules:
  0.0 104.2 jit_solution(3389024820872492911)
XLA Ops:
  0.6 1.4 %shard_map.59 = bf16[24,24,128]{2,1,0:T(8,128)(2,1)} custom-call(bf16[32,64]{1,0:T(8,128)(2,1)} %rp_ref.1, bf16[32,32]{1,0:T(8,128)(2,1)} %rs_ref.1), custom_call_target="tpu_custom_call" | custom-call | tf_op jit(solution)/shard_map/pallas_call | solution.py:186
  2.1 17.8 %all-to-all-start = ((bf16[24,24,128]{2,1,0:T(8,128)(2,1)}), bf16[24,24,128]{2,1,0:T(8,128)(2,1)S(1)}, u32[]{:S(2)}, u32[]{:S(2)}) async-start(bf16[24,24,128]{2,1,0:T(8,128)(2,1)} %shard_map.59), calls=%async_computation | async-start | bytes 294912 | tf_op jit(solution)/shard_map/all_to_all | solution.py:198
  19.9 1.7 %shard_map.60 = bf16[8,240,128]{2,1,0:T(8,128)(2,1)} custom-call(bf16[64,320]{1,0:T(8,128)(2,1)} %bitcast.7, bf16[32,320]{1,0:T(8,128)(2,1)} %bitcast.8), custom_call_target="tpu_custom_call" | custom-call | tf_op jit(solution)/shard_map/pallas_call | solution.py:192
  21.6 12.7 %all-to-all-done = bf16[24,24,128]{2,1,0:T(8,128)(2,1)S(1)} async-done(((bf16[24,24,128]{2,1,0:T(8,128)(2,1)}), bf16[24,24,128]{2,1,0:T(8,128)(2,1)S(1)}, u32[]{:S(2)}, u32[]{:S(2)}) %all-to-all-start) | async-done | bytes 147488 | tf_op jit(solution)/shard_map/all_to_all | solution.py:198
  34.3 7.5 %all-to-all-start.1 = ((bf16[8,240,128]{2,1,0:T(8,128)(2,1)}), bf16[8,240,128]{2,1,0:T(8,128)(2,1)S(1)}, u32[]{:S(2)}, u32[]{:S(2)}) async-start(bf16[8,240,128]{2,1,0:T(8,128)(2,1)} %shard_map.60), calls=%async_computation.1 | async-start | bytes 983040 | tf_op jit(solution)/shard_map/all_to_all | solution.py:200
  41.8 6.7 %all_gather.3.r_ref = bf16[2304,128]{1,0:T(8,128)(2,1)S(1)} all-gather(bf16[576,128]{1,0:T(8,128)(2,1)S(1)} %bitcast.5), channel_id=1, replica_groups=mesh['y'=8,'zh'=3,'xa'=2,'xb'=2,'zl'=4,'core'=2] {'xb','core'}, dimensions={0}, use_global_device_ids=true | all-gather | bytes 737280 | tf_op jit(solution)/shard_map/all_gather | solution.py:201
  48.5 4.8 %all-to-all-done.1.p_ref = bf16[8,240,128]{2,1,0:T(8,128)(2,1)S(1)} async-done(((bf16[8,240,128]{2,1,0:T(8,128)(2,1)}), bf16[8,240,128]{2,1,0:T(8,128)(2,1)S(1)}, u32[]{:S(2)}, u32[]{:S(2)}) %all-to-all-start.1) | async-done | bytes 491552 | tf_op jit(solution)/shard_map/all_to_all | solution.py:200
  53.3 16.5 %shard_map.61 = (f32[4,192,128]{2,1,0:T(8,128)S(1)}, bf16[4,192,128]{2,1,0:T(8,128)(2,1)S(1)}, bf16[8,160,128]{2,1,0:T(8,128)(2,1)}) custom-call(bf16[2304,128]{1,0:T(8,128)(2,1)S(1)} %all_gather.3.r_ref, bf16[8,240,128]{2,1,0:T(8,128)(2,1)S(1)} %all-to-all-done.1.p_ref), custom_call_target="tpu_custom_call" | custom-call | tf_op jit(solution)/shard_map/pallas_call | solution.py:203
  69.8 4.7 %all-to-all-start.2 = ((bf16[8,160,128]{2,1,0:T(8,128)(2,1)}), bf16[8,160,128]{2,1,0:T(8,128)(2,1)S(1)}, u32[]{:S(2)}, u32[]{:S(2)}) async-start(bf16[8,160,128]{2,1,0:T(8,128)(2,1)} %get-tuple-element.17), calls=%async_computation.2 | async-start | bytes 655360 | tf_op jit(solution)/shard_map/all_to_all | solution.py:224
  74.4 1.9 %collective-permute-start = (bf16[4,192,128]{2,1,0:T(8,128)(2,1)S(1)}, bf16[4,192,128]{2,1,0:T(8,128)(2,1)S(1)}, u32[]{:S(2)}, u32[]{:S(2)}) collective-permute-start(bf16[4,192,128]{2,1,0:T(8,128)(2,1)S(1)} %get-tuple-element.14), channel_id=1, source_target_pairs={{0,1},{1,0},{2,3},{3,2},{4,5},{5,4},{6,7},{7,6},{8,9},{9,8},{10,11... | collective-permute-start | bytes 589832 | tf_op jit(solution)/shard_map/ppermute | solution.py:225
  76.3 1.4 %collective-permute-done.got_ref = bf16[4,192,128]{2,1,0:T(8,128)(2,1)S(1)} collective-permute-done((bf16[4,192,128]{2,1,0:T(8,128)(2,1)S(1)}, bf16[4,192,128]{2,1,0:T(8,128)(2,1)S(1)}, u32[]{:S(2)}, u32[]{:S(2)}) %collective-permute-start) | collective-permute-done | bytes 196640 | tf_op jit(solution)/shard_map/ppermute | solution.py:225
  77.8 2.5 %collective-permute-start.1 = (bf16[2,192,128]{2,1,0:T(8,128)(2,1)S(1)}, bf16[2,192,128]{2,1,0:T(8,128)(2,1)S(1)}, u32[]{:S(2)}, u32[]{:S(2)}) collective-permute-start(bf16[2,192,128]{2,1,0:T(8,128)(2,1)S(1)} %get-tuple-element.16), channel_id=1, source_target_pairs={{0,8},{8,0},{1,9},{9,1},{2,10},{10,2},{3,11},{11,3},{4,12},{12,4},... | collective-permute-start | bytes 294920 | tf_op jit(solution)/shard_map/ppermute | solution.py:226
  80.3 4.2 %collective-permute-done.1 = bf16[2,192,128]{2,1,0:T(8,128)(2,1)S(1)} collective-permute-done((bf16[2,192,128]{2,1,0:T(8,128)(2,1)S(1)}, bf16[2,192,128]{2,1,0:T(8,128)(2,1)S(1)}, u32[]{:S(2)}, u32[]{:S(2)}) %collective-permute-start.1) | collective-permute-done | bytes 98336 | tf_op jit(solution)/shard_map/ppermute | solution.py:226
  84.5 0.7 add_convert_fusion
  85.2 0.0 all-to-all-done.2.col_ref
  85.2 5.9 %all-to-all-start.3 = ((bf16[24,16,128]{2,1,0:T(8,128)(2,1)}), bf16[24,16,128]{2,1,0:T(8,128)(2,1)S(1)}, u32[]{:S(2)}, u32[]{:S(2)}) async-start(bf16[24,16,128]{2,1,0:T(8,128)(2,1)} %bitcast.3), calls=%async_computation.3 | async-start | bytes 196608 | tf_op jit(solution)/shard_map/all_to_all | solution.py:229
  91.1 0.7 shard_map.64
  91.8 11.7 %all-to-all-done.3.row_ref = bf16[24,16,128]{2,1,0:T(8,128)(2,1)S(1)} async-done(((bf16[24,16,128]{2,1,0:T(8,128)(2,1)}), bf16[24,16,128]{2,1,0:T(8,128)(2,1)S(1)}, u32[]{:S(2)}, u32[]{:S(2)}) %all-to-all-start.3) | async-done | bytes 98336 | tf_op jit(solution)/shard_map/all_to_all | solution.py:229
  103.5 0.7 shard_map.63
  (1 shorter events, 0.0 us)
Async XLA Ops:
  2.1 32.2 %all-to-all-start = ((bf16[24,24,128]{2,1,0:T(8,128)(2,1)}), bf16[24,24,128]{2,1,0:T(8,128)(2,1)S(1)}, u32[]{:S(2)}, u32[]{:S(2)}) async-start(bf16[24,24,128]{2,1,0:T(8,128)(2,1)} %shard_map.59), calls=%async_computation | async-start | bytes 294912 | tf_op jit(solution)/shard_map/all_to_all | solution.py:198
  34.3 19.0 %all-to-all-start.1 = ((bf16[8,240,128]{2,1,0:T(8,128)(2,1)}), bf16[8,240,128]{2,1,0:T(8,128)(2,1)S(1)}, u32[]{:S(2)}, u32[]{:S(2)}) async-start(bf16[8,240,128]{2,1,0:T(8,128)(2,1)} %shard_map.60), calls=%async_computation.1 | async-start | bytes 983040 | tf_op jit(solution)/shard_map/all_to_all | solution.py:200
  69.8 15.4 %all-to-all-start.2 = ((bf16[8,160,128]{2,1,0:T(8,128)(2,1)}), bf16[8,160,128]{2,1,0:T(8,128)(2,1)S(1)}, u32[]{:S(2)}, u32[]{:S(2)}) async-start(bf16[8,160,128]{2,1,0:T(8,128)(2,1)} %get-tuple-element.17), calls=%async_computation.2 | async-start | bytes 655360 | tf_op jit(solution)/shard_map/all_to_all | solution.py:224
  74.4 3.3 %collective-permute-start = (bf16[4,192,128]{2,1,0:T(8,128)(2,1)S(1)}, bf16[4,192,128]{2,1,0:T(8,128)(2,1)S(1)}, u32[]{:S(2)}, u32[]{:S(2)}) collective-permute-start(bf16[4,192,128]{2,1,0:T(8,128)(2,1)S(1)} %get-tuple-element.14), channel_id=1, source_target_pairs={{0,1},{1,0},{2,3},{3,2},{4,5},{5,4},{6,7},{7,6},{8,9},{9,8},{10,11... | collective-permute-start | bytes 589832 | tf_op jit(solution)/shard_map/ppermute | solution.py:225
  77.8 6.7 %collective-permute-start.1 = (bf16[2,192,128]{2,1,0:T(8,128)(2,1)S(1)}, bf16[2,192,128]{2,1,0:T(8,128)(2,1)S(1)}, u32[]{:S(2)}, u32[]{:S(2)}) collective-permute-start(bf16[2,192,128]{2,1,0:T(8,128)(2,1)S(1)} %get-tuple-element.16), channel_id=1, source_target_pairs={{0,8},{8,0},{1,9},{9,1},{2,10},{10,2},{3,11},{11,3},{4,12},{12,4},... | collective-permute-start | bytes 294920 | tf_op jit(solution)/shard_map/ppermute | solution.py:226
  85.2 18.3 %all-to-all-start.3 = ((bf16[24,16,128]{2,1,0:T(8,128)(2,1)}), bf16[24,16,128]{2,1,0:T(8,128)(2,1)S(1)}, u32[]{:S(2)}, u32[]{:S(2)}) async-start(bf16[24,16,128]{2,1,0:T(8,128)(2,1)} %bitcast.3), calls=%async_computation.3 | async-start | bytes 196608 | tf_op jit(solution)/shard_map/all_to_all | solution.py:229

commit v8 on v7

--- a/solution.py
+++ b/solution.py
@@ -38,7 +38,7 @@
         ],
         axis=0,
     ).astype(bf16)
-    for k in range(2 * NZ):
+    for k in range(NZ):
         row_ref[k] = rec
 
 
@@ -115,9 +115,9 @@
         t = a[:, :F] - a[:, NORM:NORM + 1] * buf[2][:, :F]
         t = t.reshape(BI // PR, 2, PR // 2, F)
         t = jnp.concatenate([t[:, 0], t[:, 1]], axis=-1).reshape(BI // 2, 128)
-        at = 4 * jnp.int32(i % 2 != core) + 2 * jnp.int32(i // 2 != xb)
+        at = 2 * jnp.int32(i % 2 != xb) + i // 2
         for h in range(2):
-            part[at + h] = t[h * (BI // 4):(h + 1) * (BI // 4)]
+            part[at + 4 * jnp.int32(h != core)] = t[h * (BI // 4):(h + 1) * (BI // 4)]
 
     def both(i, new, old):
         rb = front(i, new)
@@ -185,7 +185,7 @@
     shape = jax.ShapeDtypeStruct
     rows = pl.pallas_call(
         pack_rows,
-        out_shape=shape((2 * NZ, 24, 128), bf16),
+        out_shape=shape((NZ, 24, 128), bf16),
         in_specs=[VM] * 2,
         out_specs=VM,
     )(row_points, row_solves)
@@ -195,10 +195,10 @@
         in_specs=[VM] * 2,
         out_specs=VM,
     )(col_points.T, col_probes.T)
-    rows = lax.all_to_all(rows, XZ, 0, 0, tiled=True)
+    rows = lax.all_to_all(rows, ("zh", "zl"), 0, 0, tiled=True)
     rows, cols = lax.optimization_barrier((rows, cols))
     cols = lax.all_to_all(cols, "y", 0, 0, tiled=True, axis_index_groups=ORDER)
-    rows = lax.all_gather(rows.reshape(2 * NZ * 24, 128), ("xb", "core"), axis=0, tiled=True)
+    rows = lax.all_gather(rows.reshape(NZ * 24, 128), ("xa", "xb", "core"), axis=0, tiled=True)
     part = R // (2 * NX * NC)
     keep, swap, col_part = pl.pallas_call(
         main_kernel,

time: 105 us -> 103 us (0.981)
  blocking collectives: 6.68 us -> 13.5 us
  waiting for transfers between devices: 34.8 us -> 28 us
  starting transfers between devices: 40.3 us -> 38.8 us
    all_gather x1, blocking collectives: 6.68 us -> 13.5 us  [body(): lax.all_gather(rows.reshape(NZ * 24, 128), ('xa', 'xb', 'core'), axis=0,...]
    all_to_all x1, waiting for transfers between devices: 4.78 us -> 0.01 us  [body(): cols = lax.all_to_all(cols, 'y', 0, 0, tiled=True, axis_index_groups=ORDER)]
    all_to_all x1, waiting for transfers between devices: 12.7 us -> 9.56 us  [body(): rows = lax.all_to_all(rows, ('zh', 'zl'), 0, 0, tiled=True)]
    all_to_all x1, starting transfers between devices: 17.8 us -> 15.2 us  [body(): rows = lax.all_to_all(rows, ('zh', 'zl'), 0, 0, tiled=True)]
    all_to_all x1, starting transfers between devices: 4.65 us -> 7.21 us  [body(): lax.all_to_all(col_part, 'y', 0, 0, tiled=True, axis_index_groups=ORDER)]
    all_to_all x1, starting transfers between devices: 5.86 us -> 3.82 us  [body(): row_part = lax.all_to_all(row_part, XZ, 0, 0, tiled=True)]
    all_to_all x1, waiting for transfers between devices: 0.01 us -> 1.57 us  [body(): lax.all_to_all(col_part, 'y', 0, 0, tiled=True, axis_index_groups=ORDER)]
where the time goes in v8:
time: 103 us
  starting transfers between devices  38.8 us (38%)
  waiting for transfers between devices  28 us (27%)
  Pallas kernels  21.1 us (20%)
  blocking collectives  13.5 us (13%)
    pallas_call x1, Pallas kernels, body(): pl.pallas_call(main_kernel, out_shape=(shape((NX, part, 128), f32), shape...  16.5 us
    all_to_all x1, starting transfers between devices, body(): rows = lax.all_to_all(rows, ('zh', 'zl'), 0, 0, tiled=True)  15.2 us
    all_gather x1, blocking collectives, body(): lax.all_gather(rows.reshape(NZ * 24, 128), ('xa', 'xb', 'core'), axis=0,...  13.5 us
    all_to_all x1, waiting for transfers between devices, body(): row_part = lax.all_to_all(row_part, XZ, 0, 0, tiled=True)  11.8 us
    all_to_all x1, waiting for transfers between devices, body(): rows = lax.all_to_all(rows, ('zh', 'zl'), 0, 0, tiled=True)  9.56 us
    all_to_all x1, starting transfers between devices, body(): cols = lax.all_to_all(cols, 'y', 0, 0, tiled=True, axis_index_groups=ORDER)  7.55 us
    all_to_all x1, starting transfers between devices, body(): lax.all_to_all(col_part, 'y', 0, 0, tiled=True, axis_index_groups=ORDER)  7.21 us
    all_to_all x1, starting transfers between devices, body(): row_part = lax.all_to_all(row_part, XZ, 0, 0, tiled=True)  3.82 us
  transfers between devices with their start and end apart: 6, of which 5 were waited for; matrix products, arithmetic and copies ran while one was open for 1% of the time, Pallas kernels for 2%

profile of v8, /device:TPU:8, one launch (start us, length us, event | category | flops | bytes accessed | tf_op | source)
XLA Modules:
  0.0 102.6 jit_solution(2609697587587149733)
XLA Ops:
  0.6 1.4 %shard_map.59 = bf16[12,24,128]{2,1,0:T(8,128)(2,1)} custom-call(bf16[32,64]{1,0:T(8,128)(2,1)} %rp_ref.1, bf16[32,32]{1,0:T(8,128)(2,1)} %rs_ref.1), custom_call_target="tpu_custom_call" | custom-call | tf_op jit(solution)/shard_map/pallas_call | solution.py:186
  2.1 15.2 %all-to-all-start = ((bf16[12,24,128]{2,1,0:T(8,128)(2,1)}), bf16[12,24,128]{2,1,0:T(8,128)(2,1)S(1)}, u32[]{:S(2)}, u32[]{:S(2)}) async-start(bf16[12,24,128]{2,1,0:T(8,128)(2,1)} %shard_map.59), calls=%async_computation | async-start | bytes 147456 | tf_op jit(solution)/shard_map/all_to_all | solution.py:198
  17.2 1.7 %shard_map.60 = bf16[8,240,128]{2,1,0:T(8,128)(2,1)} custom-call(bf16[64,320]{1,0:T(8,128)(2,1)} %bitcast.7, bf16[32,320]{1,0:T(8,128)(2,1)} %bitcast.8), custom_call_target="tpu_custom_call" | custom-call | tf_op jit(solution)/shard_map/pallas_call | solution.py:192
  18.9 9.6 %all-to-all-done = bf16[12,24,128]{2,1,0:T(8,128)(2,1)S(1)} async-done(((bf16[12,24,128]{2,1,0:T(8,128)(2,1)}), bf16[12,24,128]{2,1,0:T(8,128)(2,1)S(1)}, u32[]{:S(2)}, u32[]{:S(2)}) %all-to-all-start) | async-done | bytes 73760 | tf_op jit(solution)/shard_map/all_to_all | solution.py:198
  28.4 7.5 %all-to-all-start.1 = ((bf16[8,240,128]{2,1,0:T(8,128)(2,1)}), bf16[8,240,128]{2,1,0:T(8,128)(2,1)S(1)}, u32[]{:S(2)}, u32[]{:S(2)}) async-start(bf16[8,240,128]{2,1,0:T(8,128)(2,1)} %shard_map.60), calls=%async_computation.1 | async-start | bytes 983040 | tf_op jit(solution)/shard_map/all_to_all | solution.py:200
  36.0 13.5 %all_gather.3.r_ref = bf16[2304,128]{1,0:T(8,128)(2,1)S(1)} all-gather(bf16[288,128]{1,0:T(8,128)(2,1)S(1)} %bitcast.5), channel_id=1, replica_groups=mesh['y'=8,'zh'=3,'xa'=2,'xb'=2,'zl'=4,'core'=2] {'xa','xb','core'}, dimensions={0}, use_global_device_ids=true | all-gather | bytes 663552 | tf_op jit(solution)/shard_map/all_gather | solution.py:201
  49.5 0.0 all-to-all-done.1.p_ref
  49.5 16.5 %shard_map.61 = (f32[4,192,128]{2,1,0:T(8,128)S(1)}, bf16[4,192,128]{2,1,0:T(8,128)(2,1)S(1)}, bf16[8,160,128]{2,1,0:T(8,128)(2,1)}) custom-call(bf16[2304,128]{1,0:T(8,128)(2,1)S(1)} %all_gather.3.r_ref, bf16[8,240,128]{2,1,0:T(8,128)(2,1)S(1)} %all-to-all-done.1.p_ref), custom_call_target="tpu_custom_call" | custom-call | tf_op jit(solution)/shard_map/pallas_call | solution.py:203
  66.0 7.2 %all-to-all-start.2 = ((bf16[8,160,128]{2,1,0:T(8,128)(2,1)}), bf16[8,160,128]{2,1,0:T(8,128)(2,1)S(1)}, u32[]{:S(2)}, u32[]{:S(2)}) async-start(bf16[8,160,128]{2,1,0:T(8,128)(2,1)} %get-tuple-element.17), calls=%async_computation.2 | async-start | bytes 655360 | tf_op jit(solution)/shard_map/all_to_all | solution.py:224
  73.2 1.9 %collective-permute-start = (bf16[4,192,128]{2,1,0:T(8,128)(2,1)S(1)}, bf16[4,192,128]{2,1,0:T(8,128)(2,1)S(1)}, u32[]{:S(2)}, u32[]{:S(2)}) collective-permute-start(bf16[4,192,128]{2,1,0:T(8,128)(2,1)S(1)} %get-tuple-element.14), channel_id=1, source_target_pairs={{0,1},{1,0},{2,3},{3,2},{4,5},{5,4},{6,7},{7,6},{8,9},{9,8},{10,11... | collective-permute-start | bytes 589832 | tf_op jit(solution)/shard_map/ppermute | solution.py:225
  75.2 1.4 %collective-permute-done.got_ref = bf16[4,192,128]{2,1,0:T(8,128)(2,1)S(1)} collective-permute-done((bf16[4,192,128]{2,1,0:T(8,128)(2,1)S(1)}, bf16[4,192,128]{2,1,0:T(8,128)(2,1)S(1)}, u32[]{:S(2)}, u32[]{:S(2)}) %collective-permute-start) | collective-permute-done | bytes 196640 | tf_op jit(solution)/shard_map/ppermute | solution.py:225
  76.6 3.1 %collective-permute-start.1 = (bf16[2,192,128]{2,1,0:T(8,128)(2,1)S(1)}, bf16[2,192,128]{2,1,0:T(8,128)(2,1)S(1)}, u32[]{:S(2)}, u32[]{:S(2)}) collective-permute-start(bf16[2,192,128]{2,1,0:T(8,128)(2,1)S(1)} %get-tuple-element.16), channel_id=1, source_target_pairs={{0,8},{8,0},{1,9},{9,1},{2,10},{10,2},{3,11},{11,3},{4,12},{12,4},... | collective-permute-start | bytes 294920 | tf_op jit(solution)/shard_map/ppermute | solution.py:226
  79.7 3.6 %collective-permute-done.1 = bf16[2,192,128]{2,1,0:T(8,128)(2,1)S(1)} collective-permute-done((bf16[2,192,128]{2,1,0:T(8,128)(2,1)S(1)}, bf16[2,192,128]{2,1,0:T(8,128)(2,1)S(1)}, u32[]{:S(2)}, u32[]{:S(2)}) %collective-permute-start.1) | collective-permute-done | bytes 98336 | tf_op jit(solution)/shard_map/ppermute | solution.py:226
  83.3 0.7 add_convert_fusion
  84.0 1.6 %all-to-all-done.2.col_ref = bf16[8,160,128]{2,1,0:T(8,128)(2,1)S(1)} async-done(((bf16[8,160,128]{2,1,0:T(8,128)(2,1)}), bf16[8,160,128]{2,1,0:T(8,128)(2,1)S(1)}, u32[]{:S(2)}, u32[]{:S(2)}) %all-to-all-start.2) | async-done | bytes 327712 | tf_op jit(solution)/shard_map/all_to_all | solution.py:224
  85.6 3.8 %all-to-all-start.3 = ((bf16[24,16,128]{2,1,0:T(8,128)(2,1)}), bf16[24,16,128]{2,1,0:T(8,128)(2,1)S(1)}, u32[]{:S(2)}, u32[]{:S(2)}) async-start(bf16[24,16,128]{2,1,0:T(8,128)(2,1)} %bitcast.3), calls=%async_computation.3 | async-start | bytes 196608 | tf_op jit(solution)/shard_map/all_to_all | solution.py:229
  89.4 0.7 shard_map.64
  90.1 11.8 %all-to-all-done.3.row_ref = bf16[24,16,128]{2,1,0:T(8,128)(2,1)S(1)} async-done(((bf16[24,16,128]{2,1,0:T(8,128)(2,1)}), bf16[24,16,128]{2,1,0:T(8,128)(2,1)S(1)}, u32[]{:S(2)}, u32[]{:S(2)}) %all-to-all-start.3) | async-done | bytes 98336 | tf_op jit(solution)/shard_map/all_to_all | solution.py:229
  101.9 0.7 shard_map.63
  (1 shorter events, 0.0 us)
Async XLA Ops:
  2.1 26.4 %all-to-all-start = ((bf16[12,24,128]{2,1,0:T(8,128)(2,1)}), bf16[12,24,128]{2,1,0:T(8,128)(2,1)S(1)}, u32[]{:S(2)}, u32[]{:S(2)}) async-start(bf16[12,24,128]{2,1,0:T(8,128)(2,1)} %shard_map.59), calls=%async_computation | async-start | bytes 147456 | tf_op jit(solution)/shard_map/all_to_all | solution.py:198
  28.4 21.1 %all-to-all-start.1 = ((bf16[8,240,128]{2,1,0:T(8,128)(2,1)}), bf16[8,240,128]{2,1,0:T(8,128)(2,1)S(1)}, u32[]{:S(2)}, u32[]{:S(2)}) async-start(bf16[8,240,128]{2,1,0:T(8,128)(2,1)} %shard_map.60), calls=%async_computation.1 | async-start | bytes 983040 | tf_op jit(solution)/shard_map/all_to_all | solution.py:200
  66.0 19.5 %all-to-all-start.2 = ((bf16[8,160,128]{2,1,0:T(8,128)(2,1)}), bf16[8,160,128]{2,1,0:T(8,128)(2,1)S(1)}, u32[]{:S(2)}, u32[]{:S(2)}) async-start(bf16[8,160,128]{2,1,0:T(8,128)(2,1)} %get-tuple-element.17), calls=%async_computation.2 | async-start | bytes 655360 | tf_op jit(solution)/shard_map/all_to_all | solution.py:224
  73.2 3.3 %collective-permute-start = (bf16[4,192,128]{2,1,0:T(8,128)(2,1)S(1)}, bf16[4,192,128]{2,1,0:T(8,128)(2,1)S(1)}, u32[]{:S(2)}, u32[]{:S(2)}) collective-permute-start(bf16[4,192,128]{2,1,0:T(8,128)(2,1)S(1)} %get-tuple-element.14), channel_id=1, source_target_pairs={{0,1},{1,0},{2,3},{3,2},{4,5},{5,4},{6,7},{7,6},{8,9},{9,8},{10,11... | collective-permute-start | bytes 589832 | tf_op jit(solution)/shard_map/ppermute | solution.py:225
  76.6 6.7 %collective-permute-start.1 = (bf16[2,192,128]{2,1,0:T(8,128)(2,1)S(1)}, bf16[2,192,128]{2,1,0:T(8,128)(2,1)S(1)}, u32[]{:S(2)}, u32[]{:S(2)}) collective-permute-start(bf16[2,192,128]{2,1,0:T(8,128)(2,1)S(1)} %get-tuple-element.16), channel_id=1, source_target_pairs={{0,8},{8,0},{1,9},{9,1},{2,10},{10,2},{3,11},{11,3},{4,12},{12,4},... | collective-permute-start | bytes 294920 | tf_op jit(solution)/shard_map/ppermute | solution.py:226
  85.6 16.4 %all-to-all-start.3 = ((bf16[24,16,128]{2,1,0:T(8,128)(2,1)}), bf16[24,16,128]{2,1,0:T(8,128)(2,1)S(1)}, u32[]{:S(2)}, u32[]{:S(2)}) async-start(bf16[24,16,128]{2,1,0:T(8,128)(2,1)} %bitcast.3), calls=%async_computation.3 | async-start | bytes 196608 | tf_op jit(solution)/shard_map/all_to_all | solution.py:229

commit v9 on v8

--- a/solution.py
+++ b/solution.py
@@ -10,7 +10,10 @@
 NAMES = ("y", "zh", "xa", "xb", "zl", "core")
 SIZES = (8, 3, 2, 2, 4, 2)
 XZ = ("xa", "zh", "zl")
-ORDER = [[0, 2, 4, 6, 1, 3, 5, 7]]
+Y_ORDER = [0, 2, 4, 6, 1, 3, 5, 7]
+Z_ORDER = [0, 2, 4, 6, 8, 10, 1, 3, 5, 7, 9, 11]
+TURN = 3
+XZ_ORDER = [12 * a + z for a in range(2) for z in Z_ORDER[TURN:] + Z_ORDER[:TURN]]
 NX, NY, NZ, NC = 4, 8, 12, 2
 PR, PC, F, Q = 32, 320, 64, 32
 R, C = PR * NX * NZ * NC, PC * NY
@@ -195,9 +198,9 @@
         in_specs=[VM] * 2,
         out_specs=VM,
     )(col_points.T, col_probes.T)
-    rows = lax.all_to_all(rows, ("zh", "zl"), 0, 0, tiled=True)
+    rows = lax.all_to_all(rows, ("zh", "zl"), 0, 0, tiled=True, axis_index_groups=[Z_ORDER])
     rows, cols = lax.optimization_barrier((rows, cols))
-    cols = lax.all_to_all(cols, "y", 0, 0, tiled=True, axis_index_groups=ORDER)
+    cols = lax.all_to_all(cols, "y", 0, 0, tiled=True, axis_index_groups=[Y_ORDER])
     rows = lax.all_gather(rows.reshape(NZ * 24, 128), ("xa", "xb", "core"), axis=0, tiled=True)
     part = R // (2 * NX * NC)
     keep, swap, col_part = pl.pallas_call(
@@ -221,12 +224,13 @@
         ],
         compiler_params=pltpu.CompilerParams(vmem_limit_bytes=40 * 2**20),
     )(rows, cols)
-    col_part = lax.all_to_all(col_part, "y", 0, 0, tiled=True, axis_index_groups=ORDER)
+    col_part = lax.all_to_all(col_part, "y", 0, 0, tiled=True, axis_index_groups=[Y_ORDER])
     keep, out = add(keep, lax.ppermute(swap, "core", [(0, 1), (1, 0)]))
     row_part = keep + lax.ppermute(out, "xb", [(0, 1), (1, 0)]).astype(f32)
-    row_part = row_part.astype(bf16).reshape(2 * NZ, PR // 2, 128)
+    row_part = row_part.astype(bf16).reshape(2, NZ, PR // 2, 128)
+    row_part = jnp.concatenate([row_part[:, TURN:], row_part[:, :TURN]], axis=1).reshape(2 * NZ, PR // 2, 128)
     row_part, col_part = lax.optimization_barrier((row_part, col_part))
-    row_part = lax.all_to_all(row_part, XZ, 0, 0, tiled=True)
+    row_part = lax.all_to_all(row_part, XZ, 0, 0, tiled=True, axis_index_groups=[XZ_ORDER])
     row_grad = pl.pallas_call(
         finish_rows,
         out_shape=shape((PR, F), f32),

time: 103 us -> 105 us (1.019)
  the two profiles are of different devices: /device:TPU:8 before, /device:TPU:10 now
where the time goes in v9:
time: 105 us
  starting transfers between devices  45.6 us (43%)
  waiting for transfers between devices  23.4 us (22%)
  Pallas kernels  21.1 us (20%)
  blocking collectives  13.2 us (13%)
    pallas_call x1, Pallas kernels, body(): pl.pallas_call(main_kernel, out_shape=(shape((NX, part, 128), f32), shape...  16.5 us
    all_to_all x1, starting transfers between devices, body(): lax.all_to_all(rows, ('zh', 'zl'), 0, 0, tiled=True, axis_index_groups=[Z...  15.2 us
    all_gather x1, blocking collectives, body(): lax.all_gather(rows.reshape(NZ * 24, 128), ('xa', 'xb', 'core'), axis=0,...  13.2 us
    all_to_all x1, starting transfers between devices, body(): lax.all_to_all(row_part, XZ, 0, 0, tiled=True, axis_index_groups=[XZ_ORDER])  11.2 us
    all_to_all x1, waiting for transfers between devices, body(): lax.all_to_all(rows, ('zh', 'zl'), 0, 0, tiled=True, axis_index_groups=[Z...  8.83 us
    all_to_all x1, starting transfers between devices, body(): lax.all_to_all(cols, 'y', 0, 0, tiled=True, axis_index_groups=[Y_ORDER])  7.55 us
    all_to_all x1, starting transfers between devices, body(): lax.all_to_all(col_part, 'y', 0, 0, tiled=True, axis_index_groups=[Y_ORDER])  7.1 us
    all_to_all x1, waiting for transfers between devices, body(): lax.all_to_all(row_part, XZ, 0, 0, tiled=True, axis_index_groups=[XZ_ORDER])  5.48 us
  transfers between devices with their start and end apart: 6, of which 5 were waited for; matrix products, arithmetic and copies ran while one was open for 1% of the time, Pallas kernels for 2%

profile of v9, /device:TPU:10, one launch (start us, length us, event | category | flops | bytes accessed | tf_op | source)
XLA Modules:
  0.0 104.7 jit_solution(127638800226983991)
XLA Ops:
  0.6 1.4 %shard_map.59 = bf16[12,24,128]{2,1,0:T(8,128)(2,1)} custom-call(bf16[32,64]{1,0:T(8,128)(2,1)} %rp_ref.1, bf16[32,32]{1,0:T(8,128)(2,1)} %rs_ref.1), custom_call_target="tpu_custom_call" | custom-call | tf_op jit(solution)/shard_map/pallas_call | solution.py:189
  2.1 15.2 %all-to-all-start = ((bf16[12,24,128]{2,1,0:T(8,128)(2,1)}), bf16[12,24,128]{2,1,0:T(8,128)(2,1)S(1)}, u32[]{:S(2)}, u32[]{:S(2)}) async-start(bf16[12,24,128]{2,1,0:T(8,128)(2,1)} %shard_map.59), calls=%async_computation | async-start | bytes 147456 | tf_op jit(solution)/shard_map/all_to_all | solution.py:201
  17.2 1.7 %shard_map.60 = bf16[8,240,128]{2,1,0:T(8,128)(2,1)} custom-call(bf16[64,320]{1,0:T(8,128)(2,1)} %bitcast.10, bf16[32,320]{1,0:T(8,128)(2,1)} %bitcast.11), custom_call_target="tpu_custom_call" | custom-call | tf_op jit(solution)/shard_map/pallas_call | solution.py:195
  18.9 8.8 %all-to-all-done = bf16[12,24,128]{2,1,0:T(8,128)(2,1)S(1)} async-done(((bf16[12,24,128]{2,1,0:T(8,128)(2,1)}), bf16[12,24,128]{2,1,0:T(8,128)(2,1)S(1)}, u32[]{:S(2)}, u32[]{:S(2)}) %all-to-all-start) | async-done | bytes 73760 | tf_op jit(solution)/shard_map/all_to_all | solution.py:201
  27.7 7.5 %all-to-all-start.1 = ((bf16[8,240,128]{2,1,0:T(8,128)(2,1)}), bf16[8,240,128]{2,1,0:T(8,128)(2,1)S(1)}, u32[]{:S(2)}, u32[]{:S(2)}) async-start(bf16[8,240,128]{2,1,0:T(8,128)(2,1)} %shard_map.60), calls=%async_computation.1 | async-start | bytes 983040 | tf_op jit(solution)/shard_map/all_to_all | solution.py:203
  35.3 13.2 %all_gather.3.r_ref = bf16[2304,128]{1,0:T(8,128)(2,1)S(1)} all-gather(bf16[288,128]{1,0:T(8,128)(2,1)S(1)} %bitcast.8), channel_id=1, replica_groups=mesh['y'=8,'zh'=3,'xa'=2,'xb'=2,'zl'=4,'core'=2] {'xa','xb','core'}, dimensions={0}, use_global_device_ids=true | all-gather | bytes 663552 | tf_op jit(solution)/shard_map/all_gather | solution.py:204
  48.5 0.5 all-to-all-done.1.p_ref
  48.9 16.5 %shard_map.61 = (f32[4,192,128]{2,1,0:T(8,128)S(1)}, bf16[4,192,128]{2,1,0:T(8,128)(2,1)S(1)}, bf16[8,160,128]{2,1,0:T(8,128)(2,1)}) custom-call(bf16[2304,128]{1,0:T(8,128)(2,1)S(1)} %all_gather.3.r_ref, bf16[8,240,128]{2,1,0:T(8,128)(2,1)S(1)} %all-to-all-done.1.p_ref), custom_call_target="tpu_custom_call" | custom-call | tf_op jit(solution)/shard_map/pallas_call | solution.py:206
  65.5 1.9 %collective-permute-start = (bf16[4,192,128]{2,1,0:T(8,128)(2,1)S(1)}, bf16[4,192,128]{2,1,0:T(8,128)(2,1)S(1)}, u32[]{:S(2)}, u32[]{:S(2)}) collective-permute-start(bf16[4,192,128]{2,1,0:T(8,128)(2,1)S(1)} %get-tuple-element.14), channel_id=1, source_target_pairs={{0,1},{1,0},{2,3},{3,2},{4,5},{5,4},{6,7},{7,6},{8,9},{9,8},{10,11... | collective-permute-start | bytes 589832 | tf_op jit(solution)/shard_map/ppermute | solution.py:228
  67.4 7.1 %all-to-all-start.2 = ((bf16[8,160,128]{2,1,0:T(8,128)(2,1)}), bf16[8,160,128]{2,1,0:T(8,128)(2,1)S(1)}, u32[]{:S(2)}, u32[]{:S(2)}) async-start(bf16[8,160,128]{2,1,0:T(8,128)(2,1)} %get-tuple-element.17), calls=%async_computation.2 | async-start | bytes 655360 | tf_op jit(solution)/shard_map/all_to_all | solution.py:227
  74.5 0.0 collective-permute-done.got_ref
  74.5 2.7 %collective-permute-start.1 = (bf16[2,192,128]{2,1,0:T(8,128)(2,1)S(1)}, bf16[2,192,128]{2,1,0:T(8,128)(2,1)S(1)}, u32[]{:S(2)}, u32[]{:S(2)}) collective-permute-start(bf16[2,192,128]{2,1,0:T(8,128)(2,1)S(1)} %get-tuple-element.16), channel_id=1, source_target_pairs={{0,8},{8,0},{1,9},{9,1},{2,10},{10,2},{3,11},{11,3},{4,12},{12,4},... | collective-permute-start | bytes 294920 | tf_op jit(solution)/shard_map/ppermute | solution.py:229
  77.3 3.8 %collective-permute-done.1 = bf16[2,192,128]{2,1,0:T(8,128)(2,1)S(1)} collective-permute-done((bf16[2,192,128]{2,1,0:T(8,128)(2,1)S(1)}, bf16[2,192,128]{2,1,0:T(8,128)(2,1)S(1)}, u32[]{:S(2)}, u32[]{:S(2)}) %collective-permute-start.1) | collective-permute-done | bytes 98336 | tf_op jit(solution)/shard_map/ppermute | solution.py:229
  81.1 0.6 pad_maximum_fusion
  81.7 4.9 %all-to-all-done.2.col_ref = bf16[8,160,128]{2,1,0:T(8,128)(2,1)S(1)} async-done(((bf16[8,160,128]{2,1,0:T(8,128)(2,1)}), bf16[8,160,128]{2,1,0:T(8,128)(2,1)S(1)}, u32[]{:S(2)}, u32[]{:S(2)}) %all-to-all-start.2) | async-done | bytes 327712 | tf_op jit(solution)/shard_map/all_to_all | solution.py:227
  86.6 11.2 %all-to-all-start.3 = ((bf16[24,16,128]{2,1,0:T(8,128)(2,1)}), bf16[24,16,128]{2,1,0:T(8,128)(2,1)S(1)}, u32[]{:S(2)}, u32[]{:S(2)}) async-start(bf16[24,16,128]{2,1,0:T(8,128)(2,1)} %bitcast.4), calls=%async_computation.3 | async-start | bytes 196608 | tf_op jit(solution)/shard_map/all_to_all | solution.py:233
  97.8 0.7 shard_map.64
  98.5 5.5 %all-to-all-done.3.row_ref = bf16[24,16,128]{2,1,0:T(8,128)(2,1)S(1)} async-done(((bf16[24,16,128]{2,1,0:T(8,128)(2,1)}), bf16[24,16,128]{2,1,0:T(8,128)(2,1)S(1)}, u32[]{:S(2)}, u32[]{:S(2)}) %all-to-all-start.3) | async-done | bytes 98336 | tf_op jit(solution)/shard_map/all_to_all | solution.py:233
  104.0 0.7 shard_map.63
  (4 shorter events, 0.1 us)
Async XLA Ops:
  2.1 25.7 %all-to-all-start = ((bf16[12,24,128]{2,1,0:T(8,128)(2,1)}), bf16[12,24,128]{2,1,0:T(8,128)(2,1)S(1)}, u32[]{:S(2)}, u32[]{:S(2)}) async-start(bf16[12,24,128]{2,1,0:T(8,128)(2,1)} %shard_map.59), calls=%async_computation | async-start | bytes 147456 | tf_op jit(solution)/shard_map/all_to_all | solution.py:201
  27.7 21.2 %all-to-all-start.1 = ((bf16[8,240,128]{2,1,0:T(8,128)(2,1)}), bf16[8,240,128]{2,1,0:T(8,128)(2,1)S(1)}, u32[]{:S(2)}, u32[]{:S(2)}) async-start(bf16[8,240,128]{2,1,0:T(8,128)(2,1)} %shard_map.60), calls=%async_computation.1 | async-start | bytes 983040 | tf_op jit(solution)/shard_map/all_to_all | solution.py:203
  65.5 9.0 %collective-permute-start = (bf16[4,192,128]{2,1,0:T(8,128)(2,1)S(1)}, bf16[4,192,128]{2,1,0:T(8,128)(2,1)S(1)}, u32[]{:S(2)}, u32[]{:S(2)}) collective-permute-start(bf16[4,192,128]{2,1,0:T(8,128)(2,1)S(1)} %get-tuple-element.14), channel_id=1, source_target_pairs={{0,1},{1,0},{2,3},{3,2},{4,5},{5,4},{6,7},{7,6},{8,9},{9,8},{10,11... | collective-permute-start | bytes 589832 | tf_op jit(solution)/shard_map/ppermute | solution.py:228
  67.4 19.3 %all-to-all-start.2 = ((bf16[8,160,128]{2,1,0:T(8,128)(2,1)}), bf16[8,160,128]{2,1,0:T(8,128)(2,1)S(1)}, u32[]{:S(2)}, u32[]{:S(2)}) async-start(bf16[8,160,128]{2,1,0:T(8,128)(2,1)} %get-tuple-element.17), calls=%async_computation.2 | async-start | bytes 655360 | tf_op jit(solution)/shard_map/all_to_all | solution.py:227
  74.5 6.5 %collective-permute-start.1 = (bf16[2,192,128]{2,1,0:T(8,128)(2,1)S(1)}, bf16[2,192,128]{2,1,0:T(8,128)(2,1)S(1)}, u32[]{:S(2)}, u32[]{:S(2)}) collective-permute-start(bf16[2,192,128]{2,1,0:T(8,128)(2,1)S(1)} %get-tuple-element.16), channel_id=1, source_target_pairs={{0,8},{8,0},{1,9},{9,1},{2,10},{10,2},{3,11},{11,3},{4,12},{12,4},... | collective-permute-start | bytes 294920 | tf_op jit(solution)/shard_map/ppermute | solution.py:229
  86.6 17.4 %all-to-all-start.3 = ((bf16[24,16,128]{2,1,0:T(8,128)(2,1)}), bf16[24,16,128]{2,1,0:T(8,128)(2,1)S(1)}, u32[]{:S(2)}, u32[]{:S(2)}) async-start(bf16[24,16,128]{2,1,0:T(8,128)(2,1)} %bitcast.4), calls=%async_computation.3 | async-start | bytes 196608 | tf_op jit(solution)/shard_map/all_to_all | solution.py:233

commit v10 on v9

--- a/solution.py
+++ b/solution.py
@@ -12,8 +12,7 @@
 XZ = ("xa", "zh", "zl")
 Y_ORDER = [0, 2, 4, 6, 1, 3, 5, 7]
 Z_ORDER = [0, 2, 4, 6, 8, 10, 1, 3, 5, 7, 9, 11]
-TURN = 3
-XZ_ORDER = [12 * a + z for a in range(2) for z in Z_ORDER[TURN:] + Z_ORDER[:TURN]]
+XZ_ORDER = [12 * a + z for a in range(2) for z in Z_ORDER]
 NX, NY, NZ, NC = 4, 8, 12, 2
 PR, PC, F, Q = 32, 320, 64, 32
 R, C = PR * NX * NZ * NC, PC * NY
@@ -227,8 +226,7 @@
     col_part = lax.all_to_all(col_part, "y", 0, 0, tiled=True, axis_index_groups=[Y_ORDER])
     keep, out = add(keep, lax.ppermute(swap, "core", [(0, 1), (1, 0)]))
     row_part = keep + lax.ppermute(out, "xb", [(0, 1), (1, 0)]).astype(f32)
-    row_part = row_part.astype(bf16).reshape(2, NZ, PR // 2, 128)
-    row_part = jnp.concatenate([row_part[:, TURN:], row_part[:, :TURN]], axis=1).reshape(2 * NZ, PR // 2, 128)
+    row_part = row_part.astype(bf16).reshape(2 * NZ, PR // 2, 128)
     row_part, col_part = lax.optimization_barrier((row_part, col_part))
     row_part = lax.all_to_all(row_part, XZ, 0, 0, tiled=True, axis_index_groups=[XZ_ORDER])
     row_grad = pl.pallas_call(

time: 105 us -> 104 us (level)
  starting transfers between devices: 45.6 us -> 39 us
  waiting for transfers between devices: 23.4 us -> 29 us
    all_to_all x1, waiting for transfers between devices: 5.48 us -> 12.7 us  [body(): lax.all_to_all(row_part, XZ, 0, 0, tiled=True, axis_index_groups=[XZ_ORDER])]
    all_to_all x1, starting transfers between devices: 11.2 us -> 4.93 us  [body(): lax.all_to_all(row_part, XZ, 0, 0, tiled=True, axis_index_groups=[XZ_ORDER])]
    all_to_all x1, waiting for transfers between devices: 4.91 us -> 1.56 us  [body(): lax.all_to_all(col_part, 'y', 0, 0, tiled=True, axis_index_groups=[Y_ORDER])]
    ppermute x1, waiting for transfers between devices: 0.01 us -> 1.41 us  [body(): keep, out = add(keep, lax.ppermute(swap, 'core', [(0, 1), (1, 0)]))]
  transfers between devices with their start and end apart: 6 -> 6, of which waited for: 5 -> 6; matrix products, arithmetic and copies ran while one was open for 1% -> 1% of each run, Pallas kernels for 2% -> 2%
where the time goes in v10:
time: 104 us
  starting transfers between devices  39 us (38%)
  waiting for transfers between devices  29 us (28%)
  Pallas kernels  21.1 us (20%)
  blocking collectives  13.2 us (13%)
    pallas_call x1, Pallas kernels, body(): pl.pallas_call(main_kernel, out_shape=(shape((NX, part, 128), f32), shape...  16.5 us
    all_to_all x1, starting transfers between devices, body(): lax.all_to_all(rows, ('zh', 'zl'), 0, 0, tiled=True, axis_index_groups=[Z...  15.2 us
    all_gather x1, blocking collectives, body(): lax.all_gather(rows.reshape(NZ * 24, 128), ('xa', 'xb', 'core'), axis=0,...  13.2 us
    all_to_all x1, waiting for transfers between devices, body(): lax.all_to_all(row_part, XZ, 0, 0, tiled=True, axis_index_groups=[XZ_ORDER])  12.7 us
    all_to_all x1, waiting for transfers between devices, body(): lax.all_to_all(rows, ('zh', 'zl'), 0, 0, tiled=True, axis_index_groups=[Z...  8.83 us
    all_to_all x1, starting transfers between devices, body(): lax.all_to_all(cols, 'y', 0, 0, tiled=True, axis_index_groups=[Y_ORDER])  7.55 us
    all_to_all x1, starting transfers between devices, body(): lax.all_to_all(col_part, 'y', 0, 0, tiled=True, axis_index_groups=[Y_ORDER])  6.76 us
    all_to_all x1, starting transfers between devices, body(): lax.all_to_all(row_part, XZ, 0, 0, tiled=True, axis_index_groups=[XZ_ORDER])  4.93 us
  transfers between devices with their start and end apart: 6, of which 6 were waited for; matrix products, arithmetic and copies ran while one was open for 1% of the time, Pallas kernels for 2%

profile of v10, /device:TPU:10, one launch (start us, length us, event | category | flops | bytes accessed | tf_op | source)
XLA Modules:
  0.0 103.6 jit_solution(12883910403579473710)
XLA Ops:
  0.6 1.4 %shard_map.59 = bf16[12,24,128]{2,1,0:T(8,128)(2,1)} custom-call(bf16[32,64]{1,0:T(8,128)(2,1)} %rp_ref.1, bf16[32,32]{1,0:T(8,128)(2,1)} %rs_ref.1), custom_call_target="tpu_custom_call" | custom-call | tf_op jit(solution)/shard_map/pallas_call | solution.py:188
  2.1 15.2 %all-to-all-start = ((bf16[12,24,128]{2,1,0:T(8,128)(2,1)}), bf16[12,24,128]{2,1,0:T(8,128)(2,1)S(1)}, u32[]{:S(2)}, u32[]{:S(2)}) async-start(bf16[12,24,128]{2,1,0:T(8,128)(2,1)} %shard_map.59), calls=%async_computation | async-start | bytes 147456 | tf_op jit(solution)/shard_map/all_to_all | solution.py:200
  17.2 1.7 %shard_map.60 = bf16[8,240,128]{2,1,0:T(8,128)(2,1)} custom-call(bf16[64,320]{1,0:T(8,128)(2,1)} %bitcast.7, bf16[32,320]{1,0:T(8,128)(2,1)} %bitcast.8), custom_call_target="tpu_custom_call" | custom-call | tf_op jit(solution)/shard_map/pallas_call | solution.py:194
  18.9 8.8 %all-to-all-done = bf16[12,24,128]{2,1,0:T(8,128)(2,1)S(1)} async-done(((bf16[12,24,128]{2,1,0:T(8,128)(2,1)}), bf16[12,24,128]{2,1,0:T(8,128)(2,1)S(1)}, u32[]{:S(2)}, u32[]{:S(2)}) %all-to-all-start) | async-done | bytes 73760 | tf_op jit(solution)/shard_map/all_to_all | solution.py:200
  27.7 7.5 %all-to-all-start.1 = ((bf16[8,240,128]{2,1,0:T(8,128)(2,1)}), bf16[8,240,128]{2,1,0:T(8,128)(2,1)S(1)}, u32[]{:S(2)}, u32[]{:S(2)}) async-start(bf16[8,240,128]{2,1,0:T(8,128)(2,1)} %shard_map.60), calls=%async_computation.1 | async-start | bytes 983040 | tf_op jit(solution)/shard_map/all_to_all | solution.py:202
  35.3 13.2 %all_gather.3.r_ref = bf16[2304,128]{1,0:T(8,128)(2,1)S(1)} all-gather(bf16[288,128]{1,0:T(8,128)(2,1)S(1)} %bitcast.5), channel_id=1, replica_groups=mesh['y'=8,'zh'=3,'xa'=2,'xb'=2,'zl'=4,'core'=2] {'xa','xb','core'}, dimensions={0}, use_global_device_ids=true | all-gather | bytes 663552 | tf_op jit(solution)/shard_map/all_gather | solution.py:203
  48.5 0.5 all-to-all-done.1.p_ref
  48.9 16.5 %shard_map.61 = (f32[4,192,128]{2,1,0:T(8,128)S(1)}, bf16[4,192,128]{2,1,0:T(8,128)(2,1)S(1)}, bf16[8,160,128]{2,1,0:T(8,128)(2,1)}) custom-call(bf16[2304,128]{1,0:T(8,128)(2,1)S(1)} %all_gather.3.r_ref, bf16[8,240,128]{2,1,0:T(8,128)(2,1)S(1)} %all-to-all-done.1.p_ref), custom_call_target="tpu_custom_call" | custom-call | tf_op jit(solution)/shard_map/pallas_call | solution.py:205
  65.5 6.8 %all-to-all-start.2 = ((bf16[8,160,128]{2,1,0:T(8,128)(2,1)}), bf16[8,160,128]{2,1,0:T(8,128)(2,1)S(1)}, u32[]{:S(2)}, u32[]{:S(2)}) async-start(bf16[8,160,128]{2,1,0:T(8,128)(2,1)} %get-tuple-element.17), calls=%async_computation.2 | async-start | bytes 655360 | tf_op jit(solution)/shard_map/all_to_all | solution.py:226
  72.2 1.9 %collective-permute-start = (bf16[4,192,128]{2,1,0:T(8,128)(2,1)S(1)}, bf16[4,192,128]{2,1,0:T(8,128)(2,1)S(1)}, u32[]{:S(2)}, u32[]{:S(2)}) collective-permute-start(bf16[4,192,128]{2,1,0:T(8,128)(2,1)S(1)} %get-tuple-element.14), channel_id=1, source_target_pairs={{0,1},{1,0},{2,3},{3,2},{4,5},{5,4},{6,7},{7,6},{8,9},{9,8},{10,11... | collective-permute-start | bytes 589832 | tf_op jit(solution)/shard_map/ppermute | solution.py:227
  74.1 1.4 %collective-permute-done.got_ref = bf16[4,192,128]{2,1,0:T(8,128)(2,1)S(1)} collective-permute-done((bf16[4,192,128]{2,1,0:T(8,128)(2,1)S(1)}, bf16[4,192,128]{2,1,0:T(8,128)(2,1)S(1)}, u32[]{:S(2)}, u32[]{:S(2)}) %collective-permute-start) | collective-permute-done | bytes 196640 | tf_op jit(solution)/shard_map/ppermute | solution.py:227
  75.6 2.7 %collective-permute-start.1 = (bf16[2,192,128]{2,1,0:T(8,128)(2,1)S(1)}, bf16[2,192,128]{2,1,0:T(8,128)(2,1)S(1)}, u32[]{:S(2)}, u32[]{:S(2)}) collective-permute-start(bf16[2,192,128]{2,1,0:T(8,128)(2,1)S(1)} %get-tuple-element.16), channel_id=1, source_target_pairs={{0,8},{8,0},{1,9},{9,1},{2,10},{10,2},{3,11},{11,3},{4,12},{12,4},... | collective-permute-start | bytes 294920 | tf_op jit(solution)/shard_map/ppermute | solution.py:228
  78.3 4.0 %collective-permute-done.1 = bf16[2,192,128]{2,1,0:T(8,128)(2,1)S(1)} collective-permute-done((bf16[2,192,128]{2,1,0:T(8,128)(2,1)S(1)}, bf16[2,192,128]{2,1,0:T(8,128)(2,1)S(1)}, u32[]{:S(2)}, u32[]{:S(2)}) %collective-permute-start.1) | collective-permute-done | bytes 98336 | tf_op jit(solution)/shard_map/ppermute | solution.py:228
  82.3 0.7 add_convert_fusion
  83.0 1.6 %all-to-all-done.2.col_ref = bf16[8,160,128]{2,1,0:T(8,128)(2,1)S(1)} async-done(((bf16[8,160,128]{2,1,0:T(8,128)(2,1)}), bf16[8,160,128]{2,1,0:T(8,128)(2,1)S(1)}, u32[]{:S(2)}, u32[]{:S(2)}) %all-to-all-start.2) | async-done | bytes 327712 | tf_op jit(solution)/shard_map/all_to_all | solution.py:226
  84.5 4.9 %all-to-all-start.3 = ((bf16[24,16,128]{2,1,0:T(8,128)(2,1)}), bf16[24,16,128]{2,1,0:T(8,128)(2,1)S(1)}, u32[]{:S(2)}, u32[]{:S(2)}) async-start(bf16[24,16,128]{2,1,0:T(8,128)(2,1)} %bitcast.3), calls=%async_computation.3 | async-start | bytes 196608 | tf_op jit(solution)/shard_map/all_to_all | solution.py:231
  89.5 0.7 shard_map.64
  90.2 12.7 %all-to-all-done.3.row_ref = bf16[24,16,128]{2,1,0:T(8,128)(2,1)S(1)} async-done(((bf16[24,16,128]{2,1,0:T(8,128)(2,1)}), bf16[24,16,128]{2,1,0:T(8,128)(2,1)S(1)}, u32[]{:S(2)}, u32[]{:S(2)}) %all-to-all-start.3) | async-done | bytes 98336 | tf_op jit(solution)/shard_map/all_to_all | solution.py:231
  102.9 0.7 shard_map.63
  (1 shorter events, 0.0 us)
Async XLA Ops:
  2.1 25.7 %all-to-all-start = ((bf16[12,24,128]{2,1,0:T(8,128)(2,1)}), bf16[12,24,128]{2,1,0:T(8,128)(2,1)S(1)}, u32[]{:S(2)}, u32[]{:S(2)}) async-start(bf16[12,24,128]{2,1,0:T(8,128)(2,1)} %shard_map.59), calls=%async_computation | async-start | bytes 147456 | tf_op jit(solution)/shard_map/all_to_all | solution.py:200
  27.7 21.2 %all-to-all-start.1 = ((bf16[8,240,128]{2,1,0:T(8,128)(2,1)}), bf16[8,240,128]{2,1,0:T(8,128)(2,1)S(1)}, u32[]{:S(2)}, u32[]{:S(2)}) async-start(bf16[8,240,128]{2,1,0:T(8,128)(2,1)} %shard_map.60), calls=%async_computation.1 | async-start | bytes 983040 | tf_op jit(solution)/shard_map/all_to_all | solution.py:202
  65.5 19.1 %all-to-all-start.2 = ((bf16[8,160,128]{2,1,0:T(8,128)(2,1)}), bf16[8,160,128]{2,1,0:T(8,128)(2,1)S(1)}, u32[]{:S(2)}, u32[]{:S(2)}) async-start(bf16[8,160,128]{2,1,0:T(8,128)(2,1)} %get-tuple-element.17), calls=%async_computation.2 | async-start | bytes 655360 | tf_op jit(solution)/shard_map/all_to_all | solution.py:226
  72.2 3.3 %collective-permute-start = (bf16[4,192,128]{2,1,0:T(8,128)(2,1)S(1)}, bf16[4,192,128]{2,1,0:T(8,128)(2,1)S(1)}, u32[]{:S(2)}, u32[]{:S(2)}) collective-permute-start(bf16[4,192,128]{2,1,0:T(8,128)(2,1)S(1)} %get-tuple-element.14), channel_id=1, source_target_pairs={{0,1},{1,0},{2,3},{3,2},{4,5},{5,4},{6,7},{7,6},{8,9},{9,8},{10,11... | collective-permute-start | bytes 589832 | tf_op jit(solution)/shard_map/ppermute | solution.py:227
  75.6 6.7 %collective-permute-start.1 = (bf16[2,192,128]{2,1,0:T(8,128)(2,1)S(1)}, bf16[2,192,128]{2,1,0:T(8,128)(2,1)S(1)}, u32[]{:S(2)}, u32[]{:S(2)}) collective-permute-start(bf16[2,192,128]{2,1,0:T(8,128)(2,1)S(1)} %get-tuple-element.16), channel_id=1, source_target_pairs={{0,8},{8,0},{1,9},{9,1},{2,10},{10,2},{3,11},{11,3},{4,12},{12,4},... | collective-permute-start | bytes 294920 | tf_op jit(solution)/shard_map/ppermute | solution.py:228
  84.5 18.3 %all-to-all-start.3 = ((bf16[24,16,128]{2,1,0:T(8,128)(2,1)}), bf16[24,16,128]{2,1,0:T(8,128)(2,1)S(1)}, u32[]{:S(2)}, u32[]{:S(2)}) async-start(bf16[24,16,128]{2,1,0:T(8,128)(2,1)} %bitcast.3), calls=%async_computation.3 | async-start | bytes 196608 | tf_op jit(solution)/shard_map/all_to_all | solution.py:231

commit v11 on v10

--- a/solution.py
+++ b/solution.py
@@ -12,7 +12,6 @@
 XZ = ("xa", "zh", "zl")
 Y_ORDER = [0, 2, 4, 6, 1, 3, 5, 7]
 Z_ORDER = [0, 2, 4, 6, 8, 10, 1, 3, 5, 7, 9, 11]
-XZ_ORDER = [12 * a + z for a in range(2) for z in Z_ORDER]
 NX, NY, NZ, NC = 4, 8, 12, 2
 PR, PC, F, Q = 32, 320, 64, 32
 R, C = PR * NX * NZ * NC, PC * NY
@@ -119,7 +118,8 @@
         t = jnp.concatenate([t[:, 0], t[:, 1]], axis=-1).reshape(BI // 2, 128)
         at = 2 * jnp.int32(i % 2 != xb) + i // 2
         for h in range(2):
-            part[at + 4 * jnp.int32(h != core)] = t[h * (BI // 4):(h + 1) * (BI // 4)]
+            v = t[h * (BI // 4):(h + 1) * (BI // 4)].reshape(2, NZ // 2, PR // 2, 128)
+            part[at + 4 * jnp.int32(h != core)] = jnp.stack([v[0], v[1]], axis=1).reshape(BI // 4, 128)
 
     def both(i, new, old):
         rb = front(i, new)
@@ -228,7 +228,7 @@
     row_part = keep + lax.ppermute(out, "xb", [(0, 1), (1, 0)]).astype(f32)
     row_part = row_part.astype(bf16).reshape(2 * NZ, PR // 2, 128)
     row_part, col_part = lax.optimization_barrier((row_part, col_part))
-    row_part = lax.all_to_all(row_part, XZ, 0, 0, tiled=True, axis_index_groups=[XZ_ORDER])
+    row_part = lax.all_to_all(row_part, XZ, 0, 0, tiled=True)
     row_grad = pl.pallas_call(
         finish_rows,
         out_shape=shape((PR, F), f32),

time: 104 us -> 103 us (level)
  no operation moved by 1% of the time
where the time goes in v11:
time: 103 us
  starting transfers between devices  39 us (38%)
  waiting for transfers between devices  28.1 us (27%)
  Pallas kernels  21.1 us (20%)
  blocking collectives  13.2 us (13%)
    pallas_call x1, Pallas kernels, body(): pl.pallas_call(main_kernel, out_shape=(shape((NX, part, 128), f32), shape...  16.5 us
    all_to_all x1, starting transfers between devices, body(): lax.all_to_all(rows, ('zh', 'zl'), 0, 0, tiled=True, axis_index_groups=[Z...  15.2 us
    all_gather x1, blocking collectives, body(): lax.all_gather(rows.reshape(NZ * 24, 128), ('xa', 'xb', 'core'), axis=0,...  13.2 us
    all_to_all x1, waiting for transfers between devices, body(): row_part = lax.all_to_all(row_part, XZ, 0, 0, tiled=True)  11.8 us
    all_to_all x1, waiting for transfers between devices, body(): lax.all_to_all(rows, ('zh', 'zl'), 0, 0, tiled=True, axis_index_groups=[Z...  8.83 us
    all_to_all x1, starting transfers between devices, body(): lax.all_to_all(cols, 'y', 0, 0, tiled=True, axis_index_groups=[Y_ORDER])  7.55 us
    all_to_all x1, starting transfers between devices, body(): lax.all_to_all(col_part, 'y', 0, 0, tiled=True, axis_index_groups=[Y_ORDER])  6.76 us
    all_to_all x1, starting transfers between devices, body(): row_part = lax.all_to_all(row_part, XZ, 0, 0, tiled=True)  4.93 us
  transfers between devices with their start and end apart: 6, of which 6 were waited for; matrix products, arithmetic and copies ran while one was open for 1% of the time, Pallas kernels for 2%

profile of v11, /device:TPU:10, one launch (start us, length us, event | category | flops | bytes accessed | tf_op | source)
XLA Modules:
  0.0 102.7 jit_solution(5204218418424167919)
XLA Ops:
  0.6 1.4 %shard_map.59 = bf16[12,24,128]{2,1,0:T(8,128)(2,1)} custom-call(bf16[32,64]{1,0:T(8,128)(2,1)} %rp_ref.1, bf16[32,32]{1,0:T(8,128)(2,1)} %rs_ref.1), custom_call_target="tpu_custom_call" | custom-call | tf_op jit(solution)/shard_map/pallas_call | solution.py:188
  2.1 15.2 %all-to-all-start = ((bf16[12,24,128]{2,1,0:T(8,128)(2,1)}), bf16[12,24,128]{2,1,0:T(8,128)(2,1)S(1)}, u32[]{:S(2)}, u32[]{:S(2)}) async-start(bf16[12,24,128]{2,1,0:T(8,128)(2,1)} %shard_map.59), calls=%async_computation | async-start | bytes 147456 | tf_op jit(solution)/shard_map/all_to_all | solution.py:200
  17.2 1.7 %shard_map.60 = bf16[8,240,128]{2,1,0:T(8,128)(2,1)} custom-call(bf16[64,320]{1,0:T(8,128)(2,1)} %bitcast.7, bf16[32,320]{1,0:T(8,128)(2,1)} %bitcast.8), custom_call_target="tpu_custom_call" | custom-call | tf_op jit(solution)/shard_map/pallas_call | solution.py:194
  18.9 8.8 %all-to-all-done = bf16[12,24,128]{2,1,0:T(8,128)(2,1)S(1)} async-done(((bf16[12,24,128]{2,1,0:T(8,128)(2,1)}), bf16[12,24,128]{2,1,0:T(8,128)(2,1)S(1)}, u32[]{:S(2)}, u32[]{:S(2)}) %all-to-all-start) | async-done | bytes 73760 | tf_op jit(solution)/shard_map/all_to_all | solution.py:200
  27.7 7.5 %all-to-all-start.1 = ((bf16[8,240,128]{2,1,0:T(8,128)(2,1)}), bf16[8,240,128]{2,1,0:T(8,128)(2,1)S(1)}, u32[]{:S(2)}, u32[]{:S(2)}) async-start(bf16[8,240,128]{2,1,0:T(8,128)(2,1)} %shard_map.60), calls=%async_computation.1 | async-start | bytes 983040 | tf_op jit(solution)/shard_map/all_to_all | solution.py:202
  35.3 13.2 %all_gather.3.r_ref = bf16[2304,128]{1,0:T(8,128)(2,1)S(1)} all-gather(bf16[288,128]{1,0:T(8,128)(2,1)S(1)} %bitcast.5), channel_id=1, replica_groups=mesh['y'=8,'zh'=3,'xa'=2,'xb'=2,'zl'=4,'core'=2] {'xa','xb','core'}, dimensions={0}, use_global_device_ids=true | all-gather | bytes 663552 | tf_op jit(solution)/shard_map/all_gather | solution.py:203
  48.5 0.5 all-to-all-done.1.p_ref
  48.9 16.5 %shard_map.61 = (f32[4,192,128]{2,1,0:T(8,128)S(1)}, bf16[4,192,128]{2,1,0:T(8,128)(2,1)S(1)}, bf16[8,160,128]{2,1,0:T(8,128)(2,1)}) custom-call(bf16[2304,128]{1,0:T(8,128)(2,1)S(1)} %all_gather.3.r_ref, bf16[8,240,128]{2,1,0:T(8,128)(2,1)S(1)} %all-to-all-done.1.p_ref), custom_call_target="tpu_custom_call" | custom-call | tf_op jit(solution)/shard_map/pallas_call | solution.py:205
  65.5 6.8 %all-to-all-start.2 = ((bf16[8,160,128]{2,1,0:T(8,128)(2,1)}), bf16[8,160,128]{2,1,0:T(8,128)(2,1)S(1)}, u32[]{:S(2)}, u32[]{:S(2)}) async-start(bf16[8,160,128]{2,1,0:T(8,128)(2,1)} %get-tuple-element.17), calls=%async_computation.2 | async-start | bytes 655360 | tf_op jit(solution)/shard_map/all_to_all | solution.py:226
  72.2 1.9 %collective-permute-start = (bf16[4,192,128]{2,1,0:T(8,128)(2,1)S(1)}, bf16[4,192,128]{2,1,0:T(8,128)(2,1)S(1)}, u32[]{:S(2)}, u32[]{:S(2)}) collective-permute-start(bf16[4,192,128]{2,1,0:T(8,128)(2,1)S(1)} %get-tuple-element.14), channel_id=1, source_target_pairs={{0,1},{1,0},{2,3},{3,2},{4,5},{5,4},{6,7},{7,6},{8,9},{9,8},{10,11... | collective-permute-start | bytes 589832 | tf_op jit(solution)/shard_map/ppermute | solution.py:227
  74.1 1.4 %collective-permute-done.got_ref = bf16[4,192,128]{2,1,0:T(8,128)(2,1)S(1)} collective-permute-done((bf16[4,192,128]{2,1,0:T(8,128)(2,1)S(1)}, bf16[4,192,128]{2,1,0:T(8,128)(2,1)S(1)}, u32[]{:S(2)}, u32[]{:S(2)}) %collective-permute-start) | collective-permute-done | bytes 196640 | tf_op jit(solution)/shard_map/ppermute | solution.py:227
  75.6 2.7 %collective-permute-start.1 = (bf16[2,192,128]{2,1,0:T(8,128)(2,1)S(1)}, bf16[2,192,128]{2,1,0:T(8,128)(2,1)S(1)}, u32[]{:S(2)}, u32[]{:S(2)}) collective-permute-start(bf16[2,192,128]{2,1,0:T(8,128)(2,1)S(1)} %get-tuple-element.16), channel_id=1, source_target_pairs={{0,8},{8,0},{1,9},{9,1},{2,10},{10,2},{3,11},{11,3},{4,12},{12,4},... | collective-permute-start | bytes 294920 | tf_op jit(solution)/shard_map/ppermute | solution.py:228
  78.3 4.0 %collective-permute-done.1 = bf16[2,192,128]{2,1,0:T(8,128)(2,1)S(1)} collective-permute-done((bf16[2,192,128]{2,1,0:T(8,128)(2,1)S(1)}, bf16[2,192,128]{2,1,0:T(8,128)(2,1)S(1)}, u32[]{:S(2)}, u32[]{:S(2)}) %collective-permute-start.1) | collective-permute-done | bytes 98336 | tf_op jit(solution)/shard_map/ppermute | solution.py:228
  82.3 0.7 add_convert_fusion
  83.0 1.6 %all-to-all-done.2.col_ref = bf16[8,160,128]{2,1,0:T(8,128)(2,1)S(1)} async-done(((bf16[8,160,128]{2,1,0:T(8,128)(2,1)}), bf16[8,160,128]{2,1,0:T(8,128)(2,1)S(1)}, u32[]{:S(2)}, u32[]{:S(2)}) %all-to-all-start.2) | async-done | bytes 327712 | tf_op jit(solution)/shard_map/all_to_all | solution.py:226
  84.5 4.9 %all-to-all-start.3 = ((bf16[24,16,128]{2,1,0:T(8,128)(2,1)}), bf16[24,16,128]{2,1,0:T(8,128)(2,1)S(1)}, u32[]{:S(2)}, u32[]{:S(2)}) async-start(bf16[24,16,128]{2,1,0:T(8,128)(2,1)} %bitcast.3), calls=%async_computation.3 | async-start | bytes 196608 | tf_op jit(solution)/shard_map/all_to_all | solution.py:231
  89.5 0.7 shard_map.64
  90.2 11.8 %all-to-all-done.3.row_ref = bf16[24,16,128]{2,1,0:T(8,128)(2,1)S(1)} async-done(((bf16[24,16,128]{2,1,0:T(8,128)(2,1)}), bf16[24,16,128]{2,1,0:T(8,128)(2,1)S(1)}, u32[]{:S(2)}, u32[]{:S(2)}) %all-to-all-start.3) | async-done | bytes 98336 | tf_op jit(solution)/shard_map/all_to_all | solution.py:231
  102.0 0.7 shard_map.63
  (1 shorter events, 0.0 us)
Async XLA Ops:
  2.1 25.7 %all-to-all-start = ((bf16[12,24,128]{2,1,0:T(8,128)(2,1)}), bf16[12,24,128]{2,1,0:T(8,128)(2,1)S(1)}, u32[]{:S(2)}, u32[]{:S(2)}) async-start(bf16[12,24,128]{2,1,0:T(8,128)(2,1)} %shard_map.59), calls=%async_computation | async-start | bytes 147456 | tf_op jit(solution)/shard_map/all_to_all | solution.py:200
  27.7 21.2 %all-to-all-start.1 = ((bf16[8,240,128]{2,1,0:T(8,128)(2,1)}), bf16[8,240,128]{2,1,0:T(8,128)(2,1)S(1)}, u32[]{:S(2)}, u32[]{:S(2)}) async-start(bf16[8,240,128]{2,1,0:T(8,128)(2,1)} %shard_map.60), calls=%async_computation.1 | async-start | bytes 983040 | tf_op jit(solution)/shard_map/all_to_all | solution.py:202
  65.5 19.1 %all-to-all-start.2 = ((bf16[8,160,128]{2,1,0:T(8,128)(2,1)}), bf16[8,160,128]{2,1,0:T(8,128)(2,1)S(1)}, u32[]{:S(2)}, u32[]{:S(2)}) async-start(bf16[8,160,128]{2,1,0:T(8,128)(2,1)} %get-tuple-element.17), calls=%async_computation.2 | async-start | bytes 655360 | tf_op jit(solution)/shard_map/all_to_all | solution.py:226
  72.2 3.3 %collective-permute-start = (bf16[4,192,128]{2,1,0:T(8,128)(2,1)S(1)}, bf16[4,192,128]{2,1,0:T(8,128)(2,1)S(1)}, u32[]{:S(2)}, u32[]{:S(2)}) collective-permute-start(bf16[4,192,128]{2,1,0:T(8,128)(2,1)S(1)} %get-tuple-element.14), channel_id=1, source_target_pairs={{0,1},{1,0},{2,3},{3,2},{4,5},{5,4},{6,7},{7,6},{8,9},{9,8},{10,11... | collective-permute-start | bytes 589832 | tf_op jit(solution)/shard_map/ppermute | solution.py:227
  75.6 6.7 %collective-permute-start.1 = (bf16[2,192,128]{2,1,0:T(8,128)(2,1)S(1)}, bf16[2,192,128]{2,1,0:T(8,128)(2,1)S(1)}, u32[]{:S(2)}, u32[]{:S(2)}) collective-permute-start(bf16[2,192,128]{2,1,0:T(8,128)(2,1)S(1)} %get-tuple-element.16), channel_id=1, source_target_pairs={{0,8},{8,0},{1,9},{9,1},{2,10},{10,2},{3,11},{11,3},{4,12},{12,4},... | collective-permute-start | bytes 294920 | tf_op jit(solution)/shard_map/ppermute | solution.py:228
  84.5 17.5 %all-to-all-start.3 = ((bf16[24,16,128]{2,1,0:T(8,128)(2,1)}), bf16[24,16,128]{2,1,0:T(8,128)(2,1)S(1)}, u32[]{:S(2)}, u32[]{:S(2)}) async-start(bf16[24,16,128]{2,1,0:T(8,128)(2,1)} %bitcast.3), calls=%async_computation.3 | async-start | bytes 196608 | tf_op jit(solution)/shard_map/all_to_all | solution.py:231

commit v12 on v11

--- a/solution.py
+++ b/solution.py
@@ -10,7 +10,7 @@
 NAMES = ("y", "zh", "xa", "xb", "zl", "core")
 SIZES = (8, 3, 2, 2, 4, 2)
 XZ = ("xa", "zh", "zl")
-Y_ORDER = [0, 2, 4, 6, 1, 3, 5, 7]
+Y_ORDER = [0, 4, 1, 5, 2, 6, 3, 7]
 Z_ORDER = [0, 2, 4, 6, 8, 10, 1, 3, 5, 7, 9, 11]
 NX, NY, NZ, NC = 4, 8, 12, 2
 PR, PC, F, Q = 32, 320, 64, 32

time: 103 us -> 104 us (level)
  transfers between devices with their start and end apart: 6 -> 6, of which waited for: 6 -> 5; matrix products, arithmetic and copies ran while one was open for 1% -> 1% of each run, Pallas kernels for 2% -> 2%
where the time goes in v12:
time: 104 us; the launch traced here: 103 us
  starting transfers between devices  39.5 us (38%)
  waiting for transfers between devices  28 us (27%)
  Pallas kernels  21.1 us (20%)
  blocking collectives  13.2 us (13%)
    pallas_call x1, Pallas kernels, body(): pl.pallas_call(main_kernel, out_shape=(shape((NX, part, 128), f32), shape...  16.5 us
    all_to_all x1, starting transfers between devices, body(): lax.all_to_all(rows, ('zh', 'zl'), 0, 0, tiled=True, axis_index_groups=[Z...  15.2 us
    all_gather x1, blocking collectives, body(): lax.all_gather(rows.reshape(NZ * 24, 128), ('xa', 'xb', 'core'), axis=0,...  13.2 us
    all_to_all x1, waiting for transfers between devices, body(): row_part = lax.all_to_all(row_part, XZ, 0, 0, tiled=True)  12.6 us
    all_to_all x1, waiting for transfers between devices, body(): lax.all_to_all(rows, ('zh', 'zl'), 0, 0, tiled=True, axis_index_groups=[Z...  8.83 us
    all_to_all x1, starting transfers between devices, body(): lax.all_to_all(cols, 'y', 0, 0, tiled=True, axis_index_groups=[Y_ORDER])  7.55 us
    all_to_all x1, starting transfers between devices, body(): lax.all_to_all(col_part, 'y', 0, 0, tiled=True, axis_index_groups=[Y_ORDER])  7.2 us
    all_to_all x1, starting transfers between devices, body(): row_part = lax.all_to_all(row_part, XZ, 0, 0, tiled=True)  4.93 us
  transfers between devices with their start and end apart: 6, of which 5 were waited for; matrix products, arithmetic and copies ran while one was open for 1% of the time, Pallas kernels for 2%

profile of v12, /device:TPU:10, one launch (start us, length us, event | category | flops | bytes accessed | tf_op | source)
XLA Modules:
  0.0 103.1 jit_solution(15661486042290983169)
XLA Ops:
  0.6 1.4 %shard_map.59 = bf16[12,24,128]{2,1,0:T(8,128)(2,1)} custom-call(bf16[32,64]{1,0:T(8,128)(2,1)} %rp_ref.1, bf16[32,32]{1,0:T(8,128)(2,1)} %rs_ref.1), custom_call_target="tpu_custom_call" | custom-call | tf_op jit(solution)/shard_map/pallas_call | solution.py:188
  2.1 15.2 %all-to-all-start = ((bf16[12,24,128]{2,1,0:T(8,128)(2,1)}), bf16[12,24,128]{2,1,0:T(8,128)(2,1)S(1)}, u32[]{:S(2)}, u32[]{:S(2)}) async-start(bf16[12,24,128]{2,1,0:T(8,128)(2,1)} %shard_map.59), calls=%async_computation | async-start | bytes 147456 | tf_op jit(solution)/shard_map/all_to_all | solution.py:200
  17.2 1.7 %shard_map.60 = bf16[8,240,128]{2,1,0:T(8,128)(2,1)} custom-call(bf16[64,320]{1,0:T(8,128)(2,1)} %bitcast.7, bf16[32,320]{1,0:T(8,128)(2,1)} %bitcast.8), custom_call_target="tpu_custom_call" | custom-call | tf_op jit(solution)/shard_map/pallas_call | solution.py:194
  18.9 8.8 %all-to-all-done = bf16[12,24,128]{2,1,0:T(8,128)(2,1)S(1)} async-done(((bf16[12,24,128]{2,1,0:T(8,128)(2,1)}), bf16[12,24,128]{2,1,0:T(8,128)(2,1)S(1)}, u32[]{:S(2)}, u32[]{:S(2)}) %all-to-all-start) | async-done | bytes 73760 | tf_op jit(solution)/shard_map/all_to_all | solution.py:200
  27.7 7.5 %all-to-all-start.1 = ((bf16[8,240,128]{2,1,0:T(8,128)(2,1)}), bf16[8,240,128]{2,1,0:T(8,128)(2,1)S(1)}, u32[]{:S(2)}, u32[]{:S(2)}) async-start(bf16[8,240,128]{2,1,0:T(8,128)(2,1)} %shard_map.60), calls=%async_computation.1 | async-start | bytes 983040 | tf_op jit(solution)/shard_map/all_to_all | solution.py:202
  35.3 13.2 %all_gather.3.r_ref = bf16[2304,128]{1,0:T(8,128)(2,1)S(1)} all-gather(bf16[288,128]{1,0:T(8,128)(2,1)S(1)} %bitcast.5), channel_id=1, replica_groups=mesh['y'=8,'zh'=3,'xa'=2,'xb'=2,'zl'=4,'core'=2] {'xa','xb','core'}, dimensions={0}, use_global_device_ids=true | all-gather | bytes 663552 | tf_op jit(solution)/shard_map/all_gather | solution.py:203
  48.5 0.0 all-to-all-done.1.p_ref
  48.5 16.5 %shard_map.61 = (f32[4,192,128]{2,1,0:T(8,128)S(1)}, bf16[4,192,128]{2,1,0:T(8,128)(2,1)S(1)}, bf16[8,160,128]{2,1,0:T(8,128)(2,1)}) custom-call(bf16[2304,128]{1,0:T(8,128)(2,1)S(1)} %all_gather.3.r_ref, bf16[8,240,128]{2,1,0:T(8,128)(2,1)S(1)} %all-to-all-done.1.p_ref), custom_call_target="tpu_custom_call" | custom-call | tf_op jit(solution)/shard_map/pallas_call | solution.py:205
  65.0 7.2 %all-to-all-start.2 = ((bf16[8,160,128]{2,1,0:T(8,128)(2,1)}), bf16[8,160,128]{2,1,0:T(8,128)(2,1)S(1)}, u32[]{:S(2)}, u32[]{:S(2)}) async-start(bf16[8,160,128]{2,1,0:T(8,128)(2,1)} %get-tuple-element.17), calls=%async_computation.2 | async-start | bytes 655360 | tf_op jit(solution)/shard_map/all_to_all | solution.py:226
  72.2 1.9 %collective-permute-start = (bf16[4,192,128]{2,1,0:T(8,128)(2,1)S(1)}, bf16[4,192,128]{2,1,0:T(8,128)(2,1)S(1)}, u32[]{:S(2)}, u32[]{:S(2)}) collective-permute-start(bf16[4,192,128]{2,1,0:T(8,128)(2,1)S(1)} %get-tuple-element.14), channel_id=1, source_target_pairs={{0,1},{1,0},{2,3},{3,2},{4,5},{5,4},{6,7},{7,6},{8,9},{9,8},{10,11... | collective-permute-start | bytes 589832 | tf_op jit(solution)/shard_map/ppermute | solution.py:227
  74.1 1.4 %collective-permute-done.got_ref = bf16[4,192,128]{2,1,0:T(8,128)(2,1)S(1)} collective-permute-done((bf16[4,192,128]{2,1,0:T(8,128)(2,1)S(1)}, bf16[4,192,128]{2,1,0:T(8,128)(2,1)S(1)}, u32[]{:S(2)}, u32[]{:S(2)}) %collective-permute-start) | collective-permute-done | bytes 196640 | tf_op jit(solution)/shard_map/ppermute | solution.py:227
  75.6 2.7 %collective-permute-start.1 = (bf16[2,192,128]{2,1,0:T(8,128)(2,1)S(1)}, bf16[2,192,128]{2,1,0:T(8,128)(2,1)S(1)}, u32[]{:S(2)}, u32[]{:S(2)}) collective-permute-start(bf16[2,192,128]{2,1,0:T(8,128)(2,1)S(1)} %get-tuple-element.16), channel_id=1, source_target_pairs={{0,8},{8,0},{1,9},{9,1},{2,10},{10,2},{3,11},{11,3},{4,12},{12,4},... | collective-permute-start | bytes 294920 | tf_op jit(solution)/shard_map/ppermute | solution.py:228
  78.3 4.0 %collective-permute-done.1 = bf16[2,192,128]{2,1,0:T(8,128)(2,1)S(1)} collective-permute-done((bf16[2,192,128]{2,1,0:T(8,128)(2,1)S(1)}, bf16[2,192,128]{2,1,0:T(8,128)(2,1)S(1)}, u32[]{:S(2)}, u32[]{:S(2)}) %collective-permute-start.1) | collective-permute-done | bytes 98336 | tf_op jit(solution)/shard_map/ppermute | solution.py:228
  82.3 0.7 add_convert_fusion
  83.0 1.1 %all-to-all-done.2.col_ref = bf16[8,160,128]{2,1,0:T(8,128)(2,1)S(1)} async-done(((bf16[8,160,128]{2,1,0:T(8,128)(2,1)}), bf16[8,160,128]{2,1,0:T(8,128)(2,1)S(1)}, u32[]{:S(2)}, u32[]{:S(2)}) %all-to-all-start.2) | async-done | bytes 327712 | tf_op jit(solution)/shard_map/all_to_all | solution.py:226
  84.1 4.9 %all-to-all-start.3 = ((bf16[24,16,128]{2,1,0:T(8,128)(2,1)}), bf16[24,16,128]{2,1,0:T(8,128)(2,1)S(1)}, u32[]{:S(2)}, u32[]{:S(2)}) async-start(bf16[24,16,128]{2,1,0:T(8,128)(2,1)} %bitcast.3), calls=%async_computation.3 | async-start | bytes 196608 | tf_op jit(solution)/shard_map/all_to_all | solution.py:231
  89.0 0.7 shard_map.64
  89.8 12.6 %all-to-all-done.3.row_ref = bf16[24,16,128]{2,1,0:T(8,128)(2,1)S(1)} async-done(((bf16[24,16,128]{2,1,0:T(8,128)(2,1)}), bf16[24,16,128]{2,1,0:T(8,128)(2,1)S(1)}, u32[]{:S(2)}, u32[]{:S(2)}) %all-to-all-start.3) | async-done | bytes 98336 | tf_op jit(solution)/shard_map/all_to_all | solution.py:231
  102.4 0.7 shard_map.63
  (1 shorter events, 0.0 us)
Async XLA Ops:
  2.1 25.7 %all-to-all-start = ((bf16[12,24,128]{2,1,0:T(8,128)(2,1)}), bf16[12,24,128]{2,1,0:T(8,128)(2,1)S(1)}, u32[]{:S(2)}, u32[]{:S(2)}) async-start(bf16[12,24,128]{2,1,0:T(8,128)(2,1)} %shard_map.59), calls=%async_computation | async-start | bytes 147456 | tf_op jit(solution)/shard_map/all_to_all | solution.py:200
  27.7 20.8 %all-to-all-start.1 = ((bf16[8,240,128]{2,1,0:T(8,128)(2,1)}), bf16[8,240,128]{2,1,0:T(8,128)(2,1)S(1)}, u32[]{:S(2)}, u32[]{:S(2)}) async-start(bf16[8,240,128]{2,1,0:T(8,128)(2,1)} %shard_map.60), calls=%async_computation.1 | async-start | bytes 983040 | tf_op jit(solution)/shard_map/all_to_all | solution.py:202
  65.0 19.1 %all-to-all-start.2 = ((bf16[8,160,128]{2,1,0:T(8,128)(2,1)}), bf16[8,160,128]{2,1,0:T(8,128)(2,1)S(1)}, u32[]{:S(2)}, u32[]{:S(2)}) async-start(bf16[8,160,128]{2,1,0:T(8,128)(2,1)} %get-tuple-element.17), calls=%async_computation.2 | async-start | bytes 655360 | tf_op jit(solution)/shard_map/all_to_all | solution.py:226
  72.2 3.3 %collective-permute-start = (bf16[4,192,128]{2,1,0:T(8,128)(2,1)S(1)}, bf16[4,192,128]{2,1,0:T(8,128)(2,1)S(1)}, u32[]{:S(2)}, u32[]{:S(2)}) collective-permute-start(bf16[4,192,128]{2,1,0:T(8,128)(2,1)S(1)} %get-tuple-element.14), channel_id=1, source_target_pairs={{0,1},{1,0},{2,3},{3,2},{4,5},{5,4},{6,7},{7,6},{8,9},{9,8},{10,11... | collective-permute-start | bytes 589832 | tf_op jit(solution)/shard_map/ppermute | solution.py:227
  75.6 6.7 %collective-permute-start.1 = (bf16[2,192,128]{2,1,0:T(8,128)(2,1)S(1)}, bf16[2,192,128]{2,1,0:T(8,128)(2,1)S(1)}, u32[]{:S(2)}, u32[]{:S(2)}) collective-permute-start(bf16[2,192,128]{2,1,0:T(8,128)(2,1)S(1)} %get-tuple-element.16), channel_id=1, source_target_pairs={{0,8},{8,0},{1,9},{9,1},{2,10},{10,2},{3,11},{11,3},{4,12},{12,4},... | collective-permute-start | bytes 294920 | tf_op jit(solution)/shard_map/ppermute | solution.py:228
  84.1 18.3 %all-to-all-start.3 = ((bf16[24,16,128]{2,1,0:T(8,128)(2,1)}), bf16[24,16,128]{2,1,0:T(8,128)(2,1)S(1)}, u32[]{:S(2)}, u32[]{:S(2)}) async-start(bf16[24,16,128]{2,1,0:T(8,128)(2,1)} %bitcast.3), calls=%async_computation.3 | async-start | bytes 196608 | tf_op jit(solution)/shard_map/all_to_all | solution.py:231
